TPU v7x, 32 devices: a whole 2x2x4 slice. The times are simulated.
32 devices in a mesh: slab: 4 (over x, core), dom: 8 (over z, y).
Axes of the slice: x: 2, y: 2, z: 4, core: 2. Of those that a mesh axis runs over, the one named last changes fastest.
Arguments:
- coords: float32 [3, 4, 8, 512], P(None, 'slab', 'dom'), may hold values from -6 to 6
- velocity: float32 [3, 4, 8, 512], P(None, 'slab', 'dom'), may hold values from -6 to 6
- charge: float32 [4, 8, 512], P('slab', 'dom'), may hold values from -1 to 1
- inv_mass: float32 [4, 8, 512], P('slab', 'dom'), may hold values from 0.0625 to 1
- tile_block: int32 [4, 8, 64], P('slab', 'dom'), may hold values from 0 to 3
- tile_atoms: int32 [4, 8, 64, 128], P('slab', 'dom'), may hold values from 0 to 2047
- active_tile_count: int32 [4, 8], P('slab', 'dom'), may hold values from 1 to 64
- bond_atoms: int32 [2, 4, 8, 256], P(None, 'slab', 'dom'), may hold values from 0 to 511, as said below
- cross_atoms: int32 [2, 4, 8, 128], P(None, 'slab', 'dom'), may hold values from 0 to 255
- cross_side: int32 [4, 8, 128], P('slab', 'dom'), may hold values from 0 to 3
- cross_count: int32 [4, 8], P('slab', 'dom'), may hold values from 1 to 128
Outputs:
- coords_out: float32 [3, 4, 8, 512], P(None, 'slab', 'dom')
- velocity_out: float32 [3, 4, 8, 512], P(None, 'slab', 'dom')
Inputs may be any that keep to these rules, and one draw needn't show every extreme that they name: `bond_atoms`: each bond joins two different atoms of the domain that holds it. `cross_atoms`: row 0 is an atom of the owning domain, row 1 an atom of the neighbour named by cross_side; both are among the first 256 atoms of their domains. `cross_side`: codes 0 to 3 name the in-slab neighbours at offsets +1, -1, +2, -2 along dom, cyclically. `cross_count`: slots below the count are live. `active_tile_count`: tiles below the count are live. `tile_atoms`: entries index the domain's halo list as in the first step.
All inputs are finite; a program needn't handle non-finite values.
Results may differ from a plain program's by a relative error of at most 0.0003.
Values sent between devices are 32-bit elements; how exact they have to be, the bound alone decides.
No kernel may reach another device: no remote copies, remote signals or barrier semaphores. Data moves between devices by JAX's collectives and lax.ppermute only.
A program may use at most 64 MiB of HBM per device.

v0:
```python
import jax
import jax.numpy as jnp
from jax import lax
from jax.sharding import PartitionSpec as P

TILE = 128
ORDER = 4


time_step = 0.1
cutoff_sq = 16.0
force_scale = 4.0
length_floor = 0.25


def passed_along(array, axis, by):
    length = lax.axis_size(axis)
    return lax.ppermute(array, axis, [(i, (i + by) % length) for i in range(length)])


def group_force(own_blocks, halo_data, block_ids, atom_ids, live_flags):
    near_data = jnp.take(own_blocks, block_ids, axis=1)
    far_data = jnp.take(halo_data, atom_ids, axis=1)
    offset_vec = near_data[:3, :, :, None] - far_data[:3, :, None, :]
    dist_sq = jnp.sum(offset_vec * offset_vec, axis=0)
    inverse = 1.0 / (dist_sq + 1.0)
    switch = jnp.maximum(1.0 - dist_sq / cutoff_sq, 0.0) ** 2
    strength = (
        force_scale
        * (2.0 * inverse**3 - near_data[3][:, :, None] * far_data[3][:, None, :] * inverse**2)
        * switch
    )
    forces = jnp.sum(strength[None] * offset_vec, axis=3)
    return forces * live_flags[None, :, None]


def geometry(atom_first, atom_second, mass_first, mass_second):
    offset_vec = atom_first - atom_second
    length = jnp.sqrt(jnp.sum(offset_vec * offset_vec, axis=0) + length_floor)
    return (offset_vec / length, lax.rsqrt(mass_first + mass_second))


def project_bond(direction, bond_scale, atom_first, atom_second):
    return bond_scale * jnp.sum(direction * (atom_first - atom_second), axis=0)


def from_domains(rim_data, row_width):
    strides = (1, -1, row_width, -row_width)
    return jnp.concatenate([passed_along(rim_data, "dom", -stride) for stride in strides], axis=1)


def order_fields(rim_data, row_width):
    strides = (1, -1, row_width, -row_width)
    return jnp.concatenate([passed_along(rim_data, "dom", -stride) for stride in strides], axis=1)


def shards(
    coords,
    velocity,
    charge,
    inv_mass,
    tile_block,
    tile_atoms,
    active_tile_count,
    bond_atoms,
    cross_atoms,
    cross_side,
    cross_count,
):
    atom_count = coords.shape[-1]
    shell_size = atom_count // 2
    row_width = max(2, lax.axis_size("dom") // 8)
    strides = (1, -1, row_width, -row_width)
    coords = coords.reshape(3, atom_count)
    velocity = velocity.reshape(3, atom_count)
    inv_mass = inv_mass.reshape(atom_count)
    tile_block = tile_block.reshape(-1)
    tile_atoms = tile_atoms.reshape(-1, TILE)
    live_tiles = active_tile_count.reshape(())
    bond_left = bond_atoms.reshape(2, -1)[0]
    bond_partner_right = bond_atoms.reshape(2, -1)[1]
    cross_left = cross_atoms.reshape(2, -1)[0]
    cross_right = cross_atoms.reshape(2, -1)[1]
    side_code = cross_side.reshape(-1)
    slot_count = side_code.shape[0]
    cross_live = jnp.arange(slot_count, dtype=jnp.int32) < cross_count.reshape(())
    cross_flag = cross_live.astype(jnp.float32)
    own_data = jnp.concatenate([coords, charge.reshape(1, atom_count), inv_mass[None]], axis=0)
    outer_rim = own_data[:, :shell_size]
    slab_pieces = [passed_along(outer_rim, "slab", stride) for stride in (1, -1)]
    halo_data = jnp.concatenate(
        [own_data, from_domains(outer_rim, row_width)] + slab_pieces, axis=1
    )
    tiles = tile_atoms.shape[0]
    group_size = min(16, tiles)
    grouped = tiles // group_size
    block_count = atom_count // TILE
    own_blocks = own_data.reshape(5, block_count, TILE)
    tile_flags = (jnp.arange(tiles, dtype=jnp.int32) < live_tiles).astype(jnp.float32)
    block_range = jnp.arange(block_count, dtype=jnp.int32)

    def add_group(group, totals):
        start = group * group_size
        block_ids = lax.dynamic_slice_in_dim(tile_block, start, group_size, 0)
        atom_ids = lax.dynamic_slice_in_dim(tile_atoms, start, group_size, 0)
        live_flags = lax.dynamic_slice_in_dim(tile_flags, start, group_size, 0)
        group_values = group_force(own_blocks, halo_data, block_ids, atom_ids, live_flags)
        pick_entries = (block_ids[:, None] == block_range[None, :]).astype(jnp.float32)
        return totals + jnp.einsum(
            "gb,agx->abx", pick_entries, group_values, precision=lax.Precision.HIGHEST
        )

    force_blocks = lax.fori_loop(
        0, grouped, add_group, jnp.zeros((3, block_count, TILE), jnp.float32)
    )
    forces = force_blocks.reshape(3, atom_count)
    velocity_half = velocity + time_step * forces * inv_mass[None]
    displace = time_step * velocity_half
    updated_positions = coords + displace
    far_data = halo_data[:, atom_count : atom_count + 4 * shell_size]
    local_dir, local_scale = geometry(
        coords[:, bond_left],
        coords[:, bond_partner_right],
        inv_mass[bond_left],
        inv_mass[bond_partner_right],
    )
    cross_index = side_code * shell_size + cross_right
    cross_dir, cross_scale = geometry(
        coords[:, cross_left],
        far_data[:3, cross_index],
        inv_mass[cross_left],
        far_data[4, cross_index],
    )
    displace_far = from_domains(displace[:, :shell_size], row_width)
    local_rhs = project_bond(
        local_dir, local_scale, displace[:, bond_left], displace[:, bond_partner_right]
    )
    cross_rhs = (
        project_bond(cross_dir, cross_scale, displace[:, cross_left], displace_far[:, cross_index])
        * cross_flag
    )
    residue = (local_rhs, cross_rhs)

    def collect(values):
        pushed = local_dir * (local_scale * values[0])
        totals = (
            jnp.zeros((3, atom_count), jnp.float32)
            .at[:, bond_left]
            .add(pushed)
            .at[:, bond_partner_right]
            .add(-pushed)
        )
        cross_push = cross_dir * (cross_scale * values[1])
        totals = totals.at[:, cross_left].add(cross_push)
        outward = jnp.zeros((3, 4 * shell_size), jnp.float32).at[:, cross_index].add(-cross_push)
        returned = [
            passed_along(
                outward[:, neighbour * shell_size : (neighbour + 1) * shell_size],
                "dom",
                strides[neighbour],
            )
            for neighbour in range(4)
        ]
        arrived = returned[0] + returned[1] + returned[2] + returned[3]
        totals = totals + jnp.pad(arrived, ((0, 0), (0, atom_count - shell_size)))
        return inv_mass[None] * totals

    def changes(spread_now, far_cross):
        local_change = project_bond(
            local_dir, local_scale, spread_now[:, bond_left], spread_now[:, bond_partner_right]
        )
        cross_change = (
            project_bond(cross_dir, cross_scale, spread_now[:, cross_left], far_cross) * cross_flag
        )
        return (local_change, cross_change)

    accumulated_sum = residue
    for expansion in range(ORDER):
        spread_now = collect(residue)
        spread_far = order_fields(spread_now[:, :shell_size], row_width)
        far_cross = spread_far[:, cross_index]
        residue = tuple(
            (
                value_now - value_step
                for value_now, value_step in zip(residue, changes(spread_now, far_cross))
            )
        )
        accumulated_sum = tuple(
            (value_sum + value_now for value_sum, value_now in zip(accumulated_sum, residue))
        )
    correction = collect(accumulated_sum)
    coords_out = (updated_positions - correction).reshape(3, 1, 1, atom_count)
    velocity_out = (velocity_half - correction / time_step).reshape(3, 1, 1, atom_count)
    return (coords_out, velocity_out)


def solution(mesh):
    return jax.shard_map(
        shards,
        mesh=mesh,
        in_specs=(
            P(None, "slab", "dom", None),
            P(None, "slab", "dom", None),
            P("slab", "dom", None),
            P("slab", "dom", None),
            P("slab", "dom", None),
            P("slab", "dom", None, None),
            P("slab", "dom"),
            P(None, "slab", "dom", None),
            P(None, "slab", "dom", None),
            P("slab", "dom", None),
            P("slab", "dom"),
        ),
        out_specs=(P(None, "slab", "dom", None), P(None, "slab", "dom", None)),
        check_vma=False,
    )
```

profile of v0, /device:TPU:0, one launch (start us, length us, event | category | flops | bytes accessed | tf_op | source)
XLA Modules:
  0.0 486.2 jit_solution(13940457296058512761)
XLA Ops:
  2.4 6.1 %collective-permute-start = (f32[5,256]{1,0:T(8,128)S(1)}, f32[5,256]{1,0:T(8,128)S(1)}, u32[]{:S(2)}, u32[]{:S(2)}) collective-permute-start(f32[5,256]{1,0:T(8,128)S(1)} %slice.228), channel_id=1, source_target_pairs={{0,7},{1,0},{2,1},{3,2},{4,3},{5,4},{6,5},{7,6},{8,15},{9,8},{10,9... | collective-permute-start | bytes 15368 | tf_op jit(solution)/shard_map/ppermute | solution.py:18
  24.5 42.0 %while.16 = (s32[]{:T(128)}, f32[3,4,128]{2,1,0:T(4,128)S(1)}, s32[64]{0:T(128)S(1)}, f32[5,4,128]{2,0,1:T(8,128)S(1)}, s32[64,128]{1,0:T(8,128)S(1)}, /*index=5...) while((s32[]{:T(128)}, f32[3,4,128]{2,1,0:T(4,128)S(1)}, ...), condition=%wide.region_3.4_spmd.clone, body=%wide.region_0.3_spmd.clone.sunk | while | flops 8466647 | bytes 5002069 | solution.py:113
  25.4 5.5 %gather_fusion = f32[2048,5]{1,0:T(8,128)S(1)} fusion(f32[5,2048]{0,1:T(8,128)S(1)} %get-tuple-element.407, s32[2048]{0:T(1024)S(1)} %bitcast_clamp_fusion.2), kind=kCustom, calls=%fused_computation.1.clone.clone.1 | custom fusion | bytes 90112 | tf_op jit(solution)/shard_map/while/body/eval_jaxpr/jit(_take)/gather | solution.py:23
  35.8 5.5 %gather_fusion = f32[2048,5]{1,0:T(8,128)S(1)} fusion(f32[5,2048]{0,1:T(8,128)S(1)} %get-tuple-element.407, s32[2048]{0:T(1024)S(1)} %bitcast_clamp_fusion.2), kind=kCustom, calls=%fused_computation.1.clone.clone.1 | custom fusion | bytes 90112 | tf_op jit(solution)/shard_map/while/body/eval_jaxpr/jit(_take)/gather | solution.py:23
  46.3 5.5 %gather_fusion = f32[2048,5]{1,0:T(8,128)S(1)} fusion(f32[5,2048]{0,1:T(8,128)S(1)} %get-tuple-element.407, s32[2048]{0:T(1024)S(1)} %bitcast_clamp_fusion.2), kind=kCustom, calls=%fused_computation.1.clone.clone.1 | custom fusion | bytes 90112 | tf_op jit(solution)/shard_map/while/body/eval_jaxpr/jit(_take)/gather | solution.py:23
  56.8 5.5 %gather_fusion = f32[2048,5]{1,0:T(8,128)S(1)} fusion(f32[5,2048]{0,1:T(8,128)S(1)} %get-tuple-element.407, s32[2048]{0:T(1024)S(1)} %bitcast_clamp_fusion.2), kind=kCustom, calls=%fused_computation.1.clone.clone.1 | custom fusion | bytes 90112 | tf_op jit(solution)/shard_map/while/body/eval_jaxpr/jit(_take)/gather | solution.py:23
  68.3 6.6 %collective-permute-start.6 = (f32[3,256]{0,1:T(8,128)S(1)}, f32[3,256]{0,1:T(8,128)S(1)}, u32[]{:S(2)}, u32[]{:S(2)}) collective-permute-start(f32[3,256]{0,1:T(8,128)S(1)} %slice.229), channel_id=1, source_target_pairs={{0,7},{1,0},{2,1},{3,2},{4,3},{5,4},{6,5},{7,6},{8,15},{9,8},{10,9... | collective-permute-start | bytes 9224 | tf_op jit(solution)/shard_map/ppermute | solution.py:18
  77.1 244.1 %while.15 = (s32[]{:T(128)}, f32[5,1024]{0,1:T(8,128)S(1)}, s32[128,2]{0,1:T(2,128)S(1)}, f32[128,3]{1,0:T(8,128)S(1)}, s32[]{:T(128)}, /*index=5*/s32[]{:T(128)}) while((s32[]{:T(128)}, f32[5,1024]{0,1:T(8,128)S(1)}, s32[128,2]{0,1:T(2,128)S(1)}, f32[128,3]{1,0:T(8,128)S(1)}, s32[]{:T(128)}, /*index=5*/s32[]{:T(128)}) %tuple.100), condition=%wide.while_cond, body=%wide.while_body.sunk | while | flops 2 | bytes 165 | solution.py:130
  325.7 3.3 collective-permute-start.10
  329.0 3.3 collective-permute-start.11
  332.3 3.8 collective-permute-start.13
  351.1 4.3 collective-permute-start.16
  356.2 3.0 collective-permute-done.15
  359.2 3.0 collective-permute-done.17
  366.2 3.0 collective-permute-start.19
  369.2 3.8 collective-permute-start.21
  386.0 4.2 collective-permute-start.24
  391.1 4.1 collective-permute-done.23
  400.7 3.3 collective-permute-start.27
  403.9 3.8 collective-permute-start.29
  407.8 2.9 collective-permute-done.28
  420.3 3.8 collective-permute-start.32
  425.0 3.4 collective-permute-done.31
  434.6 3.3 collective-permute-start.35
  437.8 3.8 collective-permute-start.37
  441.7 2.9 collective-permute-done.36
  454.2 3.8 collective-permute-start.40
  458.9 3.0 collective-permute-done.39
  461.9 3.0 collective-permute-done.41
  469.0 2.8 collective-permute-start.43
  471.9 3.8 collective-permute-start.45
  475.7 2.9 collective-permute-done.44
  (800 shorter events, 365.2 us)
Async XLA Ops:
  2.4 18.6 %collective-permute-start = (f32[5,256]{1,0:T(8,128)S(1)}, f32[5,256]{1,0:T(8,128)S(1)}, u32[]{:S(2)}, u32[]{:S(2)}) collective-permute-start(f32[5,256]{1,0:T(8,128)S(1)} %slice.228), channel_id=1, source_target_pairs={{0,7},{1,0},{2,1},{3,2},{4,3},{5,4},{6,5},{7,6},{8,15},{9,8},{10,9... | collective-permute-start | bytes 15368 | tf_op jit(solution)/shard_map/ppermute | solution.py:18
  8.5 14.3 %collective-permute-start.1 = (f32[5,256]{1,0:T(8,128)S(1)}, f32[5,256]{1,0:T(8,128)S(1)}, u32[]{:S(2)}, u32[]{:S(2)}) collective-permute-start(f32[5,256]{1,0:T(8,128)S(1)} %slice.228), channel_id=1, source_target_pairs={{0,1},{1,2},{2,3},{3,4},{4,5},{5,6},{6,7},{7,0},{8,9},{9,10},{10,1... | collective-permute-start | bytes 15368 | tf_op jit(solution)/shard_map/ppermute | solution.py:18
  8.5 14.3 %collective-permute-start.2 = (f32[5,256]{1,0:T(8,128)S(1)}, f32[5,256]{1,0:T(8,128)S(1)}, u32[]{:S(2)}, u32[]{:S(2)}) collective-permute-start(f32[5,256]{1,0:T(8,128)S(1)} %slice.228), channel_id=1, source_target_pairs={{0,6},{1,7},{2,0},{3,1},{4,2},{5,3},{6,4},{7,5},{8,14},{9,15},{10,... | collective-permute-start | bytes 15368 | tf_op jit(solution)/shard_map/ppermute | solution.py:18
  9.5 13.3 %collective-permute-start.3 = (f32[5,256]{1,0:T(8,128)S(1)}, f32[5,256]{1,0:T(8,128)S(1)}, u32[]{:S(2)}, u32[]{:S(2)}) collective-permute-start(f32[5,256]{1,0:T(8,128)S(1)} %slice.228), channel_id=1, source_target_pairs={{0,2},{1,3},{2,4},{3,5},{4,6},{5,7},{6,0},{7,1},{8,10},{9,11},{10,... | collective-permute-start | bytes 15368 | tf_op jit(solution)/shard_map/ppermute | solution.py:18
  10.5 12.4 %collective-permute-start.4 = (f32[5,256]{1,0:T(8,128)S(1)}, f32[5,256]{1,0:T(8,128)S(1)}, u32[]{:S(2)}, u32[]{:S(2)}) collective-permute-start(f32[5,256]{1,0:T(8,128)S(1)} %slice.228), channel_id=1, source_target_pairs={{0,8},{8,16},{16,24},{24,0},{1,9},{9,17},{17,25},{25,1},{2,10},{10... | collective-permute-start | bytes 15368 | tf_op jit(solution)/shard_map/ppermute | solution.py:18
  68.3 255.2 %collective-permute-start.6 = (f32[3,256]{0,1:T(8,128)S(1)}, f32[3,256]{0,1:T(8,128)S(1)}, u32[]{:S(2)}, u32[]{:S(2)}) collective-permute-start(f32[3,256]{0,1:T(8,128)S(1)} %slice.229), channel_id=1, source_target_pairs={{0,7},{1,0},{2,1},{3,2},{4,3},{5,4},{6,5},{7,6},{8,15},{9,8},{10,9... | collective-permute-start | bytes 9224 | tf_op jit(solution)/shard_map/ppermute | solution.py:18
  74.8 248.6 %collective-permute-start.7 = (f32[3,256]{0,1:T(8,128)S(1)}, f32[3,256]{0,1:T(8,128)S(1)}, u32[]{:S(2)}, u32[]{:S(2)}) collective-permute-start(f32[3,256]{0,1:T(8,128)S(1)} %slice.229), channel_id=1, source_target_pairs={{0,1},{1,2},{2,3},{3,4},{4,5},{5,6},{6,7},{7,0},{8,9},{9,10},{10,1... | collective-permute-start | bytes 9224 | tf_op jit(solution)/shard_map/ppermute | solution.py:18
  74.8 248.6 %collective-permute-start.8 = (f32[3,256]{0,1:T(8,128)S(1)}, f32[3,256]{0,1:T(8,128)S(1)}, u32[]{:S(2)}, u32[]{:S(2)}) collective-permute-start(f32[3,256]{0,1:T(8,128)S(1)} %slice.229), channel_id=1, source_target_pairs={{0,6},{1,7},{2,0},{3,1},{4,2},{5,3},{6,4},{7,5},{8,14},{9,15},{10,... | collective-permute-start | bytes 9224 | tf_op jit(solution)/shard_map/ppermute | solution.py:18
  75.5 248.0 %collective-permute-start.9 = (f32[3,256]{0,1:T(8,128)S(1)}, f32[3,256]{0,1:T(8,128)S(1)}, u32[]{:S(2)}, u32[]{:S(2)}) collective-permute-start(f32[3,256]{0,1:T(8,128)S(1)} %slice.229), channel_id=1, source_target_pairs={{0,2},{1,3},{2,4},{3,5},{4,6},{5,7},{6,0},{7,1},{8,10},{9,11},{10,... | collective-permute-start | bytes 9224 | tf_op jit(solution)/shard_map/ppermute | solution.py:18
  325.7 11.1 %collective-permute-start.10 = (f32[3,256]{0,1:T(8,128)S(1)}, f32[3,256]{0,1:T(8,128)S(1)}, u32[]{:S(2)}, u32[]{:S(2)}) collective-permute-start(f32[3,256]{0,1:T(8,128)S(1)} %get-tuple-element.286), channel_id=1, source_target_pairs={{0,1},{1,2},{2,3},{3,4},{4,5},{5,6},{6,7},{7,0},{8,9},{9,10},{10,1... | collective-permute-start | bytes 9224 | tf_op jit(solution)/shard_map/ppermute | solution.py:18
  329.0 8.7 %collective-permute-start.11 = (f32[3,256]{0,1:T(8,128)S(1)}, f32[3,256]{0,1:T(8,128)S(1)}, u32[]{:S(2)}, u32[]{:S(2)}) collective-permute-start(f32[3,256]{0,1:T(8,128)S(1)} %get-tuple-element.283), channel_id=1, source_target_pairs={{0,7},{1,0},{2,1},{3,2},{4,3},{5,4},{6,5},{7,6},{8,15},{9,8},{10,9... | collective-permute-start | bytes 9224 | tf_op jit(solution)/shard_map/ppermute | solution.py:18
  332.3 8.1 %collective-permute-start.12 = (f32[3,256]{0,1:T(8,128)S(1)}, f32[3,256]{0,1:T(8,128)S(1)}, u32[]{:S(2)}, u32[]{:S(2)}) collective-permute-start(f32[3,256]{0,1:T(8,128)S(1)} %get-tuple-element.285), channel_id=1, source_target_pairs={{0,2},{1,3},{2,4},{3,5},{4,6},{5,7},{6,0},{7,1},{8,10},{9,11},{10,... | collective-permute-start | bytes 9224 | tf_op jit(solution)/shard_map/ppermute | solution.py:18
  332.3 9.0 %collective-permute-start.13 = (f32[3,256]{0,1:T(8,128)S(1)}, f32[3,256]{0,1:T(8,128)S(1)}, u32[]{:S(2)}, u32[]{:S(2)}) collective-permute-start(f32[3,256]{0,1:T(8,128)S(1)} %get-tuple-element.284), channel_id=1, source_target_pairs={{0,6},{1,7},{2,0},{3,1},{4,2},{5,3},{6,4},{7,5},{8,14},{9,15},{10,... | collective-permute-start | bytes 9224 | tf_op jit(solution)/shard_map/ppermute | solution.py:18
  349.0 7.2 %collective-permute-start.14 = (f32[3,256]{0,1:T(8,128)S(1)}, f32[3,256]{0,1:T(8,128)S(1)}, u32[]{:S(2)}, u32[]{:S(2)}) collective-permute-start(f32[3,256]{0,1:T(8,128)S(1)} %slice.234), channel_id=1, source_target_pairs={{0,7},{1,0},{2,1},{3,2},{4,3},{5,4},{6,5},{7,6},{8,15},{9,8},{10,9... | collective-permute-start | bytes 9224 | tf_op jit(solution)/shard_map/ppermute | solution.py:18
  350.1 9.1 %collective-permute-start.15 = (f32[3,256]{0,1:T(8,128)S(1)}, f32[3,256]{0,1:T(8,128)S(1)}, u32[]{:S(2)}, u32[]{:S(2)}) collective-permute-start(f32[3,256]{0,1:T(8,128)S(1)} %slice.234), channel_id=1, source_target_pairs={{0,1},{1,2},{2,3},{3,4},{4,5},{5,6},{6,7},{7,0},{8,9},{9,10},{10,1... | collective-permute-start | bytes 9224 | tf_op jit(solution)/shard_map/ppermute | solution.py:18
  351.1 8.2 %collective-permute-start.16 = (f32[3,256]{0,1:T(8,128)S(1)}, f32[3,256]{0,1:T(8,128)S(1)}, u32[]{:S(2)}, u32[]{:S(2)}) collective-permute-start(f32[3,256]{0,1:T(8,128)S(1)} %slice.234), channel_id=1, source_target_pairs={{0,6},{1,7},{2,0},{3,1},{4,2},{5,3},{6,4},{7,5},{8,14},{9,15},{10,... | collective-permute-start | bytes 9224 | tf_op jit(solution)/shard_map/ppermute | solution.py:18
  364.4 9.2 %collective-permute-start.18 = (f32[3,256]{0,1:T(8,128)S(1)}, f32[3,256]{0,1:T(8,128)S(1)}, u32[]{:S(2)}, u32[]{:S(2)}) collective-permute-start(f32[3,256]{0,1:T(8,128)S(1)} %get-tuple-element.282), channel_id=1, source_target_pairs={{0,1},{1,2},{2,3},{3,4},{4,5},{5,6},{6,7},{7,0},{8,9},{9,10},{10,1... | collective-permute-start | bytes 9224 | tf_op jit(solution)/shard_map/ppermute | solution.py:18
  366.2 7.4 %collective-permute-start.19 = (f32[3,256]{0,1:T(8,128)S(1)}, f32[3,256]{0,1:T(8,128)S(1)}, u32[]{:S(2)}, u32[]{:S(2)}) collective-permute-start(f32[3,256]{0,1:T(8,128)S(1)} %get-tuple-element.279), channel_id=1, source_target_pairs={{0,7},{1,0},{2,1},{3,2},{4,3},{5,4},{6,5},{7,6},{8,15},{9,8},{10,9... | collective-permute-start | bytes 9224 | tf_op jit(solution)/shard_map/ppermute | solution.py:18
  369.2 7.0 %collective-permute-start.20 = (f32[3,256]{0,1:T(8,128)S(1)}, f32[3,256]{0,1:T(8,128)S(1)}, u32[]{:S(2)}, u32[]{:S(2)}) collective-permute-start(f32[3,256]{0,1:T(8,128)S(1)} %get-tuple-element.281), channel_id=1, source_target_pairs={{0,2},{1,3},{2,4},{3,5},{4,6},{5,7},{6,0},{7,1},{8,10},{9,11},{10,... | collective-permute-start | bytes 9224 | tf_op jit(solution)/shard_map/ppermute | solution.py:18
  369.2 7.2 %collective-permute-start.21 = (f32[3,256]{0,1:T(8,128)S(1)}, f32[3,256]{0,1:T(8,128)S(1)}, u32[]{:S(2)}, u32[]{:S(2)}) collective-permute-start(f32[3,256]{0,1:T(8,128)S(1)} %get-tuple-element.280), channel_id=1, source_target_pairs={{0,6},{1,7},{2,0},{3,1},{4,2},{5,3},{6,4},{7,5},{8,14},{9,15},{10,... | collective-permute-start | bytes 9224 | tf_op jit(solution)/shard_map/ppermute | solution.py:18
  384.0 7.1 %collective-permute-start.22 = (f32[3,256]{0,1:T(8,128)S(1)}, f32[3,256]{0,1:T(8,128)S(1)}, u32[]{:S(2)}, u32[]{:S(2)}) collective-permute-start(f32[3,256]{0,1:T(8,128)S(1)} %slice.239), channel_id=1, source_target_pairs={{0,7},{1,0},{2,1},{3,2},{4,3},{5,4},{6,5},{7,6},{8,15},{9,8},{10,9... | collective-permute-start | bytes 9224 | tf_op jit(solution)/shard_map/ppermute | solution.py:18
  385.9 9.2 %collective-permute-start.23 = (f32[3,256]{0,1:T(8,128)S(1)}, f32[3,256]{0,1:T(8,128)S(1)}, u32[]{:S(2)}, u32[]{:S(2)}) collective-permute-start(f32[3,256]{0,1:T(8,128)S(1)} %slice.239), channel_id=1, source_target_pairs={{0,1},{1,2},{2,3},{3,4},{4,5},{5,6},{6,7},{7,0},{8,9},{9,10},{10,1... | collective-permute-start | bytes 9224 | tf_op jit(solution)/shard_map/ppermute | solution.py:18
  386.0 9.1 %collective-permute-start.24 = (f32[3,256]{0,1:T(8,128)S(1)}, f32[3,256]{0,1:T(8,128)S(1)}, u32[]{:S(2)}, u32[]{:S(2)}) collective-permute-start(f32[3,256]{0,1:T(8,128)S(1)} %slice.239), channel_id=1, source_target_pairs={{0,6},{1,7},{2,0},{3,1},{4,2},{5,3},{6,4},{7,5},{8,14},{9,15},{10,... | collective-permute-start | bytes 9224 | tf_op jit(solution)/shard_map/ppermute | solution.py:18
  399.2 8.7 %collective-permute-start.26 = (f32[3,256]{0,1:T(8,128)S(1)}, f32[3,256]{0,1:T(8,128)S(1)}, u32[]{:S(2)}, u32[]{:S(2)}) collective-permute-start(f32[3,256]{0,1:T(8,128)S(1)} %get-tuple-element.278), channel_id=1, source_target_pairs={{0,1},{1,2},{2,3},{3,4},{4,5},{5,6},{6,7},{7,0},{8,9},{9,10},{10,1... | collective-permute-start | bytes 9224 | tf_op jit(solution)/shard_map/ppermute | solution.py:18
  400.7 7.2 %collective-permute-start.27 = (f32[3,256]{0,1:T(8,128)S(1)}, f32[3,256]{0,1:T(8,128)S(1)}, u32[]{:S(2)}, u32[]{:S(2)}) collective-permute-start(f32[3,256]{0,1:T(8,128)S(1)} %get-tuple-element.275), channel_id=1, source_target_pairs={{0,7},{1,0},{2,1},{3,2},{4,3},{5,4},{6,5},{7,6},{8,15},{9,8},{10,9... | collective-permute-start | bytes 9224 | tf_op jit(solution)/shard_map/ppermute | solution.py:18
  420.3 8.1 %collective-permute-start.31 = (f32[3,256]{0,1:T(8,128)S(1)}, f32[3,256]{0,1:T(8,128)S(1)}, u32[]{:S(2)}, u32[]{:S(2)}) collective-permute-start(f32[3,256]{0,1:T(8,128)S(1)} %slice.244), channel_id=1, source_target_pairs={{0,1},{1,2},{2,3},{3,4},{4,5},{5,6},{6,7},{7,0},{8,9},{9,10},{10,1... | collective-permute-start | bytes 9224 | tf_op jit(solution)/shard_map/ppermute | solution.py:18
  420.3 8.1 %collective-permute-start.32 = (f32[3,256]{0,1:T(8,128)S(1)}, f32[3,256]{0,1:T(8,128)S(1)}, u32[]{:S(2)}, u32[]{:S(2)}) collective-permute-start(f32[3,256]{0,1:T(8,128)S(1)} %slice.244), channel_id=1, source_target_pairs={{0,6},{1,7},{2,0},{3,1},{4,2},{5,3},{6,4},{7,5},{8,14},{9,15},{10,... | collective-permute-start | bytes 9224 | tf_op jit(solution)/shard_map/ppermute | solution.py:18
  433.1 8.6 %collective-permute-start.34 = (f32[3,256]{0,1:T(8,128)S(1)}, f32[3,256]{0,1:T(8,128)S(1)}, u32[]{:S(2)}, u32[]{:S(2)}) collective-permute-start(f32[3,256]{0,1:T(8,128)S(1)} %get-tuple-element.274), channel_id=1, source_target_pairs={{0,1},{1,2},{2,3},{3,4},{4,5},{5,6},{6,7},{7,0},{8,9},{9,10},{10,1... | collective-permute-start | bytes 9224 | tf_op jit(solution)/shard_map/ppermute | solution.py:18
  434.6 7.1 %collective-permute-start.35 = (f32[3,256]{0,1:T(8,128)S(1)}, f32[3,256]{0,1:T(8,128)S(1)}, u32[]{:S(2)}, u32[]{:S(2)}) collective-permute-start(f32[3,256]{0,1:T(8,128)S(1)} %get-tuple-element.271), channel_id=1, source_target_pairs={{0,7},{1,0},{2,1},{3,2},{4,3},{5,4},{6,5},{7,6},{8,15},{9,8},{10,9... | collective-permute-start | bytes 9224 | tf_op jit(solution)/shard_map/ppermute | solution.py:18
  454.2 7.7 %collective-permute-start.39 = (f32[3,256]{0,1:T(8,128)S(1)}, f32[3,256]{0,1:T(8,128)S(1)}, u32[]{:S(2)}, u32[]{:S(2)}) collective-permute-start(f32[3,256]{0,1:T(8,128)S(1)} %slice.249), channel_id=1, source_target_pairs={{0,1},{1,2},{2,3},{3,4},{4,5},{5,6},{6,7},{7,0},{8,9},{9,10},{10,1... | collective-permute-start | bytes 9224 | tf_op jit(solution)/shard_map/ppermute | solution.py:18
  454.2 7.7 %collective-permute-start.40 = (f32[3,256]{0,1:T(8,128)S(1)}, f32[3,256]{0,1:T(8,128)S(1)}, u32[]{:S(2)}, u32[]{:S(2)}) collective-permute-start(f32[3,256]{0,1:T(8,128)S(1)} %slice.249), channel_id=1, source_target_pairs={{0,6},{1,7},{2,0},{3,1},{4,2},{5,3},{6,4},{7,5},{8,14},{9,15},{10,... | collective-permute-start | bytes 9224 | tf_op jit(solution)/shard_map/ppermute | solution.py:18
  467.1 8.6 %collective-permute-start.42 = (f32[3,256]{0,1:T(8,128)S(1)}, f32[3,256]{0,1:T(8,128)S(1)}, u32[]{:S(2)}, u32[]{:S(2)}) collective-permute-start(f32[3,256]{0,1:T(8,128)S(1)} %get-tuple-element.270), channel_id=1, source_target_pairs={{0,1},{1,2},{2,3},{3,4},{4,5},{5,6},{6,7},{7,0},{8,9},{9,10},{10,1... | collective-permute-start | bytes 9224 | tf_op jit(solution)/shard_map/ppermute | solution.py:18
  (22 other events, 175.4 us)
where the time goes:
time: 491 us; the launch traced here: 486 us
  local copies, waits for them, and re-layouts  295 us (60%)
  starting transfers between devices  87.7 us (18%)
  other arithmetic  55.8 us (11%)
  waiting for transfers between devices  42.6 us (9%)
    gather x512, local copies, waits for them, and re-layouts  243 us
    ppermute x46, starting transfers between devices, passed_along(): lax.ppermute(array, axis, [(i, (i + by) % length) for i in range(length)])  87.7 us
    ppermute x46, waiting for transfers between devices, passed_along(): lax.ppermute(array, axis, [(i, (i + by) % length) for i in range(length)])  42.6 us
    gather x8, local copies, waits for them, and re-layouts, group_force(): far_data = jnp.take(halo_data, atom_ids, axis=1)  23.2 us
    scatter-add x10, other arithmetic, collect(): totals = jnp.zeros((3, atom_count), jnp.float32).at[:, bond_left].add(pus...  21.8 us
  transfers between devices with their start and end apart: 46, of which 20 were waited for; matrix products, arithmetic and copies ran while one was open for 53% of the time, Pallas kernels for 0%

commit v1 on v0

v1 whole, which is shorter than its diff:
```python
import functools

import jax
import jax.numpy as jnp
from jax import lax
from jax.experimental import pallas as pl
from jax.experimental.pallas import tpu as pltpu
from jax.sharding import PartitionSpec as P

TILE = 128
ORDER = 4
LANES = 128
SUBLANES = 8

time_step = 0.1
cutoff_sq = 16.0
force_scale = 4.0
length_floor = 0.25

VMEM_LIMIT = 48 * 1024 * 1024


def passed_along(array, axis, by):
    length = lax.axis_size(axis)
    return lax.ppermute(array, axis, [(i, (i + by) % length) for i in range(length)])


def strides_of(domains):
    row_width = max(2, domains // 8)
    return (1, -1, row_width, -row_width)


def round_up(count, step):
    return -(-count // step) * step


class Rows:
    def __init__(self, atoms, bonds, slots):
        self.atom_rows = atoms // LANES
        self.shell_rows = atoms // 2 // LANES
        self.bond_rows = bonds // LANES
        self.slot_rows = slots // LANES
        at = 0
        self.coords = []
        for _ in range(3):
            self.coords.append(at)
            at += self.atom_rows
        self.charge = at
        at += self.atom_rows
        self.mass = at
        at += self.atom_rows
        self.bond_first = at
        at += self.bond_rows
        self.bond_second = at
        at += self.bond_rows
        self.cross_first = at
        at += self.slot_rows
        self.cross_second = at
        at += self.slot_rows
        self.side = at
        at += self.slot_rows
        self.live = at
        at += self.slot_rows
        self.used = at
        self.count = round_up(at, SUBLANES)
        self.disp_used = 3 * self.atom_rows
        self.disp_count = round_up(self.disp_used, SUBLANES)


def take_lanes(table, lanes):
    return jnp.take_along_axis(table, lanes, axis=1, mode="promise_in_bounds")


def pick(tables, index):
    lanes = index & (LANES - 1)
    chunk = index >> 7
    result = take_lanes(tables[0], lanes)
    for k in range(1, len(tables)):
        result = jnp.where(chunk == k, take_lanes(tables[k], lanes), result)
    return result


def rsqrt(value):
    guess = lax.rsqrt(value)
    return guess * (1.5 - 0.5 * value * guess * guess)


def pack_kernel(
    rows, copies, count_ref, coords_ref, charge_ref, mass_ref, bonds_ref, cross_ref, side_ref, out_ref, rim_ref
):
    def put(row, value):
        for part in range(value.shape[1] // LANES):
            piece = value[:, part * LANES : (part + 1) * LANES]
            for copy in range(copies):
                out_ref[pl.ds(copy * rows.count + row + part, 1), :] = piece

    shell = rows.shell_rows * LANES
    fields = [coords_ref[c, 0] for c in range(3)] + [charge_ref[0]]
    for c in range(4):
        at = rows.coords[c] if c < 3 else rows.charge
        put(at, fields[c])
        for part in range(rows.shell_rows):
            rim_ref[pl.ds(c * rows.shell_rows + part, 1), :] = fields[c][:, part * LANES : (part + 1) * LANES]
    put(rows.mass, mass_ref[0])
    put(rows.bond_first, bonds_ref[0, 0].astype(jnp.float32))
    put(rows.bond_second, bonds_ref[1, 0].astype(jnp.float32))
    put(rows.cross_first, cross_ref[0, 0].astype(jnp.float32))
    put(rows.cross_second, cross_ref[1, 0].astype(jnp.float32))
    side = side_ref[0]
    put(rows.side, side.astype(jnp.float32))
    slot = lax.broadcasted_iota(jnp.int32, side.shape, 1)
    put(rows.live, jnp.where(slot < count_ref[0, 0], 1.0, 0.0))
    if rows.count > rows.used:
        for copy in range(copies):
            out_ref[pl.ds(copy * rows.count + rows.used, rows.count - rows.used), :] = jnp.zeros(
                (rows.count - rows.used, LANES), jnp.float32
            )


def force_kernel(
    rows,
    copies,
    holders,
    here_ref,
    live_ref,
    block_ref,
    around_ref,
    below_ref,
    above_ref,
    velocity_ref,
    atoms_ref,
    out_ref,
    table_ref,
    far_ref,
    own_ref,
    sum_ref,
):
    atom_rows, shell_rows = rows.atom_rows, rows.shell_rows
    tiles = atoms_ref.shape[2]
    me = here_ref[0]
    starts = [rows.coords[0], rows.coords[1], rows.coords[2], rows.charge]
    entry_rows = atom_rows + 6 * shell_rows
    blocks = around_ref.shape[0] // rows.count
    shrink = 1.0 / 4.0

    def broadcast(row):
        return jnp.broadcast_to(row, (SUBLANES, LANES))

    for c in range(4):
        factor = shrink if c < 3 else 1.0
        at = 0
        for part in range(atom_rows):
            table_ref[c, at] = broadcast(around_ref[pl.ds(me * rows.count + starts[c] + part, 1), :] * factor)
            at += 1
        for neighbour in range(4):
            base = lax.rem(me + holders[neighbour], blocks) * rows.count + starts[c]
            for part in range(shell_rows):
                table_ref[c, at] = broadcast(around_ref[pl.ds(base + part, 1), :] * factor)
                at += 1
        for slab_ref in (below_ref, above_ref):
            for part in range(shell_rows):
                table_ref[c, at] = broadcast(slab_ref[pl.ds(c * shell_rows + part, 1), :] * factor)
                at += 1

    for group in range(tiles // SUBLANES):
        index = atoms_ref[0, 0, pl.ds(group * SUBLANES, SUBLANES), :]
        lanes = index & (LANES - 1)
        chunk = index >> 7
        values = [take_lanes(table_ref[c, 0], lanes) for c in range(4)]
        for k in range(1, entry_rows):
            here = chunk == k
            values = [jnp.where(here, take_lanes(table_ref[c, k], lanes), values[c]) for c in range(4)]
        for c in range(4):
            far_ref[c, pl.ds(group * SUBLANES, SUBLANES), :] = values[c]

    down = lax.broadcasted_iota(jnp.int32, (SUBLANES, LANES), 0)
    zero = jnp.zeros((SUBLANES, LANES), jnp.float32)
    for part in range(atom_rows):
        for group in range(LANES // SUBLANES):
            at = part * LANES + group * SUBLANES
            for c in range(4):
                value = take_lanes(table_ref[c, part], down + group * SUBLANES)
                own_ref[c, pl.ds(at, SUBLANES), :] = value if c < 3 else value * 8.0
            for c in range(3):
                sum_ref[c, pl.ds(at, SUBLANES), :] = zero

    def add_tile(tile, _):
        base = block_ref[0, 0, tile] * TILE
        far = [broadcast(far_ref[c, pl.ds(tile, 1), :]) for c in range(4)]
        for group in range(TILE // SUBLANES):
            at = pl.ds(pl.multiple_of(base + group * SUBLANES, SUBLANES), SUBLANES)
            gap = [own_ref[c, at, :] - far[c] for c in range(3)]
            square = gap[0] * gap[0] + gap[1] * gap[1] + gap[2] * gap[2]
            shifted = square + 1.0 / cutoff_sq
            inverse = pl.reciprocal(shifted, approx=True)
            inverse = inverse * (2.0 - shifted * inverse)
            switch = jnp.maximum(1.0 - square, 0.0)
            weight = inverse * switch
            strength = (inverse - own_ref[3, at, :] * far[3]) * (weight * weight)
            for c in range(3):
                sum_ref[c, at, :] = sum_ref[c, at, :] + strength * gap[c]
        return 0

    lax.fori_loop(0, live_ref[0, 0], add_tile, 0)

    scale = time_step * time_step * force_scale * 4.0 / 2048.0
    for c in range(3):
        speed = velocity_ref[c, 0]
        for part in range(atom_rows):
            total = jnp.sum(sum_ref[c, pl.ds(part * LANES, LANES), :].T, axis=0, keepdims=True)
            mass = around_ref[pl.ds(me * rows.count + rows.mass + part, 1), :]
            moved = time_step * speed[:, part * LANES : (part + 1) * LANES] + scale * total * mass
            for copy in range(copies):
                out_ref[pl.ds(copy * rows.disp_count + c * atom_rows + part, 1), :] = moved
    if rows.disp_count > rows.disp_used:
        for copy in range(copies):
            out_ref[pl.ds(copy * rows.disp_count + rows.disp_used, rows.disp_count - rows.disp_used), :] = jnp.zeros(
                (rows.disp_count - rows.disp_used, LANES), jnp.float32
            )


def bond_kernel(rows, domains, strides, around_ref, weight_ref, inner_ref, cross_ref, key_ref):
    atom_rows, shell_rows = rows.atom_rows, rows.shell_rows

    def load(row):
        return around_ref[pl.ds(row, domains, stride=rows.count), :]

    def index(row):
        return load(row).astype(jnp.int32)

    fields = [[load(at + part) for part in range(atom_rows)] for at in rows.coords + [rows.mass]]

    def weights(first, second, row):
        gap = [first[c] - second[c] for c in range(3)]
        length_sq = gap[0] * gap[0] + gap[1] * gap[1] + gap[2] * gap[2] + length_floor
        scale = rsqrt(length_sq) * rsqrt(first[3] + second[3])
        return [gap[c] * scale for c in range(3)]

    at = 0
    for part in range(rows.bond_rows):
        first = index(rows.bond_first + part)
        second = index(rows.bond_second + part)
        values = weights([pick(f, first) for f in fields], [pick(f, second) for f in fields], at)
        for c in range(3):
            weight_ref[pl.ds((at * 3 + c) * domains, domains), :] = values[c]
        at += 1
    for part in range(rows.slot_rows):
        first = index(rows.cross_first + part)
        second = index(rows.cross_second + part)
        side = load(rows.side + part)
        live = load(rows.live + part)
        other = [jnp.zeros((domains, LANES), jnp.float32) for _ in range(4)]
        for code, stride in enumerate(strides):
            seen = pltpu.roll(second, stride % domains, 0)
            for f in range(4):
                value = pltpu.roll(pick(fields[f][:shell_rows], seen), -stride % domains, 0)
                other[f] = jnp.where(side == code, value, other[f])
            key = jnp.where(side == code, load(rows.cross_second + part), -1.0)
            key_ref[pl.ds((part * 4 + code) * domains, domains), :] = key
        values = weights([pick(f[:shell_rows], first) for f in fields], other, at)
        for c in range(3):
            weight_ref[pl.ds((at * 3 + c) * domains, domains), :] = values[c] * live
        at += 1

    down = lax.broadcasted_iota(jnp.int32, (SUBLANES, LANES), 0)
    across = lax.broadcasted_iota(jnp.int32, (SUBLANES, LANES), 1).astype(jnp.float32)
    pair = 2 * SUBLANES

    def column(row, group):
        return take_lanes(jnp.broadcast_to(row, (SUBLANES, LANES)), down + group * SUBLANES)

    def one_hot(values, part):
        return jnp.where(values == across + float(part * LANES), 1.0, 0.0)

    def build(domain, _):
        for part in range(rows.bond_rows):
            first = around_ref[pl.ds(domain * rows.count + rows.bond_first + part, 1), :]
            second = around_ref[pl.ds(domain * rows.count + rows.bond_second + part, 1), :]
            for step in range(LANES // pair):
                ends = [(column(first, 2 * step + h), column(second, 2 * step + h)) for h in range(2)]
                at = pl.multiple_of((domain * rows.bond_rows + part) * LANES + step * pair, pair)
                for block in range(atom_rows):
                    halves = [one_hot(a, block) - one_hot(b, block) for a, b in ends]
                    inner_ref[pl.ds(at, pair), block * LANES : (block + 1) * LANES] = jnp.concatenate(
                        halves, axis=0
                    ).astype(jnp.bfloat16)
        for part in range(rows.slot_rows):
            for code in range(5):
                if code == 0:
                    row = around_ref[pl.ds(domain * rows.count + rows.cross_first + part, 1), :]
                else:
                    owner = lax.rem(domain + (-strides[code - 1]) % domains, domains)
                    row = key_ref[pl.ds((part * 4 + code - 1) * domains + owner, 1), :]
                sign = 1.0 if code == 0 else -1.0
                for step in range(LANES // pair):
                    ends = [column(row, 2 * step + h) for h in range(2)]
                    at = pl.multiple_of(((domain * rows.slot_rows + part) * 5 + code) * LANES + step * pair, pair)
                    for block in range(shell_rows):
                        halves = [sign * one_hot(a, block) for a in ends]
                        cross_ref[pl.ds(at, pair), block * LANES : (block + 1) * LANES] = jnp.concatenate(
                            halves, axis=0
                        ).astype(jnp.bfloat16)
        return 0

    lax.fori_loop(0, domains, build, 0)


def solve_kernel(
    rows,
    domains,
    strides,
    here_ref,
    around_ref,
    moves_ref,
    weight_ref,
    inner_ref,
    cross_ref,
    coords_out_ref,
    velocity_out_ref,
    push_ref,
    field_ref,
):
    atom_rows, shell_rows = rows.atom_rows, rows.shell_rows
    bond_rows, slot_rows = rows.bond_rows, rows.slot_rows
    me = here_ref[0]

    def load(row):
        return around_ref[pl.ds(row, domains, stride=rows.count), :]

    def index(row):
        return load(row).astype(jnp.int32)

    inner_first = [index(rows.bond_first + p) for p in range(bond_rows)]
    inner_second = [index(rows.bond_second + p) for p in range(bond_rows)]
    cross_first = [index(rows.cross_first + p) for p in range(slot_rows)]
    cross_second = [index(rows.cross_second + p) for p in range(slot_rows)]
    sides = [load(rows.side + p) for p in range(slot_rows)]
    masses = [load(rows.mass + p) for p in range(atom_rows)]

    def weight(at, c):
        return weight_ref[pl.ds((at * 3 + c) * domains, domains), :]

    def project(fields):
        result = []
        for part in range(bond_rows):
            total = 0.0
            for c in range(3):
                ends = pick(fields[c], inner_first[part]) - pick(fields[c], inner_second[part])
                total = total + weight(part, c) * ends
            result.append(total)
        for part in range(slot_rows):
            seen = [pltpu.roll(cross_second[part], stride % domains, 0) for stride in strides]
            total = 0.0
            for c in range(3):
                shell = fields[c][:shell_rows]
                other = 0.0
                for code, stride in enumerate(strides):
                    value = pltpu.roll(pick(shell, seen[code]), -stride % domains, 0)
                    other = jnp.where(sides[part] == code, value, other)
                total = total + weight(bond_rows + part, c) * (pick(shell, cross_first[part]) - other)
            result.append(total)
        return result

    def put_pushes(values):
        for at, value in enumerate(values):
            for c in range(3):
                pushed = weight(at, c) * value
                high = pushed.astype(jnp.bfloat16).astype(jnp.float32)
                push_ref[at, pl.ds(c * domains, domains), :] = high
                push_ref[at, pl.ds((3 + c) * domains, domains), :] = pushed - high

    def pushes_of(at, domain):
        return push_ref[at, pl.ds(domain, SUBLANES, stride=domains), :].astype(jnp.bfloat16)

    def totals(domain, owners):
        inner = jnp.concatenate([pushes_of(p, domain) for p in range(bond_rows)], axis=1)
        at = domain * bond_rows * LANES
        if not isinstance(at, int):
            at = pl.multiple_of(at, LANES)
        inner_sum = jnp.dot(inner, inner_ref[pl.ds(at, bond_rows * LANES), :], preferred_element_type=jnp.float32)
        pieces = []
        for part in range(slot_rows):
            pieces.extend(pushes_of(bond_rows + part, owner) for owner in [domain] + owners)
        cross = jnp.concatenate(pieces, axis=1)
        at = domain * slot_rows * 5 * LANES
        if not isinstance(at, int):
            at = pl.multiple_of(at, LANES)
        cross_sum = jnp.dot(
            cross, cross_ref[pl.ds(at, slot_rows * 5 * LANES), :], preferred_element_type=jnp.float32
        )
        shell = shell_rows * LANES
        return [
            inner_sum[:, p * LANES : (p + 1) * LANES]
            + (cross_sum[:, p * LANES : (p + 1) * LANES] if p < shell_rows else 0.0)
            for p in range(atom_rows)
        ]

    def spread(values):
        put_pushes(values)
        for domain in range(domains):
            sums = totals(domain, [(domain - stride) % domains for stride in strides])
            for part in range(atom_rows):
                field_ref[part, pl.ds(domain, SUBLANES, stride=domains), :] = sums[part]
        return [
            [
                masses[part]
                * (
                    field_ref[part, pl.ds(c * domains, domains), :]
                    + field_ref[part, pl.ds((3 + c) * domains, domains), :]
                )
                for part in range(atom_rows)
            ]
            for c in range(3)
        ]

    moves = [
        [moves_ref[pl.ds(c * atom_rows + p, domains, stride=rows.disp_count), :] for p in range(atom_rows)]
        for c in range(3)
    ]
    push_ref[...] = jnp.zeros(push_ref.shape, jnp.float32)
    residue = project(moves)

    def expand(_, carry):
        residue, summed = carry
        change = project(spread(residue))
        residue = [now - step for now, step in zip(residue, change)]
        return residue, [a + b for a, b in zip(summed, residue)]

    residue, summed = lax.fori_loop(0, ORDER, expand, (residue, residue))
    put_pushes(summed)
    sums = totals(me, [lax.rem(me + (-stride) % domains, domains) for stride in strides])
    for part in range(atom_rows):
        lanes = slice(part * LANES, (part + 1) * LANES)
        mass = around_ref[pl.ds(me * rows.count + rows.mass + part, 1), :]
        for c in range(3):
            correction = mass * (sums[part][c : c + 1, :] + sums[part][3 + c : 4 + c, :])
            move = moves_ref[pl.ds(me * rows.disp_count + c * atom_rows + part, 1), :] - correction
            start = around_ref[pl.ds(me * rows.count + rows.coords[c] + part, 1), :]
            coords_out_ref[c, 0, :, lanes] = start + move
            velocity_out_ref[c, 0, :, lanes] = move * (1.0 / time_step)


def vmem(count):
    return [pl.BlockSpec(memory_space=pltpu.VMEM)] * count


def smem(count):
    return [pl.BlockSpec(memory_space=pltpu.SMEM)] * count


def params():
    return pltpu.CompilerParams(vmem_limit_bytes=VMEM_LIMIT)


def cost(flops, moved):
    return pl.CostEstimate(flops=flops, bytes_accessed=moved, transcendentals=0)


def shards(
    coords,
    velocity,
    charge,
    inv_mass,
    tile_block,
    tile_atoms,
    active_tile_count,
    bond_atoms,
    cross_atoms,
    cross_side,
    cross_count,
):
    atoms = coords.shape[-1]
    tiles = tile_atoms.shape[2]
    domains = lax.axis_size("dom")
    strides = strides_of(domains)
    rows = Rows(atoms, bond_atoms.shape[-1], cross_side.shape[-1])
    whole_slab = domains == SUBLANES
    copies = domains if whole_slab else 1
    f32 = jnp.float32

    packed, rim = pl.pallas_call(
        functools.partial(pack_kernel, rows, copies),
        out_shape=(
            jax.ShapeDtypeStruct((copies * rows.count, LANES), f32),
            jax.ShapeDtypeStruct((4 * rows.shell_rows, LANES), f32),
        ),
        in_specs=smem(1) + vmem(6),
        out_specs=tuple(vmem(2)),
        compiler_params=params(),
        name="pack",
    )(cross_count, coords, charge, inv_mass, bond_atoms, cross_atoms, cross_side)

    below = passed_along(rim, "slab", 1)
    above = passed_along(rim, "slab", -1)
    if whole_slab:
        around = lax.all_to_all(packed, "dom", 0, 0, tiled=True)
        here = lax.axis_index("dom").reshape(1)
        holders = [stride % domains for stride in strides]
    else:
        around = jnp.concatenate([packed] + [passed_along(packed, "dom", -stride) for stride in strides], axis=0)
        here = jnp.zeros(1, jnp.int32)
        holders = [1, 2, 3, 4]

    entry_rows = rows.atom_rows + 6 * rows.shell_rows
    moves = pl.pallas_call(
        functools.partial(force_kernel, rows, copies, holders),
        out_shape=jax.ShapeDtypeStruct((copies * rows.disp_count, LANES), f32),
        in_specs=smem(3) + vmem(5),
        out_specs=vmem(1)[0],
        scratch_shapes=[
            pltpu.VMEM((4, entry_rows, SUBLANES, LANES), f32),
            pltpu.VMEM((4, tiles, LANES), f32),
            pltpu.VMEM((4, atoms, LANES), f32),
            pltpu.VMEM((3, atoms, LANES), f32),
        ],
        compiler_params=params(),
        cost_estimate=cost(30 * tiles * TILE * TILE, 4 * around.size),
        name="force",
    )(here, active_tile_count, tile_block, around, below, above, velocity, tile_atoms)

    if not whole_slab:
        return by_exchange(rows, strides, around, moves, cross_count)

    constraint_rows = rows.bond_rows + rows.slot_rows
    weight, inner, cross = pl.pallas_call(
        functools.partial(bond_kernel, rows, domains, strides),
        out_shape=(
            jax.ShapeDtypeStruct((constraint_rows * 3 * domains, LANES), f32),
            jax.ShapeDtypeStruct((domains * rows.bond_rows * LANES, atoms), jnp.bfloat16),
            jax.ShapeDtypeStruct((domains * rows.slot_rows * 5 * LANES, atoms // 2), jnp.bfloat16),
        ),
        in_specs=vmem(1),
        out_specs=tuple(vmem(3)),
        scratch_shapes=[pltpu.VMEM((rows.slot_rows * 4 * domains, LANES), f32)],
        compiler_params=params(),
        cost_estimate=cost(8 * domains * (rows.bond_rows * LANES * atoms + rows.slot_rows * 5 * LANES * atoms // 2), 4 * around.size),
        name="bonds",
    )(around)

    every_move = lax.all_to_all(moves, "dom", 0, 0, tiled=True)

    return pl.pallas_call(
        functools.partial(solve_kernel, rows, domains, strides),
        out_shape=(
            jax.ShapeDtypeStruct(coords.shape, f32),
            jax.ShapeDtypeStruct(coords.shape, f32),
        ),
        in_specs=smem(1) + vmem(5),
        out_specs=tuple(vmem(2)),
        scratch_shapes=[
            pltpu.VMEM((constraint_rows, SUBLANES * domains, LANES), f32),
            pltpu.VMEM((rows.atom_rows, SUBLANES * domains, LANES), f32),
        ],
        compiler_params=params(),
        name="solve",
    )(here, around, every_move, weight, inner, cross)


def by_exchange(rows, strides, around, moves, cross_count):
    atom_count = rows.atom_rows * LANES
    shell = rows.shell_rows * LANES
    inside = around.reshape(5, rows.count, LANES)

    def flat(at, count):
        return inside[0, at : at + count].reshape(-1)

    def neighbours(at):
        return inside[1:, at : at + rows.shell_rows].reshape(-1)

    coords = jnp.stack([flat(at, rows.atom_rows) for at in rows.coords])
    inv_mass = flat(rows.mass, rows.atom_rows)
    displace = moves[: rows.disp_used].reshape(3, atom_count)
    left = flat(rows.bond_first, rows.bond_rows).astype(jnp.int32)
    right = flat(rows.bond_second, rows.bond_rows).astype(jnp.int32)
    cross_left = flat(rows.cross_first, rows.slot_rows).astype(jnp.int32)
    cross_right = flat(rows.cross_second, rows.slot_rows).astype(jnp.int32)
    side = flat(rows.side, rows.slot_rows).astype(jnp.int32)
    flag = flat(rows.live, rows.slot_rows)
    cross_index = side * shell + cross_right
    far_coords = jnp.stack([neighbours(at) for at in rows.coords])
    far_mass = neighbours(rows.mass)

    def weights(first, second, mass_first, mass_second):
        gap = first - second
        length = jnp.sqrt(jnp.sum(gap * gap, axis=0) + length_floor)
        return gap / length * lax.rsqrt(mass_first + mass_second)

    inner = weights(coords[:, left], coords[:, right], inv_mass[left], inv_mass[right])
    cross = flag * weights(
        coords[:, cross_left], far_coords[:, cross_index], inv_mass[cross_left], far_mass[cross_index]
    )

    def project(field):
        rim = field[:, :shell]
        far = jnp.concatenate([passed_along(rim, "dom", -stride) for stride in strides], axis=1)
        return (
            jnp.sum(inner * (field[:, left] - field[:, right]), axis=0),
            jnp.sum(cross * (field[:, cross_left] - far[:, cross_index]), axis=0),
        )

    def spread(values):
        pushed = inner * values[0]
        pushed_cross = cross * values[1]
        totals = jnp.zeros((3, atom_count), jnp.float32).at[:, left].add(pushed).at[:, right].add(-pushed)
        totals = totals.at[:, cross_left].add(pushed_cross)
        outward = jnp.zeros((3, 4 * shell), jnp.float32).at[:, cross_index].add(-pushed_cross)
        for code, stride in enumerate(strides):
            totals = totals.at[:, :shell].add(
                passed_along(outward[:, code * shell : (code + 1) * shell], "dom", stride)
            )
        return inv_mass * totals

    residue = project(displace)
    summed = residue
    for _ in range(ORDER):
        change = project(spread(residue))
        residue = tuple(now - step for now, step in zip(residue, change))
        summed = tuple(a + b for a, b in zip(summed, residue))
    move = displace - spread(summed)
    return (
        (coords + move).reshape(3, 1, 1, atom_count),
        (move * (1.0 / time_step)).reshape(3, 1, 1, atom_count),
    )


def solution(mesh):
    return jax.shard_map(
        shards,
        mesh=mesh,
        in_specs=(
            P(None, "slab", "dom", None),
            P(None, "slab", "dom", None),
            P("slab", "dom", None),
            P("slab", "dom", None),
            P("slab", "dom", None),
            P("slab", "dom", None, None),
            P("slab", "dom"),
            P(None, "slab", "dom", None),
            P(None, "slab", "dom", None),
            P("slab", "dom", None),
            P("slab", "dom"),
        ),
        out_specs=(P(None, "slab", "dom", None), P(None, "slab", "dom", None)),
        check_vma=False,
    )
```

time: 491 us -> 45.4 us (0.09)
  local copies, waits for them, and re-layouts: 295 us -> 9.09 us
  starting transfers between devices: 87.7 us -> 12.4 us
  other arithmetic: 55.8 us -> 0 us
  waiting for transfers between devices: 42.6 us -> 7.62 us
  Pallas kernels: 0 us -> 13.9 us
    gather x551 -> x0, local copies, waits for them, and re-layouts: 291 us -> none
    ppermute x46 -> x2, starting transfers between devices: 87.7 us -> 0.65 us  [passed_along(): lax.ppermute(array, axis, [(i, (i + by) % length) for i in range(length)])]
    ppermute x46 -> x2, waiting for transfers between devices: 42.6 us -> 2.38 us  [passed_along(): lax.ppermute(array, axis, [(i, (i + by) % length) for i in range(length)])]
    scatter-add x20 -> x0, other arithmetic: 35.5 us -> none  [the longest x10 21.8 us: collect(): totals = jnp.zeros((3, atom_count), jnp.float32).at[:, bond_left].add(pus...]
    reduce_sum x20 -> x0, other arithmetic: 13.9 us -> none  [the longest x4 7.7 us: group_force(): forces = jnp.sum(strength[None] * offset_vec, axis=3)]
    pallas_call x0 -> x4, Pallas kernels: none -> 13.9 us  [the longest x1 4.72 us: shards(): pl.pallas_call(functools.partial(solve_kernel, rows, domains, strides), o...]
    all_to_all x0 -> x2, starting transfers between devices: none -> 11.7 us  [the longest x1 7.28 us: shards(): around = lax.all_to_all(packed, 'dom', 0, 0, tiled=True)]
    unnamed x27 -> x22, local copies, waits for them, and re-layouts: 3.05 us -> 9.09 us
  transfers between devices with their start and end apart: 46 -> 4, of which waited for: 20 -> 4; matrix products, arithmetic and copies ran while one was open for 53% -> 0% of each run, Pallas kernels for 0% -> 9%
where the time goes in v1:
time: 45.4 us; the launch traced here: 44.9 us
  Pallas kernels  13.9 us (31%)
  starting transfers between devices  12.4 us (27%)
  local copies, waits for them, and re-layouts  9.09 us (20%)
  waiting for transfers between devices  7.62 us (17%)
  between operations  1.97 us (4%)
    unnamed x22, local copies, waits for them, and re-layouts  9.09 us
    all_to_all x1, starting transfers between devices, shards(): around = lax.all_to_all(packed, 'dom', 0, 0, tiled=True)  7.28 us
    pallas_call x1, Pallas kernels, shards(): pl.pallas_call(functools.partial(solve_kernel, rows, domains, strides), o...  4.72 us
    pallas_call x1, Pallas kernels, shards(): pl.pallas_call(functools.partial(force_kernel, rows, copies, holders), ou...  4.43 us
    all_to_all x1, starting transfers between devices, shards(): every_move = lax.all_to_all(moves, 'dom', 0, 0, tiled=True)  4.42 us
    pallas_call x1, Pallas kernels, shards(): pl.pallas_call(functools.partial(bond_kernel, rows, domains, strides), ou...  3.98 us
    all_to_all x1, waiting for transfers between devices, shards(): around = lax.all_to_all(packed, 'dom', 0, 0, tiled=True)  3.66 us
    ppermute x2, waiting for transfers between devices, passed_along(): lax.ppermute(array, axis, [(i, (i + by) % length) for i in range(length)])  2.38 us
  transfers between devices with their start and end apart: 4, of which 4 were waited for; matrix products, arithmetic and copies ran while one was open for 0% of the time, Pallas kernels for 9%

profile of v1, /device:TPU:0, one launch (start us, length us, event | category | flops | bytes accessed | tf_op | source)
XLA Modules:
  0.0 44.9 jit_solution(16203801628679845059)
XLA Ops:
  1.3 0.0 copy-start.3
  1.3 0.7 %copy-done.3 = f32[3,1,1,512]{3,2,1,0:T(1,128)S(1)} copy-done((f32[3,1,1,512]{3,2,1,0:T(1,128)S(1)}, f32[3,1,1,512]{3,2,1,0:T(1,128)}, u32[]{:S(2)}) %copy-start.3) | copy-done | bytes 6168
  2.0 0.0 copy-start.5
  2.0 0.7 %copy-done.5 = f32[1,1,512]{2,1,0:T(1,128)S(1)} copy-done((f32[1,1,512]{2,1,0:T(1,128)S(1)}, f32[1,1,512]{2,1,0:T(1,128)}, u32[]{:S(2)}) %copy-start.5) | copy-done | bytes 2072
  2.7 0.0 copy-start.6
  2.7 0.7 %copy-done.6 = f32[1,1,512]{2,1,0:T(1,128)S(1)} copy-done((f32[1,1,512]{2,1,0:T(1,128)S(1)}, f32[1,1,512]{2,1,0:T(1,128)}, u32[]{:S(2)}) %copy-start.6) | copy-done | bytes 2072
  3.3 0.0 copy-start.7
  3.3 0.7 %copy-done.7 = s32[2,1,1,256]{3,2,1,0:T(1,128)S(1)} copy-done((s32[2,1,1,256]{3,2,1,0:T(1,128)S(1)}, s32[2,1,1,256]{3,2,1,0:T(1,128)}, u32[]{:S(2)}) %copy-start.7) | copy-done | bytes 2072
  4.0 0.0 copy-start.8
  4.0 0.7 %copy-done.8 = s32[2,1,1,128]{3,2,1,0:T(1,128)S(1)} copy-done((s32[2,1,1,128]{3,2,1,0:T(1,128)S(1)}, s32[2,1,1,128]{3,2,1,0:T(1,128)}, u32[]{:S(2)}) %copy-start.8) | copy-done | bytes 1048
  4.7 0.0 copy-start.10
  4.7 0.7 %copy-done.10 = s32[1,1,128]{2,1,0:T(1,128)S(1)} copy-done((s32[1,1,128]{2,1,0:T(1,128)S(1)}, s32[1,1,128]{2,1,0:T(1,128)}, u32[]{:S(2)}) %copy-start.10) | copy-done | bytes 536
  5.4 0.7 %pack.1 = (f32[256,128]{1,0:T(8,128)}, f32[8,128]{1,0:T(8,128)S(1)}) custom-call(s32[1,1]{1,0:T(1,128)S(6)} %copy.14.count_ref, f32[3,1,1,512]{3,2,1,0:T(1,128)S(1)} %copy-done.3, f32[1,1,512]{2,1,0:T(1,128)S(1)} %copy-done.5, f32[1,1,512]{2,1,0:T(1,128)S(1)} %copy-done.6, s32[2,1,1,256]{3,2,1,0:T(1,128)S(1)} %copy-done.7, s32[2,1,1,128]{3,2,1,0:T(1,128)S(1)} %copy-done.8, ...), custom_call_target="tpu_custom_call" | custom-call | tf_op jit(solution)/shard_map/pack/pallas_call | solution.py:481
  6.1 7.3 %all-to-all-start = ((f32[8,32,128]{2,1,0:T(8,128)}), f32[8,32,128]{2,1,0:T(8,128)S(1)}, u32[]{:S(2)}, u32[]{:S(2)}) async-start(f32[8,32,128]{2,1,0:T(8,128)} %bitcast.1), calls=%async_computation | async-start | bytes 262144 | tf_op jit(solution)/shard_map/all_to_all | solution.py:496
  13.4 0.7 %collective-permute-start.1 = (f32[8,128]{1,0:T(8,128)S(1)}, f32[8,128]{1,0:T(8,128)S(1)}, u32[]{:S(2)}, u32[]{:S(2)}) collective-permute-start(f32[8,128]{1,0:T(8,128)S(1)} %get-tuple-element.8), channel_id=1, source_target_pairs={{0,24},{8,0},{16,8},{24,16},{1,25},{9,1},{17,9},{25,17},{2,26},{10... | collective-permute-start | bytes 12296 | tf_op jit(solution)/shard_map/ppermute | solution.py:25
  14.0 0.0 collective-permute-start
  14.7 0.7 %collective-permute-done.1.above_ref = f32[8,128]{1,0:T(8,128)S(1)} collective-permute-done((f32[8,128]{1,0:T(8,128)S(1)}, f32[8,128]{1,0:T(8,128)S(1)}, u32[]{:S(2)}, u32[]{:S(2)}) %collective-permute-start.1) | collective-permute-done | bytes 4128 | tf_op jit(solution)/shard_map/ppermute | solution.py:25
  15.4 1.7 %collective-permute-done.below_ref = f32[8,128]{1,0:T(8,128)S(1)} collective-permute-done((f32[8,128]{1,0:T(8,128)S(1)}, f32[8,128]{1,0:T(8,128)S(1)}, u32[]{:S(2)}, u32[]{:S(2)}) %collective-permute-start) | collective-permute-done | bytes 4128 | tf_op jit(solution)/shard_map/ppermute | solution.py:25
  17.1 3.7 %all-to-all-done = f32[8,32,128]{2,1,0:T(8,128)S(1)} async-done(((f32[8,32,128]{2,1,0:T(8,128)}), f32[8,32,128]{2,1,0:T(8,128)S(1)}, u32[]{:S(2)}, u32[]{:S(2)}) %all-to-all-start) | async-done | bytes 131104 | tf_op jit(solution)/shard_map/all_to_all | solution.py:496
  20.7 0.0 copy-start.2
  20.7 0.8 %copy-done.2 = s32[1,1,64,128]{3,2,1,0:T(8,128)S(1)} copy-done((s32[1,1,64,128]{3,2,1,0:T(8,128)S(1)}, s32[1,1,64,128]{3,2,1,0:T(8,128)}, u32[]{:S(2)}) %copy-start.2) | copy-done | bytes 32792
  21.5 0.0 copy-start.4
  21.5 0.7 %copy-done.4 = f32[3,1,1,512]{3,2,1,0:T(1,128)S(1)} copy-done((f32[3,1,1,512]{3,2,1,0:T(1,128)S(1)}, f32[3,1,1,512]{3,2,1,0:T(1,128)}, u32[]{:S(2)}) %copy-start.4) | copy-done | bytes 6168
  22.2 0.7 %copy-done.9 = s32[1,1,64]{2,1,0:T(1,128)S(1)} copy-done((s32[1,1,64]{2,1,0:T(1,128)S(1)}, s32[1,1,64]{2,1,0:T(1,128)}, u32[]{:S(2)}) %copy-start.9) | copy-done | bytes 280
  22.8 4.4 %force.1 = f32[128,128]{1,0:T(8,128)} custom-call(s32[1]{0:T(128)} %bitcast.here_ref, s32[1,1]{1,0:T(1,128)S(6)} %copy.13.live_ref, s32[1,1,64]{2,1,0:T(1,128)S(1)} %copy-done.9, f32[256,128]{1,0:T(8,128)S(1)} %bitcast.5, f32[8,128]{1,0:T(8,128)S(1)} %collective-permute-done.below_ref, f32[8,128]{1,0:T(8,128)S(1)} %collective-permute-done.1.above_ref, ...), custom_call_target="tpu_custom_call" | custom-call | flops 31457280 | bytes 131072 | tf_op jit(solution)/shard_map/force/pallas_call | solution.py:505
  27.3 4.4 %all-to-all-start.1 = ((f32[8,16,128]{2,1,0:T(8,128)}), f32[8,16,128]{2,1,0:T(8,128)S(1)}, u32[]{:S(2)}, u32[]{:S(2)}) async-start(f32[8,16,128]{2,1,0:T(8,128)} %bitcast.3), calls=%async_computation.1 | async-start | bytes 131072 | tf_op jit(solution)/shard_map/all_to_all | solution.py:540
  31.7 4.0 %bonds.1 = (f32[72,128]{1,0:T(8,128)S(1)}, bf16[2048,512]{1,0:T(8,128)(2,1)S(1)}, bf16[5120,256]{1,0:T(8,128)(2,1)S(1)}) custom-call(f32[256,128]{1,0:T(8,128)S(1)} %bitcast.6), custom_call_target="tpu_custom_call" | custom-call | flops 18874368 | bytes 131072 | tf_op jit(solution)/shard_map/bonds/pallas_call | solution.py:525
  35.7 0.0 copy-start
  35.7 1.3 %copy-done = bf16[2048,512]{1,0:T(8,128)(2,1)} copy-done((bf16[2048,512]{1,0:T(8,128)(2,1)}, bf16[2048,512]{1,0:T(8,128)(2,1)S(1)}, u32[]{:S(2)}) %copy-start) | copy-done | bytes 2097176
  37.0 1.6 %all-to-all-done.1 = f32[8,16,128]{2,1,0:T(8,128)S(1)} async-done(((f32[8,16,128]{2,1,0:T(8,128)}), f32[8,16,128]{2,1,0:T(8,128)S(1)}, u32[]{:S(2)}, u32[]{:S(2)}) %all-to-all-start.1) | async-done | bytes 65568 | tf_op jit(solution)/shard_map/all_to_all | solution.py:540
  38.6 1.6 %copy-done.1 = bf16[2048,512]{1,0:T(8,128)(2,1)S(1)} copy-done((bf16[2048,512]{1,0:T(8,128)(2,1)S(1)}, bf16[2048,512]{1,0:T(8,128)(2,1)}, u32[]{:S(2)}) %copy-start.1) | copy-done | bytes 2097176
  40.2 4.7 %solve.1 = (f32[3,1,1,512]{3,2,1,0:T(1,128)}, f32[3,1,1,512]{3,2,1,0:T(1,128)}) custom-call(s32[1]{0:T(128)} %bitcast.here_ref, f32[256,128]{1,0:T(8,128)S(1)} %bitcast.7, f32[128,128]{1,0:T(8,128)S(1)} %bitcast.8, f32[72,128]{1,0:T(8,128)S(1)} %get-tuple-element.9.weight_ref, bf16[2048,512]{1,0:T(8,128)(2,1)S(1)} %copy-done.1, ...), custom_call_target="tpu_custom_call" | custom-call | tf_op jit(solution)/shard_map/solve/pallas_call | solution.py:542
  (2 shorter events, 0.0 us)
Async XLA Ops:
  1.3 0.7 %copy-start.3 = (f32[3,1,1,512]{3,2,1,0:T(1,128)S(1)}, f32[3,1,1,512]{3,2,1,0:T(1,128)}, u32[]{:S(2)}) copy-start(f32[3,1,1,512]{3,2,1,0:T(1,128)} %coords_ref.1) | copy-start | bytes 18436
  2.0 0.7 %copy-start.5 = (f32[1,1,512]{2,1,0:T(1,128)S(1)}, f32[1,1,512]{2,1,0:T(1,128)}, u32[]{:S(2)}) copy-start(f32[1,1,512]{2,1,0:T(1,128)} %charge_ref.1) | copy-start | bytes 6148
  2.7 0.7 %copy-start.6 = (f32[1,1,512]{2,1,0:T(1,128)S(1)}, f32[1,1,512]{2,1,0:T(1,128)}, u32[]{:S(2)}) copy-start(f32[1,1,512]{2,1,0:T(1,128)} %mass_ref.1) | copy-start | bytes 6148
  3.3 0.7 %copy-start.7 = (s32[2,1,1,256]{3,2,1,0:T(1,128)S(1)}, s32[2,1,1,256]{3,2,1,0:T(1,128)}, u32[]{:S(2)}) copy-start(s32[2,1,1,256]{3,2,1,0:T(1,128)} %bonds_ref.1) | copy-start | bytes 6148
  4.0 0.7 %copy-start.8 = (s32[2,1,1,128]{3,2,1,0:T(1,128)S(1)}, s32[2,1,1,128]{3,2,1,0:T(1,128)}, u32[]{:S(2)}) copy-start(s32[2,1,1,128]{3,2,1,0:T(1,128)} %cross_ref.1) | copy-start | bytes 3076
  4.7 0.7 %copy-start.10 = (s32[1,1,128]{2,1,0:T(1,128)S(1)}, s32[1,1,128]{2,1,0:T(1,128)}, u32[]{:S(2)}) copy-start(s32[1,1,128]{2,1,0:T(1,128)} %side_ref.1) | copy-start | bytes 1540
  6.1 14.6 %all-to-all-start = ((f32[8,32,128]{2,1,0:T(8,128)}), f32[8,32,128]{2,1,0:T(8,128)S(1)}, u32[]{:S(2)}, u32[]{:S(2)}) async-start(f32[8,32,128]{2,1,0:T(8,128)} %bitcast.1), calls=%async_computation | async-start | bytes 262144 | tf_op jit(solution)/shard_map/all_to_all | solution.py:496
  13.4 2.0 %collective-permute-start.1 = (f32[8,128]{1,0:T(8,128)S(1)}, f32[8,128]{1,0:T(8,128)S(1)}, u32[]{:S(2)}, u32[]{:S(2)}) collective-permute-start(f32[8,128]{1,0:T(8,128)S(1)} %get-tuple-element.8), channel_id=1, source_target_pairs={{0,24},{8,0},{16,8},{24,16},{1,25},{9,1},{17,9},{25,17},{2,26},{10... | collective-permute-start | bytes 12296 | tf_op jit(solution)/shard_map/ppermute | solution.py:25
  14.0 3.0 %collective-permute-start = (f32[8,128]{1,0:T(8,128)S(1)}, f32[8,128]{1,0:T(8,128)S(1)}, u32[]{:S(2)}, u32[]{:S(2)}) collective-permute-start(f32[8,128]{1,0:T(8,128)S(1)} %get-tuple-element.8), channel_id=1, source_target_pairs={{0,8},{8,16},{16,24},{24,0},{1,9},{9,17},{17,25},{25,1},{2,10},{10... | collective-permute-start | bytes 12296 | tf_op jit(solution)/shard_map/ppermute | solution.py:25
  20.7 0.8 %copy-start.2 = (s32[1,1,64,128]{3,2,1,0:T(8,128)S(1)}, s32[1,1,64,128]{3,2,1,0:T(8,128)}, u32[]{:S(2)}) copy-start(s32[1,1,64,128]{3,2,1,0:T(8,128)} %atoms_ref.1) | copy-start | bytes 98308
  21.5 0.7 %copy-start.4 = (f32[3,1,1,512]{3,2,1,0:T(1,128)S(1)}, f32[3,1,1,512]{3,2,1,0:T(1,128)}, u32[]{:S(2)}) copy-start(f32[3,1,1,512]{3,2,1,0:T(1,128)} %velocity_ref.1) | copy-start | bytes 18436
  22.2 0.7 %copy-start.9 = (s32[1,1,64]{2,1,0:T(1,128)S(1)}, s32[1,1,64]{2,1,0:T(1,128)}, u32[]{:S(2)}) copy-start(s32[1,1,64]{2,1,0:T(1,128)} %block_ref.1) | copy-start | bytes 772
  27.3 11.3 %all-to-all-start.1 = ((f32[8,16,128]{2,1,0:T(8,128)}), f32[8,16,128]{2,1,0:T(8,128)S(1)}, u32[]{:S(2)}, u32[]{:S(2)}) async-start(f32[8,16,128]{2,1,0:T(8,128)} %bitcast.3), calls=%async_computation.1 | async-start | bytes 131072 | tf_op jit(solution)/shard_map/all_to_all | solution.py:540
  35.7 1.3 %copy-start = (bf16[2048,512]{1,0:T(8,128)(2,1)}, bf16[2048,512]{1,0:T(8,128)(2,1)S(1)}, u32[]{:S(2)}) copy-start(bf16[2048,512]{1,0:T(8,128)(2,1)S(1)} %get-tuple-element.10.inner_ref) | copy-start | bytes 6291460
  38.6 1.6 %copy-start.1 = (bf16[2048,512]{1,0:T(8,128)(2,1)S(1)}, bf16[2048,512]{1,0:T(8,128)(2,1)}, u32[]{:S(2)}) copy-start(bf16[2048,512]{1,0:T(8,128)(2,1)} %copy-done) | copy-start | bytes 6291460

commit v2 on v1

--- a/solution.py
+++ b/solution.py
@@ -16,8 +16,6 @@
 cutoff_sq = 16.0
 force_scale = 4.0
 length_floor = 0.25
-
-VMEM_LIMIT = 48 * 1024 * 1024
 
 
 def passed_along(array, axis, by):
@@ -85,9 +83,19 @@
     return guess * (1.5 - 0.5 * value * guess * guess)
 
 
-def pack_kernel(
-    rows, copies, count_ref, coords_ref, charge_ref, mass_ref, bonds_ref, cross_ref, side_ref, out_ref, rim_ref
-):
+def fetched(sources, targets, sem_ref):
+    copies = [pltpu.make_async_copy(s, t, sem_ref.at[n]) for n, (s, t) in enumerate(zip(sources, targets))]
+    for copy in copies:
+        copy.start()
+    return copies
+
+
+def pack_kernel(rows, copies, count_ref, *refs):
+    sources, (out_ref, rim_ref), targets, sem_ref = refs[:6], refs[6:8], refs[8:14], refs[14]
+    for copy in fetched(sources, targets, sem_ref):
+        copy.wait()
+    coords_ref, charge_ref, mass_ref, bonds_ref, cross_ref, side_ref = targets
+
     def put(row, value):
         for part in range(value.shape[1] // LANES):
             piece = value[:, part * LANES : (part + 1) * LANES]
@@ -117,41 +125,85 @@
             )
 
 
+SHRINK = 1.0 / 4.0
+
+
+def own_kernel(
+    rows, coords_hbm, charge_hbm, velocity_hbm, atoms_hbm, own_ref, far_ref, index_ref, speed_ref, coords_ref, charge_ref, velocity_ref, sem_ref
+):
+    atom_rows = rows.atom_rows
+    copies = fetched(
+        (coords_hbm, charge_hbm, atoms_hbm.at[0, 0], velocity_hbm),
+        (coords_ref, charge_ref, index_ref, velocity_ref),
+        sem_ref,
+    )
+    down = lax.broadcasted_iota(jnp.int32, (SUBLANES, LANES), 0)
+    copies[0].wait()
+    copies[1].wait()
+
+    def lanes_of(part):
+        return slice(part * LANES, (part + 1) * LANES)
+
+    table = []
+    for c in range(4):
+        field = coords_ref[c, 0] * SHRINK if c < 3 else charge_ref[0]
+        table.append(
+            [jnp.broadcast_to(field[:, lanes_of(part)], (SUBLANES, LANES)) for part in range(atom_rows)]
+        )
+    for part in range(atom_rows):
+        for group in range(LANES // SUBLANES):
+            at = part * LANES + group * SUBLANES
+            for c in range(4):
+                value = take_lanes(table[c][part], down + group * SUBLANES)
+                own_ref[c, pl.ds(at, SUBLANES), :] = value if c < 3 else value * 8.0
+    copies[2].wait()
+    for group in range(index_ref.shape[0] // SUBLANES):
+        at = pl.ds(group * SUBLANES, SUBLANES)
+        index = index_ref[at, :]
+        for c in range(4):
+            far_ref[c, at, :] = pick(table[c], index)
+    copies[3].wait()
+    for c in range(3):
+        for part in range(atom_rows):
+            speed_ref[pl.ds(c * atom_rows + part, 1), :] = velocity_ref[c, 0, :, lanes_of(part)]
+
+
 def force_kernel(
     rows,
     copies,
     holders,
     here_ref,
     live_ref,
-    block_ref,
+    block_hbm,
     around_ref,
     below_ref,
     above_ref,
-    velocity_ref,
-    atoms_ref,
+    own_ref,
+    near_ref,
+    index_ref,
+    speed_ref,
     out_ref,
     table_ref,
     far_ref,
-    own_ref,
     sum_ref,
+    block_ref,
+    sem_ref,
 ):
     atom_rows, shell_rows = rows.atom_rows, rows.shell_rows
-    tiles = atoms_ref.shape[2]
+    tiles = index_ref.shape[0]
+    block_copy = pltpu.make_async_copy(block_hbm, block_ref, sem_ref)
+    block_copy.start()
     me = here_ref[0]
     starts = [rows.coords[0], rows.coords[1], rows.coords[2], rows.charge]
-    entry_rows = atom_rows + 6 * shell_rows
+    entry_rows = 6 * shell_rows
     blocks = around_ref.shape[0] // rows.count
-    shrink = 1.0 / 4.0
 
     def broadcast(row):
         return jnp.broadcast_to(row, (SUBLANES, LANES))
 
     for c in range(4):
-        factor = shrink if c < 3 else 1.0
+        factor = SHRINK if c < 3 else 1.0
         at = 0
-        for part in range(atom_rows):
-            table_ref[c, at] = broadcast(around_ref[pl.ds(me * rows.count + starts[c] + part, 1), :] * factor)
-            at += 1
         for neighbour in range(4):
             base = lax.rem(me + holders[neighbour], blocks) * rows.count + starts[c]
             for part in range(shell_rows):
@@ -163,26 +215,19 @@
                 at += 1
 
     for group in range(tiles // SUBLANES):
-        index = atoms_ref[0, 0, pl.ds(group * SUBLANES, SUBLANES), :]
+        at = pl.ds(group * SUBLANES, SUBLANES)
+        index = index_ref[at, :]
         lanes = index & (LANES - 1)
         chunk = index >> 7
-        values = [take_lanes(table_ref[c, 0], lanes) for c in range(4)]
-        for k in range(1, entry_rows):
-            here = chunk == k
+        values = [near_ref[c, at, :] for c in range(4)]
+        for k in range(entry_rows):
+            here = chunk == atom_rows + k
             values = [jnp.where(here, take_lanes(table_ref[c, k], lanes), values[c]) for c in range(4)]
         for c in range(4):
-            far_ref[c, pl.ds(group * SUBLANES, SUBLANES), :] = values[c]
-
-    down = lax.broadcasted_iota(jnp.int32, (SUBLANES, LANES), 0)
-    zero = jnp.zeros((SUBLANES, LANES), jnp.float32)
-    for part in range(atom_rows):
-        for group in range(LANES // SUBLANES):
-            at = part * LANES + group * SUBLANES
-            for c in range(4):
-                value = take_lanes(table_ref[c, part], down + group * SUBLANES)
-                own_ref[c, pl.ds(at, SUBLANES), :] = value if c < 3 else value * 8.0
-            for c in range(3):
-                sum_ref[c, pl.ds(at, SUBLANES), :] = zero
+            far_ref[c, at, :] = values[c]
+
+    sum_ref[...] = jnp.zeros(sum_ref.shape, jnp.float32)
+    block_copy.wait()
 
     def add_tile(tile, _):
         base = block_ref[0, 0, tile] * TILE
@@ -205,11 +250,10 @@
 
     scale = time_step * time_step * force_scale * 4.0 / 2048.0
     for c in range(3):
-        speed = velocity_ref[c, 0]
         for part in range(atom_rows):
             total = jnp.sum(sum_ref[c, pl.ds(part * LANES, LANES), :].T, axis=0, keepdims=True)
             mass = around_ref[pl.ds(me * rows.count + rows.mass + part, 1), :]
-            moved = time_step * speed[:, part * LANES : (part + 1) * LANES] + scale * total * mass
+            moved = time_step * speed_ref[pl.ds(c * atom_rows + part, 1), :] + scale * total * mass
             for copy in range(copies):
                 out_ref[pl.ds(copy * rows.disp_count + c * atom_rows + part, 1), :] = moved
     if rows.disp_count > rows.disp_used:
@@ -448,12 +492,24 @@
     return [pl.BlockSpec(memory_space=pltpu.SMEM)] * count
 
 
-def params():
-    return pltpu.CompilerParams(vmem_limit_bytes=VMEM_LIMIT)
+def hbm(count):
+    return [pl.BlockSpec(memory_space=pltpu.HBM)] * count
+
+
+def in_hbm(arrays):
+    return [pltpu.with_memory_space_constraint(a, pltpu.HBM) for a in arrays]
+
+
+def params(mebibytes):
+    return pltpu.CompilerParams(vmem_limit_bytes=mebibytes * 1024 * 1024)
 
 
 def cost(flops, moved):
     return pl.CostEstimate(flops=flops, bytes_accessed=moved, transcendentals=0)
+
+
+def room_for(arrays):
+    return [pltpu.VMEM(a.shape, a.dtype) for a in arrays]
 
 
 def shards(
@@ -478,17 +534,36 @@
     copies = domains if whole_slab else 1
     f32 = jnp.float32
 
+    sent = (coords, charge, inv_mass, bond_atoms, cross_atoms, cross_side)
     packed, rim = pl.pallas_call(
         functools.partial(pack_kernel, rows, copies),
         out_shape=(
             jax.ShapeDtypeStruct((copies * rows.count, LANES), f32),
             jax.ShapeDtypeStruct((4 * rows.shell_rows, LANES), f32),
         ),
-        in_specs=smem(1) + vmem(6),
+        in_specs=smem(1) + hbm(len(sent)),
         out_specs=tuple(vmem(2)),
-        compiler_params=params(),
+        scratch_shapes=room_for(sent) + [pltpu.SemaphoreType.DMA((len(sent),))],
+        compiler_params=params(4),
         name="pack",
-    )(cross_count, coords, charge, inv_mass, bond_atoms, cross_atoms, cross_side)
+    )(cross_count, *in_hbm(sent))
+
+    alone = (coords, charge, velocity, tile_atoms)
+    own, near, index, speed = pl.pallas_call(
+        functools.partial(own_kernel, rows),
+        out_shape=(
+            jax.ShapeDtypeStruct((4, atoms, LANES), f32),
+            jax.ShapeDtypeStruct((4, tiles, TILE), f32),
+            jax.ShapeDtypeStruct((tiles, TILE), jnp.int32),
+            jax.ShapeDtypeStruct((rows.disp_used, LANES), f32),
+        ),
+        in_specs=hbm(len(alone)),
+        out_specs=tuple(vmem(4)),
+        scratch_shapes=room_for(alone[:3]) + [pltpu.SemaphoreType.DMA((len(alone),))],
+        compiler_params=params(4),
+        cost_estimate=cost(64 * atoms * LANES, 16 * atoms * LANES),
+        name="own",
+    )(*in_hbm(alone))
 
     below = passed_along(rim, "slab", 1)
     above = passed_along(rim, "slab", -1)
@@ -501,22 +576,22 @@
         here = jnp.zeros(1, jnp.int32)
         holders = [1, 2, 3, 4]
 
-    entry_rows = rows.atom_rows + 6 * rows.shell_rows
     moves = pl.pallas_call(
         functools.partial(force_kernel, rows, copies, holders),
         out_shape=jax.ShapeDtypeStruct((copies * rows.disp_count, LANES), f32),
-        in_specs=smem(3) + vmem(5),
+        in_specs=smem(2) + hbm(1) + vmem(7),
         out_specs=vmem(1)[0],
         scratch_shapes=[
-            pltpu.VMEM((4, entry_rows, SUBLANES, LANES), f32),
+            pltpu.VMEM((4, 6 * rows.shell_rows, SUBLANES, LANES), f32),
             pltpu.VMEM((4, tiles, LANES), f32),
-            pltpu.VMEM((4, atoms, LANES), f32),
             pltpu.VMEM((3, atoms, LANES), f32),
+            pltpu.SMEM(tile_block.shape, jnp.int32),
+            pltpu.SemaphoreType.DMA(()),
         ],
-        compiler_params=params(),
+        compiler_params=params(8),
         cost_estimate=cost(30 * tiles * TILE * TILE, 4 * around.size),
         name="force",
-    )(here, active_tile_count, tile_block, around, below, above, velocity, tile_atoms)
+    )(here, active_tile_count, *in_hbm([tile_block]), around, below, above, own, near, index, speed)
 
     if not whole_slab:
         return by_exchange(rows, strides, around, moves, cross_count)
@@ -532,7 +607,7 @@
         in_specs=vmem(1),
         out_specs=tuple(vmem(3)),
         scratch_shapes=[pltpu.VMEM((rows.slot_rows * 4 * domains, LANES), f32)],
-        compiler_params=params(),
+        compiler_params=params(16),
         cost_estimate=cost(8 * domains * (rows.bond_rows * LANES * atoms + rows.slot_rows * 5 * LANES * atoms // 2), 4 * around.size),
         name="bonds",
     )(around)
@@ -551,7 +626,7 @@
             pltpu.VMEM((constraint_rows, SUBLANES * domains, LANES), f32),
             pltpu.VMEM((rows.atom_rows, SUBLANES * domains, LANES), f32),
         ],
-        compiler_params=params(),
+        compiler_params=params(16),
         name="solve",
     )(here, around, every_move, weight, inner, cross)
 

time: 45.4 us -> 38.4 us (0.85)
  local copies, waits for them, and re-layouts: 9.09 us -> 2.92 us
  waiting for transfers between devices: 7.62 us -> 6.1 us
    unnamed x22 -> x4, local copies, waits for them, and re-layouts: 9.09 us -> 2.92 us
    pallas_call x1, Pallas kernels: 4.43 us -> 2.61 us  [shards(): pl.pallas_call(functools.partial(force_kernel, rows, copies, holders), ou...]
    ppermute x2, waiting for transfers between devices: 2.38 us -> 0.85 us  [passed_along(): lax.ppermute(array, axis, [(i, (i + by) % length) for i in range(length)])]
    pallas_call x0 -> x1, Pallas kernels: none -> 1.51 us  [shards(): pl.pallas_call(functools.partial(own_kernel, rows), out_shape=(jax.ShapeD...]
    pallas_call x1, Pallas kernels: 0.75 us -> 1.51 us  [shards(): pl.pallas_call(functools.partial(pack_kernel, rows, copies), out_shape=(j...]
  transfers between devices with their start and end apart: 4 -> 4, of which waited for: 4 -> 3; matrix products, arithmetic and copies ran while one was open for 0% -> 0% of each run, Pallas kernels for 9% -> 14%
where the time goes in v2:
time: 38.4 us; the launch traced here: 38.1 us
  Pallas kernels  14.3 us (37%)
  starting transfers between devices  12.8 us (33%)
  waiting for transfers between devices  6.1 us (16%)
  local copies, waits for them, and re-layouts  2.92 us (8%)
  between operations  1.98 us (5%)
    all_to_all x1, starting transfers between devices, shards(): around = lax.all_to_all(packed, 'dom', 0, 0, tiled=True)  7.29 us
    all_to_all x1, starting transfers between devices, shards(): every_move = lax.all_to_all(moves, 'dom', 0, 0, tiled=True)  4.86 us
    pallas_call x1, Pallas kernels, shards(): pl.pallas_call(functools.partial(solve_kernel, rows, domains, strides), o...  4.72 us
    pallas_call x1, Pallas kernels, shards(): pl.pallas_call(functools.partial(bond_kernel, rows, domains, strides), ou...  3.98 us
    all_to_all x1, waiting for transfers between devices, shards(): around = lax.all_to_all(packed, 'dom', 0, 0, tiled=True)  3.66 us
    unnamed x4, local copies, waits for them, and re-layouts  2.92 us
    pallas_call x1, Pallas kernels, shards(): pl.pallas_call(functools.partial(force_kernel, rows, copies, holders), ou...  2.61 us
    all_to_all x1, waiting for transfers between devices, shards(): every_move = lax.all_to_all(moves, 'dom', 0, 0, tiled=True)  1.59 us
  transfers between devices with their start and end apart: 4, of which 3 were waited for; matrix products, arithmetic and copies ran while one was open for 0% of the time, Pallas kernels for 14%

profile of v2, /device:TPU:0, one launch (start us, length us, event | category | flops | bytes accessed | tf_op | source)
XLA Modules:
  0.0 38.1 jit_solution(12538097974521981748)
XLA Ops:
  1.3 1.5 %pack.1 = (f32[256,128]{1,0:T(8,128)}, f32[8,128]{1,0:T(8,128)S(1)}) custom-call(s32[1,1]{1,0:T(1,128)S(6)} %copy.14.count_ref, f32[3,1,1,512]{3,2,1,0:T(1,128)} %coords_hbm.1, f32[1,1,512]{2,1,0:T(1,128)} %charge_hbm.1, f32[1,1,512]{2,1,0:T(1,128)} %refs_2_.1, s32[2,1,1,256]{3,2,1,0:T(1,128)} %refs_3_.1, s32[2,1,1,128]{3,2,1,0:T(1,128)} %refs_4_.1, ...), custom_call_target="tpu_custom_call" | custom-call | tf_op jit(solution)/shard_map/pack/pallas_call | solution.py:538
  2.8 7.3 %all-to-all-start = ((f32[8,32,128]{2,1,0:T(8,128)}), f32[8,32,128]{2,1,0:T(8,128)S(1)}, u32[]{:S(2)}, u32[]{:S(2)}) async-start(f32[8,32,128]{2,1,0:T(8,128)} %bitcast.1), calls=%async_computation | async-start | bytes 262144 | tf_op jit(solution)/shard_map/all_to_all | solution.py:571
  10.1 0.7 %collective-permute-start.1 = (f32[8,128]{1,0:T(8,128)S(1)}, f32[8,128]{1,0:T(8,128)S(1)}, u32[]{:S(2)}, u32[]{:S(2)}) collective-permute-start(f32[8,128]{1,0:T(8,128)S(1)} %get-tuple-element.12), channel_id=1, source_target_pairs={{0,24},{8,0},{16,8},{24,16},{1,25},{9,1},{17,9},{25,17},{2,26},{10... | collective-permute-start | bytes 12296 | tf_op jit(solution)/shard_map/ppermute | solution.py:23
  10.7 0.0 collective-permute-start
  11.4 1.5 %own.1 = (f32[4,512,128]{2,1,0:T(8,128)S(1)}, f32[4,64,128]{2,1,0:T(8,128)S(1)}, s32[64,128]{1,0:T(8,128)S(1)}, f32[12,128]{1,0:T(8,128)S(1)}) custom-call(f32[3,1,1,512]{3,2,1,0:T(1,128)} %coords_hbm.1, f32[1,1,512]{2,1,0:T(1,128)} %charge_hbm.1, f32[3,1,1,512]{3,2,1,0:T(1,128)} %velocity_hbm.1, s32[1,1,64,128]{3,2,1,0:T(8,128)} %atoms_hbm.1), custom_call_target="tpu_custom_call" | custom-call | flops 4194304 | bytes 1048576 | tf_op jit(solution)/shard_map/own/pallas_call | solution.py:552
  12.9 0.0 collective-permute-done.1.above_ref
  12.9 0.8 %collective-permute-done.below_ref = f32[8,128]{1,0:T(8,128)S(1)} collective-permute-done((f32[8,128]{1,0:T(8,128)S(1)}, f32[8,128]{1,0:T(8,128)S(1)}, u32[]{:S(2)}, u32[]{:S(2)}) %collective-permute-start) | collective-permute-done | bytes 4128 | tf_op jit(solution)/shard_map/ppermute | solution.py:23
  13.8 3.7 %all-to-all-done = f32[8,32,128]{2,1,0:T(8,128)S(1)} async-done(((f32[8,32,128]{2,1,0:T(8,128)}), f32[8,32,128]{2,1,0:T(8,128)S(1)}, u32[]{:S(2)}, u32[]{:S(2)}) %all-to-all-start) | async-done | bytes 131104 | tf_op jit(solution)/shard_map/all_to_all | solution.py:571
  17.4 2.6 %force.1 = f32[128,128]{1,0:T(8,128)} custom-call(s32[1]{0:T(128)} %bitcast.here_ref, s32[1,1]{1,0:T(1,128)S(6)} %copy.13.live_ref, s32[1,1,64]{2,1,0:T(1,128)} %block_hbm.1, f32[256,128]{1,0:T(8,128)S(1)} %bitcast.5, f32[8,128]{1,0:T(8,128)S(1)} %collective-permute-done.below_ref, f32[8,128]{1,0:T(8,128)S(1)} %collective-permute-done.1.above_ref, ...), custom_call_target="tpu_custom_call" | custom-call | flops 31457280 | bytes 131072 | tf_op jit(solution)/shard_map/force/pallas_call | solution.py:579
  20.1 4.9 %all-to-all-start.1 = ((f32[8,16,128]{2,1,0:T(8,128)}), f32[8,16,128]{2,1,0:T(8,128)S(1)}, u32[]{:S(2)}, u32[]{:S(2)}) async-start(f32[8,16,128]{2,1,0:T(8,128)} %bitcast.3), calls=%async_computation.1 | async-start | bytes 131072 | tf_op jit(solution)/shard_map/all_to_all | solution.py:615
  24.9 4.0 %bonds.1 = (f32[72,128]{1,0:T(8,128)S(1)}, bf16[2048,512]{1,0:T(8,128)(2,1)S(1)}, bf16[5120,256]{1,0:T(8,128)(2,1)S(1)}) custom-call(f32[256,128]{1,0:T(8,128)S(1)} %bitcast.6), custom_call_target="tpu_custom_call" | custom-call | flops 18874368 | bytes 131072 | tf_op jit(solution)/shard_map/bonds/pallas_call | solution.py:600
  28.9 0.0 copy-start
  28.9 1.3 %copy-done = bf16[2048,512]{1,0:T(8,128)(2,1)} copy-done((bf16[2048,512]{1,0:T(8,128)(2,1)}, bf16[2048,512]{1,0:T(8,128)(2,1)S(1)}, u32[]{:S(2)}) %copy-start) | copy-done | bytes 2097176
  30.2 1.6 %all-to-all-done.1 = f32[8,16,128]{2,1,0:T(8,128)S(1)} async-done(((f32[8,16,128]{2,1,0:T(8,128)}), f32[8,16,128]{2,1,0:T(8,128)S(1)}, u32[]{:S(2)}, u32[]{:S(2)}) %all-to-all-start.1) | async-done | bytes 65568 | tf_op jit(solution)/shard_map/all_to_all | solution.py:615
  31.8 0.0 copy-start.1
  31.8 1.6 %copy-done.1 = bf16[2048,512]{1,0:T(8,128)(2,1)S(1)} copy-done((bf16[2048,512]{1,0:T(8,128)(2,1)S(1)}, bf16[2048,512]{1,0:T(8,128)(2,1)}, u32[]{:S(2)}) %copy-start.1) | copy-done | bytes 2097176
  33.4 4.7 %solve.1 = (f32[3,1,1,512]{3,2,1,0:T(1,128)}, f32[3,1,1,512]{3,2,1,0:T(1,128)}) custom-call(s32[1]{0:T(128)} %bitcast.here_ref, f32[256,128]{1,0:T(8,128)S(1)} %bitcast.7, f32[128,128]{1,0:T(8,128)S(1)} %bitcast.8, f32[72,128]{1,0:T(8,128)S(1)} %get-tuple-element.17.weight_ref, bf16[2048,512]{1,0:T(8,128)(2,1)S(1)} %copy-done.1, ...), custom_call_target="tpu_custom_call" | custom-call | tf_op jit(solution)/shard_map/solve/pallas_call | solution.py:617
Async XLA Ops:
  2.8 14.6 %all-to-all-start = ((f32[8,32,128]{2,1,0:T(8,128)}), f32[8,32,128]{2,1,0:T(8,128)S(1)}, u32[]{:S(2)}, u32[]{:S(2)}) async-start(f32[8,32,128]{2,1,0:T(8,128)} %bitcast.1), calls=%async_computation | async-start | bytes 262144 | tf_op jit(solution)/shard_map/all_to_all | solution.py:571
  10.1 2.8 %collective-permute-start.1 = (f32[8,128]{1,0:T(8,128)S(1)}, f32[8,128]{1,0:T(8,128)S(1)}, u32[]{:S(2)}, u32[]{:S(2)}) collective-permute-start(f32[8,128]{1,0:T(8,128)S(1)} %get-tuple-element.12), channel_id=1, source_target_pairs={{0,24},{8,0},{16,8},{24,16},{1,25},{9,1},{17,9},{25,17},{2,26},{10... | collective-permute-start | bytes 12296 | tf_op jit(solution)/shard_map/ppermute | solution.py:23
  10.7 3.0 %collective-permute-start = (f32[8,128]{1,0:T(8,128)S(1)}, f32[8,128]{1,0:T(8,128)S(1)}, u32[]{:S(2)}, u32[]{:S(2)}) collective-permute-start(f32[8,128]{1,0:T(8,128)S(1)} %get-tuple-element.12), channel_id=1, source_target_pairs={{0,8},{8,16},{16,24},{24,0},{1,9},{9,17},{17,25},{25,1},{2,10},{10... | collective-permute-start | bytes 12296 | tf_op jit(solution)/shard_map/ppermute | solution.py:23
  20.1 11.8 %all-to-all-start.1 = ((f32[8,16,128]{2,1,0:T(8,128)}), f32[8,16,128]{2,1,0:T(8,128)S(1)}, u32[]{:S(2)}, u32[]{:S(2)}) async-start(f32[8,16,128]{2,1,0:T(8,128)} %bitcast.3), calls=%async_computation.1 | async-start | bytes 131072 | tf_op jit(solution)/shard_map/all_to_all | solution.py:615
  28.9 1.3 %copy-start = (bf16[2048,512]{1,0:T(8,128)(2,1)}, bf16[2048,512]{1,0:T(8,128)(2,1)S(1)}, u32[]{:S(2)}) copy-start(bf16[2048,512]{1,0:T(8,128)(2,1)S(1)} %get-tuple-element.18.inner_ref) | copy-start | bytes 6291460
  31.8 1.6 %copy-start.1 = (bf16[2048,512]{1,0:T(8,128)(2,1)S(1)}, bf16[2048,512]{1,0:T(8,128)(2,1)}, u32[]{:S(2)}) copy-start(bf16[2048,512]{1,0:T(8,128)(2,1)} %copy-done) | copy-start | bytes 6291460

commit v3 on v2

--- a/solution.py
+++ b/solution.py
@@ -43,8 +43,6 @@
         for _ in range(3):
             self.coords.append(at)
             at += self.atom_rows
-        self.charge = at
-        at += self.atom_rows
         self.mass = at
         at += self.atom_rows
         self.bond_first = at
@@ -61,6 +59,7 @@
         at += self.slot_rows
         self.used = at
         self.count = round_up(at, SUBLANES)
+        self.rim = 4 * self.shell_rows
         self.disp_used = 3 * self.atom_rows
         self.disp_count = round_up(self.disp_used, SUBLANES)
 
@@ -91,24 +90,24 @@
 
 
 def pack_kernel(rows, copies, count_ref, *refs):
-    sources, (out_ref, rim_ref), targets, sem_ref = refs[:6], refs[6:8], refs[8:14], refs[14]
+    sources, (rim_ref, spread_ref, out_ref), targets, sem_ref = refs[:6], refs[6:9], refs[9:15], refs[15]
     for copy in fetched(sources, targets, sem_ref):
         copy.wait()
     coords_ref, charge_ref, mass_ref, bonds_ref, cross_ref, side_ref = targets
 
     def put(row, value):
         for part in range(value.shape[1] // LANES):
-            piece = value[:, part * LANES : (part + 1) * LANES]
-            for copy in range(copies):
-                out_ref[pl.ds(copy * rows.count + row + part, 1), :] = piece
-
-    shell = rows.shell_rows * LANES
+            out_ref[pl.ds(row + part, 1), :] = value[:, part * LANES : (part + 1) * LANES]
+
     fields = [coords_ref[c, 0] for c in range(3)] + [charge_ref[0]]
     for c in range(4):
-        at = rows.coords[c] if c < 3 else rows.charge
-        put(at, fields[c])
         for part in range(rows.shell_rows):
-            rim_ref[pl.ds(c * rows.shell_rows + part, 1), :] = fields[c][:, part * LANES : (part + 1) * LANES]
+            piece = fields[c][:, part * LANES : (part + 1) * LANES]
+            rim_ref[pl.ds(c * rows.shell_rows + part, 1), :] = piece
+            for copy in range(copies):
+                spread_ref[pl.ds(copy * rows.rim + c * rows.shell_rows + part, 1), :] = piece
+    for c in range(3):
+        put(rows.coords[c], fields[c])
     put(rows.mass, mass_ref[0])
     put(rows.bond_first, bonds_ref[0, 0].astype(jnp.float32))
     put(rows.bond_second, bonds_ref[1, 0].astype(jnp.float32))
@@ -119,10 +118,7 @@
     slot = lax.broadcasted_iota(jnp.int32, side.shape, 1)
     put(rows.live, jnp.where(slot < count_ref[0, 0], 1.0, 0.0))
     if rows.count > rows.used:
-        for copy in range(copies):
-            out_ref[pl.ds(copy * rows.count + rows.used, rows.count - rows.used), :] = jnp.zeros(
-                (rows.count - rows.used, LANES), jnp.float32
-            )
+        out_ref[rows.used :, :] = jnp.zeros((rows.count - rows.used, LANES), jnp.float32)
 
 
 SHRINK = 1.0 / 4.0
@@ -175,9 +171,10 @@
     here_ref,
     live_ref,
     block_hbm,
-    around_ref,
+    rims_ref,
     below_ref,
     above_ref,
+    static_ref,
     own_ref,
     near_ref,
     index_ref,
@@ -194,9 +191,8 @@
     block_copy = pltpu.make_async_copy(block_hbm, block_ref, sem_ref)
     block_copy.start()
     me = here_ref[0]
-    starts = [rows.coords[0], rows.coords[1], rows.coords[2], rows.charge]
     entry_rows = 6 * shell_rows
-    blocks = around_ref.shape[0] // rows.count
+    blocks = rims_ref.shape[0] // rows.rim
 
     def broadcast(row):
         return jnp.broadcast_to(row, (SUBLANES, LANES))
@@ -205,9 +201,9 @@
         factor = SHRINK if c < 3 else 1.0
         at = 0
         for neighbour in range(4):
-            base = lax.rem(me + holders[neighbour], blocks) * rows.count + starts[c]
+            base = lax.rem(me + holders[neighbour], blocks) * rows.rim + c * shell_rows
             for part in range(shell_rows):
-                table_ref[c, at] = broadcast(around_ref[pl.ds(base + part, 1), :] * factor)
+                table_ref[c, at] = broadcast(rims_ref[pl.ds(base + part, 1), :] * factor)
                 at += 1
         for slab_ref in (below_ref, above_ref):
             for part in range(shell_rows):
@@ -252,7 +248,7 @@
     for c in range(3):
         for part in range(atom_rows):
             total = jnp.sum(sum_ref[c, pl.ds(part * LANES, LANES), :].T, axis=0, keepdims=True)
-            mass = around_ref[pl.ds(me * rows.count + rows.mass + part, 1), :]
+            mass = static_ref[pl.ds(rows.mass + part, 1), :]
             moved = time_step * speed_ref[pl.ds(c * atom_rows + part, 1), :] + scale * total * mass
             for copy in range(copies):
                 out_ref[pl.ds(copy * rows.disp_count + c * atom_rows + part, 1), :] = moved
@@ -535,14 +531,15 @@
     f32 = jnp.float32
 
     sent = (coords, charge, inv_mass, bond_atoms, cross_atoms, cross_side)
-    packed, rim = pl.pallas_call(
+    rim, rims, static = pl.pallas_call(
         functools.partial(pack_kernel, rows, copies),
         out_shape=(
-            jax.ShapeDtypeStruct((copies * rows.count, LANES), f32),
-            jax.ShapeDtypeStruct((4 * rows.shell_rows, LANES), f32),
+            jax.ShapeDtypeStruct((rows.rim, LANES), f32),
+            jax.ShapeDtypeStruct((copies * rows.rim, LANES), f32),
+            jax.ShapeDtypeStruct((rows.count, LANES), f32),
         ),
         in_specs=smem(1) + hbm(len(sent)),
-        out_specs=tuple(vmem(2)),
+        out_specs=tuple(vmem(3)),
         scratch_shapes=room_for(sent) + [pltpu.SemaphoreType.DMA((len(sent),))],
         compiler_params=params(4),
         name="pack",
@@ -568,18 +565,18 @@
     below = passed_along(rim, "slab", 1)
     above = passed_along(rim, "slab", -1)
     if whole_slab:
-        around = lax.all_to_all(packed, "dom", 0, 0, tiled=True)
+        rims = lax.all_to_all(rims, "dom", 0, 0, tiled=True)
         here = lax.axis_index("dom").reshape(1)
         holders = [stride % domains for stride in strides]
     else:
-        around = jnp.concatenate([packed] + [passed_along(packed, "dom", -stride) for stride in strides], axis=0)
+        rims = jnp.concatenate([passed_along(rim, "dom", -stride) for stride in strides], axis=0)
         here = jnp.zeros(1, jnp.int32)
-        holders = [1, 2, 3, 4]
+        holders = [0, 1, 2, 3]
 
     moves = pl.pallas_call(
         functools.partial(force_kernel, rows, copies, holders),
         out_shape=jax.ShapeDtypeStruct((copies * rows.disp_count, LANES), f32),
-        in_specs=smem(2) + hbm(1) + vmem(7),
+        in_specs=smem(2) + hbm(1) + vmem(8),
         out_specs=vmem(1)[0],
         scratch_shapes=[
             pltpu.VMEM((4, 6 * rows.shell_rows, SUBLANES, LANES), f32),
@@ -588,13 +585,16 @@
             pltpu.SMEM(tile_block.shape, jnp.int32),
             pltpu.SemaphoreType.DMA(()),
         ],
-        compiler_params=params(8),
-        cost_estimate=cost(30 * tiles * TILE * TILE, 4 * around.size),
+        compiler_params=params(4),
+        cost_estimate=cost(30 * tiles * TILE * TILE, 4 * own.size),
         name="force",
-    )(here, active_tile_count, *in_hbm([tile_block]), around, below, above, own, near, index, speed)
+    )(here, active_tile_count, *in_hbm([tile_block]), rims, below, above, static, own, near, index, speed)
 
     if not whole_slab:
-        return by_exchange(rows, strides, around, moves, cross_count)
+        around = jnp.concatenate([static] + [passed_along(static, "dom", -stride) for stride in strides], axis=0)
+        return by_exchange(rows, strides, around, moves)
+
+    around = lax.all_gather(static, "dom", tiled=True)
 
     constraint_rows = rows.bond_rows + rows.slot_rows
     weight, inner, cross = pl.pallas_call(
@@ -607,7 +607,7 @@
         in_specs=vmem(1),
         out_specs=tuple(vmem(3)),
         scratch_shapes=[pltpu.VMEM((rows.slot_rows * 4 * domains, LANES), f32)],
-        compiler_params=params(16),
+        compiler_params=params(8),
         cost_estimate=cost(8 * domains * (rows.bond_rows * LANES * atoms + rows.slot_rows * 5 * LANES * atoms // 2), 4 * around.size),
         name="bonds",
     )(around)
@@ -626,12 +626,12 @@
             pltpu.VMEM((constraint_rows, SUBLANES * domains, LANES), f32),
             pltpu.VMEM((rows.atom_rows, SUBLANES * domains, LANES), f32),
         ],
-        compiler_params=params(16),
+        compiler_params=params(8),
         name="solve",
     )(here, around, every_move, weight, inner, cross)
 
 
-def by_exchange(rows, strides, around, moves, cross_count):
+def by_exchange(rows, strides, around, moves):
     atom_count = rows.atom_rows * LANES
     shell = rows.shell_rows * LANES
     inside = around.reshape(5, rows.count, LANES)

time: 38.4 us -> 67.4 us (1.76)
  blocking collectives: 0 us -> 31.1 us
  waiting for transfers between devices: 6.1 us -> 3.85 us
  starting transfers between devices: 12.8 us -> 13.9 us
  Pallas kernels: 14.3 us -> 13.3 us
    all_gather x0 -> x1, blocking collectives: none -> 31.1 us  [shards(): around = lax.all_gather(static, 'dom', tiled=True)]
    all_to_all x1, waiting for transfers between devices: 1.59 us -> 0.01 us  [shards(): every_move = lax.all_to_all(moves, 'dom', 0, 0, tiled=True)]
    all_to_all x1, starting transfers between devices: 4.86 us -> 5.98 us  [shards(): every_move = lax.all_to_all(moves, 'dom', 0, 0, tiled=True)]
    pallas_call x1, Pallas kernels: 2.61 us -> 1.69 us  [shards(): pl.pallas_call(functools.partial(force_kernel, rows, copies, holders), ou...]
  transfers between devices with their start and end apart: 4 -> 4, of which waited for: 3 -> 2; matrix products, arithmetic and copies ran while one was open for 0% -> 0% of each run, Pallas kernels for 14% -> 8%
where the time goes in v3:
time: 67.4 us; the launch traced here: 67.1 us
  blocking collectives  31.1 us (46%)
  starting transfers between devices  13.9 us (21%)
  Pallas kernels  13.3 us (20%)
  waiting for transfers between devices  3.85 us (6%)
  local copies, waits for them, and re-layouts  2.92 us (4%)
  between operations  1.98 us (3%)
    all_gather x1, blocking collectives, shards(): around = lax.all_gather(static, 'dom', tiled=True)  31.1 us
    all_to_all x1, starting transfers between devices, shards(): rims = lax.all_to_all(rims, 'dom', 0, 0, tiled=True)  7.29 us
    all_to_all x1, starting transfers between devices, shards(): every_move = lax.all_to_all(moves, 'dom', 0, 0, tiled=True)  5.98 us
    pallas_call x1, Pallas kernels, shards(): pl.pallas_call(functools.partial(solve_kernel, rows, domains, strides), o...  4.71 us
    pallas_call x1, Pallas kernels, shards(): pl.pallas_call(functools.partial(bond_kernel, rows, domains, strides), ou...  3.95 us
    all_to_all x1, waiting for transfers between devices, shards(): rims = lax.all_to_all(rims, 'dom', 0, 0, tiled=True)  3 us
    unnamed x4, local copies, waits for them, and re-layouts  2.92 us
    pallas_call x1, Pallas kernels, shards(): pl.pallas_call(functools.partial(force_kernel, rows, copies, holders), ou...  1.69 us
  transfers between devices with their start and end apart: 4, of which 2 were waited for; matrix products, arithmetic and copies ran while one was open for 0% of the time, Pallas kernels for 8%

profile of v3, /device:TPU:0, one launch (start us, length us, event | category | flops | bytes accessed | tf_op | source)
XLA Modules:
  0.0 67.1 jit_solution(9280845771648228673)
XLA Ops:
  1.3 1.4 %pack.1 = (f32[8,128]{1,0:T(8,128)S(1)}, f32[64,128]{1,0:T(8,128)}, f32[24,128]{1,0:T(8,128)S(1)}) custom-call(s32[1,1]{1,0:T(1,128)S(6)} %copy.14.count_ref, f32[3,1,1,512]{3,2,1,0:T(1,128)} %coords_hbm.1, f32[1,1,512]{2,1,0:T(1,128)} %charge_hbm.1, f32[1,1,512]{2,1,0:T(1,128)} %refs_2_.1, s32[2,1,1,256]{3,2,1,0:T(1,128)} %refs_3_.1, ...), custom_call_target="tpu_custom_call" | custom-call | tf_op jit(solution)/shard_map/pack/pallas_call | solution.py:534
  2.7 7.3 %all-to-all-start = ((f32[8,8,128]{2,1,0:T(8,128)}), f32[8,8,128]{2,1,0:T(8,128)S(1)}, u32[]{:S(2)}, u32[]{:S(2)}) async-start(f32[8,8,128]{2,1,0:T(8,128)} %bitcast.1), calls=%async_computation | async-start | bytes 65536 | tf_op jit(solution)/shard_map/all_to_all | solution.py:568
  10.0 0.7 collective-permute-start.1
  10.7 0.0 collective-permute-start
  11.3 1.5 %own.1 = (f32[4,512,128]{2,1,0:T(8,128)S(1)}, f32[4,64,128]{2,1,0:T(8,128)S(1)}, s32[64,128]{1,0:T(8,128)S(1)}, f32[12,128]{1,0:T(8,128)S(1)}) custom-call(f32[3,1,1,512]{3,2,1,0:T(1,128)} %coords_hbm.1, f32[1,1,512]{2,1,0:T(1,128)} %charge_hbm.1, f32[3,1,1,512]{3,2,1,0:T(1,128)} %velocity_hbm.1, s32[1,1,64,128]{3,2,1,0:T(8,128)} %atoms_hbm.1), custom_call_target="tpu_custom_call" | custom-call | flops 4194304 | bytes 1048576 | tf_op jit(solution)/shard_map/own/pallas_call | solution.py:549
  12.8 0.0 collective-permute-done.1.above_ref
  12.9 0.8 %collective-permute-done.below_ref = f32[8,128]{1,0:T(8,128)S(1)} collective-permute-done((f32[8,128]{1,0:T(8,128)S(1)}, f32[8,128]{1,0:T(8,128)S(1)}, u32[]{:S(2)}, u32[]{:S(2)}) %collective-permute-start) | collective-permute-done | bytes 4128 | tf_op jit(solution)/shard_map/ppermute | solution.py:23
  13.7 3.0 %all-to-all-done = f32[8,8,128]{2,1,0:T(8,128)S(1)} async-done(((f32[8,8,128]{2,1,0:T(8,128)}), f32[8,8,128]{2,1,0:T(8,128)S(1)}, u32[]{:S(2)}, u32[]{:S(2)}) %all-to-all-start) | async-done | bytes 32800 | tf_op jit(solution)/shard_map/all_to_all | solution.py:568
  16.7 1.7 %force.1 = f32[128,128]{1,0:T(8,128)} custom-call(s32[1]{0:T(128)} %bitcast.here_ref, s32[1,1]{1,0:T(1,128)S(6)} %copy.13.live_ref, s32[1,1,64]{2,1,0:T(1,128)} %block_hbm.1, f32[64,128]{1,0:T(8,128)S(1)} %bitcast.6, f32[8,128]{1,0:T(8,128)S(1)} %collective-permute-done.below_ref, f32[8,128]{1,0:T(8,128)S(1)} %collective-permute-done.1.above_ref, ...), custom_call_target="tpu_custom_call" | custom-call | flops 31457280 | bytes 1048576 | tf_op jit(solution)/shard_map/force/pallas_call | solution.py:576
  18.4 6.0 %all-to-all-start.1 = ((f32[8,16,128]{2,1,0:T(8,128)}), f32[8,16,128]{2,1,0:T(8,128)S(1)}, u32[]{:S(2)}, u32[]{:S(2)}) async-start(f32[8,16,128]{2,1,0:T(8,128)} %bitcast.3), calls=%async_computation.1 | async-start | bytes 131072 | tf_op jit(solution)/shard_map/all_to_all | solution.py:615
  24.4 31.1 %all_gather.3.around_ref = f32[192,128]{1,0:T(8,128)S(1)} all-gather(f32[24,128]{1,0:T(8,128)S(1)} %get-tuple-element.12.static_ref), channel_id=1, replica_groups=mesh['slab'=4,'dom'=8] {'dom'}, dimensions={0}, use_global_device_ids=true | all-gather | bytes 110592 | tf_op jit(solution)/shard_map/all_gather | solution.py:597
  55.5 4.0 %bonds.1 = (f32[72,128]{1,0:T(8,128)S(1)}, bf16[2048,512]{1,0:T(8,128)(2,1)S(1)}, bf16[5120,256]{1,0:T(8,128)(2,1)S(1)}) custom-call(f32[192,128]{1,0:T(8,128)S(1)} %all_gather.3.around_ref), custom_call_target="tpu_custom_call" | custom-call | flops 18874368 | bytes 98304 | tf_op jit(solution)/shard_map/bonds/pallas_call | solution.py:600
  59.4 0.0 copy-start
  59.5 1.3 %copy-done = bf16[2048,512]{1,0:T(8,128)(2,1)} copy-done((bf16[2048,512]{1,0:T(8,128)(2,1)}, bf16[2048,512]{1,0:T(8,128)(2,1)S(1)}, u32[]{:S(2)}) %copy-start) | copy-done | bytes 2097176
  60.8 0.0 all-to-all-done.1
  60.8 0.0 copy-start.1
  60.8 1.6 %copy-done.1 = bf16[2048,512]{1,0:T(8,128)(2,1)S(1)} copy-done((bf16[2048,512]{1,0:T(8,128)(2,1)S(1)}, bf16[2048,512]{1,0:T(8,128)(2,1)}, u32[]{:S(2)}) %copy-start.1) | copy-done | bytes 2097176
  62.4 4.7 %solve.1 = (f32[3,1,1,512]{3,2,1,0:T(1,128)}, f32[3,1,1,512]{3,2,1,0:T(1,128)}) custom-call(s32[1]{0:T(128)} %bitcast.here_ref, f32[192,128]{1,0:T(8,128)S(1)} %all_gather.3.around_ref, f32[128,128]{1,0:T(8,128)S(1)} %bitcast.5, f32[72,128]{1,0:T(8,128)S(1)} %get-tuple-element.19.weight_ref, bf16[2048,512]{1,0:T(8,128)(2,1)S(1)} %copy-done.1, ...), custom_call_target="tpu_custom_call" | custom-call | tf_op jit(solution)/shard_map/solve/pallas_call | solution.py:617
Async XLA Ops:
  2.7 14.0 %all-to-all-start = ((f32[8,8,128]{2,1,0:T(8,128)}), f32[8,8,128]{2,1,0:T(8,128)S(1)}, u32[]{:S(2)}, u32[]{:S(2)}) async-start(f32[8,8,128]{2,1,0:T(8,128)} %bitcast.1), calls=%async_computation | async-start | bytes 65536 | tf_op jit(solution)/shard_map/all_to_all | solution.py:568
  10.0 2.8 %collective-permute-start.1 = (f32[8,128]{1,0:T(8,128)S(1)}, f32[8,128]{1,0:T(8,128)S(1)}, u32[]{:S(2)}, u32[]{:S(2)}) collective-permute-start(f32[8,128]{1,0:T(8,128)S(1)} %get-tuple-element.14), channel_id=1, source_target_pairs={{0,24},{8,0},{16,8},{24,16},{1,25},{9,1},{17,9},{25,17},{2,26},{10... | collective-permute-start | bytes 12296 | tf_op jit(solution)/shard_map/ppermute | solution.py:23
  10.7 3.0 %collective-permute-start = (f32[8,128]{1,0:T(8,128)S(1)}, f32[8,128]{1,0:T(8,128)S(1)}, u32[]{:S(2)}, u32[]{:S(2)}) collective-permute-start(f32[8,128]{1,0:T(8,128)S(1)} %get-tuple-element.14), channel_id=1, source_target_pairs={{0,8},{8,16},{16,24},{24,0},{1,9},{9,17},{17,25},{25,1},{2,10},{10... | collective-permute-start | bytes 12296 | tf_op jit(solution)/shard_map/ppermute | solution.py:23
  18.4 42.4 %all-to-all-start.1 = ((f32[8,16,128]{2,1,0:T(8,128)}), f32[8,16,128]{2,1,0:T(8,128)S(1)}, u32[]{:S(2)}, u32[]{:S(2)}) async-start(f32[8,16,128]{2,1,0:T(8,128)} %bitcast.3), calls=%async_computation.1 | async-start | bytes 131072 | tf_op jit(solution)/shard_map/all_to_all | solution.py:615
  59.4 1.3 %copy-start = (bf16[2048,512]{1,0:T(8,128)(2,1)}, bf16[2048,512]{1,0:T(8,128)(2,1)S(1)}, u32[]{:S(2)}) copy-start(bf16[2048,512]{1,0:T(8,128)(2,1)S(1)} %get-tuple-element.20.inner_ref) | copy-start | bytes 6291460
  60.8 1.6 %copy-start.1 = (bf16[2048,512]{1,0:T(8,128)(2,1)S(1)}, bf16[2048,512]{1,0:T(8,128)(2,1)}, u32[]{:S(2)}) copy-start(bf16[2048,512]{1,0:T(8,128)(2,1)} %copy-done) | copy-start | bytes 6291460

commit v4 on v2

--- a/solution.py
+++ b/solution.py
@@ -21,6 +21,33 @@
 def passed_along(array, axis, by):
     length = lax.axis_size(axis)
     return lax.ppermute(array, axis, [(i, (i + by) % length) for i in range(length)])
+
+
+def from_slab(block):
+    length = lax.axis_size("dom")
+    step = length // 2
+    while step:
+        other = lax.ppermute(block, "dom", [(i, i ^ step) for i in range(length)])
+        block = jnp.concatenate([block, other], axis=0)
+        step //= 2
+    return block
+
+
+def place_of(index, me, domains):
+    far = index ^ me
+    place, step, bit = 0, 1, domains // 2
+    while bit:
+        place = place + jnp.where((far & bit) != 0, step, 0)
+        step *= 2
+        bit //= 2
+    return place
+
+
+def in_order(source_ref, target_ref, me, domains):
+    count = source_ref.shape[0] // domains
+    for index in range(domains):
+        start = pl.multiple_of(place_of(index, me, domains) * count, SUBLANES)
+        target_ref[pl.ds(index * count, count), :] = source_ref[pl.ds(start, count), :]
 
 
 def strides_of(domains):
@@ -61,6 +88,10 @@
         at += self.slot_rows
         self.used = at
         self.count = round_up(at, SUBLANES)
+        self.shell_terms = (self.bond_rows + 5 * self.slot_rows) * LANES
+        self.matrix = self.shell_terms + self.bond_rows * LANES
+        self.inner_at = (0, self.shell_terms)
+        self.cross_at = self.bond_rows * LANES
         self.disp_used = 3 * self.atom_rows
         self.disp_count = round_up(self.disp_used, SUBLANES)
 
@@ -171,7 +202,7 @@
 def force_kernel(
     rows,
     copies,
-    holders,
+    holder,
     here_ref,
     live_ref,
     block_hbm,
@@ -196,7 +227,6 @@
     me = here_ref[0]
     starts = [rows.coords[0], rows.coords[1], rows.coords[2], rows.charge]
     entry_rows = 6 * shell_rows
-    blocks = around_ref.shape[0] // rows.count
 
     def broadcast(row):
         return jnp.broadcast_to(row, (SUBLANES, LANES))
@@ -205,7 +235,7 @@
         factor = SHRINK if c < 3 else 1.0
         at = 0
         for neighbour in range(4):
-            base = lax.rem(me + holders[neighbour], blocks) * rows.count + starts[c]
+            base = holder(me, neighbour) * rows.count + starts[c]
             for part in range(shell_rows):
                 table_ref[c, at] = broadcast(around_ref[pl.ds(base + part, 1), :] * factor)
                 at += 1
@@ -252,7 +282,7 @@
     for c in range(3):
         for part in range(atom_rows):
             total = jnp.sum(sum_ref[c, pl.ds(part * LANES, LANES), :].T, axis=0, keepdims=True)
-            mass = around_ref[pl.ds(me * rows.count + rows.mass + part, 1), :]
+            mass = around_ref[pl.ds(rows.mass + part, 1), :]
             moved = time_step * speed_ref[pl.ds(c * atom_rows + part, 1), :] + scale * total * mass
             for copy in range(copies):
                 out_ref[pl.ds(copy * rows.disp_count + c * atom_rows + part, 1), :] = moved
@@ -263,7 +293,8 @@
             )
 
 
-def bond_kernel(rows, domains, strides, around_ref, weight_ref, inner_ref, cross_ref, key_ref):
+def bond_kernel(rows, domains, strides, here_ref, blocks_ref, around_ref, weight_ref, matrix_ref, key_ref):
+    in_order(blocks_ref, around_ref, here_ref[0], domains)
     atom_rows, shell_rows = rows.atom_rows, rows.shell_rows
 
     def load(row):
@@ -313,21 +344,28 @@
     def column(row, group):
         return take_lanes(jnp.broadcast_to(row, (SUBLANES, LANES)), down + group * SUBLANES)
 
-    def one_hot(values, part):
-        return jnp.where(values == across + float(part * LANES), 1.0, 0.0)
+    def put(at, columns, signs, half):
+        for block in range(shell_rows):
+            lanes = across + float((half * shell_rows + block) * LANES)
+            halves = []
+            for ends in columns:
+                value = 0.0
+                for end, sign in zip(ends, signs):
+                    value = jnp.where(end == lanes, sign, value)
+                halves.append(value)
+            matrix_ref[pl.ds(at, pair), block * LANES : (block + 1) * LANES] = jnp.concatenate(
+                halves, axis=0
+            ).astype(jnp.bfloat16)
 
     def build(domain, _):
+        start = pl.multiple_of(domain * rows.matrix, LANES)
         for part in range(rows.bond_rows):
             first = around_ref[pl.ds(domain * rows.count + rows.bond_first + part, 1), :]
             second = around_ref[pl.ds(domain * rows.count + rows.bond_second + part, 1), :]
             for step in range(LANES // pair):
-                ends = [(column(first, 2 * step + h), column(second, 2 * step + h)) for h in range(2)]
-                at = pl.multiple_of((domain * rows.bond_rows + part) * LANES + step * pair, pair)
-                for block in range(atom_rows):
-                    halves = [one_hot(a, block) - one_hot(b, block) for a, b in ends]
-                    inner_ref[pl.ds(at, pair), block * LANES : (block + 1) * LANES] = jnp.concatenate(
-                        halves, axis=0
-                    ).astype(jnp.bfloat16)
+                columns = [(column(first, 2 * step + h), column(second, 2 * step + h)) for h in range(2)]
+                for half in range(2):
+                    put(start + rows.inner_at[half] + part * LANES + step * pair, columns, (1.0, -1.0), half)
         for part in range(rows.slot_rows):
             for code in range(5):
                 if code == 0:
@@ -337,13 +375,8 @@
                     row = key_ref[pl.ds((part * 4 + code - 1) * domains + owner, 1), :]
                 sign = 1.0 if code == 0 else -1.0
                 for step in range(LANES // pair):
-                    ends = [column(row, 2 * step + h) for h in range(2)]
-                    at = pl.multiple_of(((domain * rows.slot_rows + part) * 5 + code) * LANES + step * pair, pair)
-                    for block in range(shell_rows):
-                        halves = [sign * one_hot(a, block) for a in ends]
-                        cross_ref[pl.ds(at, pair), block * LANES : (block + 1) * LANES] = jnp.concatenate(
-                            halves, axis=0
-                        ).astype(jnp.bfloat16)
+                    columns = [(column(row, 2 * step + h),) for h in range(2)]
+                    put(start + rows.cross_at + (part * 5 + code) * LANES + step * pair, columns, (sign,), 0)
         return 0
 
     lax.fori_loop(0, domains, build, 0)
@@ -355,18 +388,19 @@
     strides,
     here_ref,
     around_ref,
-    moves_ref,
+    blocks_ref,
     weight_ref,
-    inner_ref,
-    cross_ref,
+    matrix_ref,
     coords_out_ref,
     velocity_out_ref,
+    moves_ref,
     push_ref,
     field_ref,
 ):
     atom_rows, shell_rows = rows.atom_rows, rows.shell_rows
     bond_rows, slot_rows = rows.bond_rows, rows.slot_rows
     me = here_ref[0]
+    in_order(blocks_ref, moves_ref, me, domains)
 
     def load(row):
         return around_ref[pl.ds(row, domains, stride=rows.count), :]
@@ -417,26 +451,25 @@
         return push_ref[at, pl.ds(domain, SUBLANES, stride=domains), :].astype(jnp.bfloat16)
 
     def totals(domain, owners):
-        inner = jnp.concatenate([pushes_of(p, domain) for p in range(bond_rows)], axis=1)
-        at = domain * bond_rows * LANES
-        if not isinstance(at, int):
-            at = pl.multiple_of(at, LANES)
-        inner_sum = jnp.dot(inner, inner_ref[pl.ds(at, bond_rows * LANES), :], preferred_element_type=jnp.float32)
-        pieces = []
+        inner = [pushes_of(p, domain) for p in range(bond_rows)]
+        cross = []
         for part in range(slot_rows):
-            pieces.extend(pushes_of(bond_rows + part, owner) for owner in [domain] + owners)
-        cross = jnp.concatenate(pieces, axis=1)
-        at = domain * slot_rows * 5 * LANES
-        if not isinstance(at, int):
-            at = pl.multiple_of(at, LANES)
-        cross_sum = jnp.dot(
-            cross, cross_ref[pl.ds(at, slot_rows * 5 * LANES), :], preferred_element_type=jnp.float32
+            cross.extend(pushes_of(bond_rows + part, owner) for owner in [domain] + owners)
+        start = domain * rows.matrix
+        if not isinstance(start, int):
+            start = pl.multiple_of(start, LANES)
+        shell_sum = jnp.dot(
+            jnp.concatenate(inner + cross, axis=1),
+            matrix_ref[pl.ds(start, rows.shell_terms), :],
+            preferred_element_type=jnp.float32,
         )
-        shell = shell_rows * LANES
+        other_sum = jnp.dot(
+            jnp.concatenate(inner, axis=1),
+            matrix_ref[pl.ds(start + rows.shell_terms, bond_rows * LANES), :],
+            preferred_element_type=jnp.float32,
+        )
         return [
-            inner_sum[:, p * LANES : (p + 1) * LANES]
-            + (cross_sum[:, p * LANES : (p + 1) * LANES] if p < shell_rows else 0.0)
-            for p in range(atom_rows)
+            half[:, p * LANES : (p + 1) * LANES] for half in (shell_sum, other_sum) for p in range(shell_rows)
         ]
 
     def spread(values):
@@ -531,7 +564,7 @@
     strides = strides_of(domains)
     rows = Rows(atoms, bond_atoms.shape[-1], cross_side.shape[-1])
     whole_slab = domains == SUBLANES
-    copies = domains if whole_slab else 1
+    copies = 1
     f32 = jnp.float32
 
     sent = (coords, charge, inv_mass, bond_atoms, cross_atoms, cross_side)
@@ -568,16 +601,22 @@
     below = passed_along(rim, "slab", 1)
     above = passed_along(rim, "slab", -1)
     if whole_slab:
-        around = lax.all_to_all(packed, "dom", 0, 0, tiled=True)
+        around = from_slab(packed)
         here = lax.axis_index("dom").reshape(1)
-        holders = [stride % domains for stride in strides]
+
+        def holder(me, neighbour):
+            return place_of(lax.rem(me + strides[neighbour] % domains, domains), me, domains)
+
     else:
         around = jnp.concatenate([packed] + [passed_along(packed, "dom", -stride) for stride in strides], axis=0)
         here = jnp.zeros(1, jnp.int32)
-        holders = [1, 2, 3, 4]
+
+        def holder(me, neighbour):
+            return neighbour + 1
+
 
     moves = pl.pallas_call(
-        functools.partial(force_kernel, rows, copies, holders),
+        functools.partial(force_kernel, rows, copies, holder),
         out_shape=jax.ShapeDtypeStruct((copies * rows.disp_count, LANES), f32),
         in_specs=smem(2) + hbm(1) + vmem(7),
         out_specs=vmem(1)[0],
@@ -597,22 +636,22 @@
         return by_exchange(rows, strides, around, moves, cross_count)
 
     constraint_rows = rows.bond_rows + rows.slot_rows
-    weight, inner, cross = pl.pallas_call(
+    ordered, weight, matrix = pl.pallas_call(
         functools.partial(bond_kernel, rows, domains, strides),
         out_shape=(
+            jax.ShapeDtypeStruct(around.shape, f32),
             jax.ShapeDtypeStruct((constraint_rows * 3 * domains, LANES), f32),
-            jax.ShapeDtypeStruct((domains * rows.bond_rows * LANES, atoms), jnp.bfloat16),
-            jax.ShapeDtypeStruct((domains * rows.slot_rows * 5 * LANES, atoms // 2), jnp.bfloat16),
+            jax.ShapeDtypeStruct((domains * rows.matrix, atoms // 2), jnp.bfloat16),
         ),
-        in_specs=vmem(1),
+        in_specs=smem(1) + vmem(1),
         out_specs=tuple(vmem(3)),
         scratch_shapes=[pltpu.VMEM((rows.slot_rows * 4 * domains, LANES), f32)],
         compiler_params=params(16),
-        cost_estimate=cost(8 * domains * (rows.bond_rows * LANES * atoms + rows.slot_rows * 5 * LANES * atoms // 2), 4 * around.size),
+        cost_estimate=cost(8 * domains * rows.matrix * atoms // 2, 4 * around.size),
         name="bonds",
-    )(around)
-
-    every_move = lax.all_to_all(moves, "dom", 0, 0, tiled=True)
+    )(here, around)
+
+    every_move = from_slab(moves)
 
     return pl.pallas_call(
         functools.partial(solve_kernel, rows, domains, strides),
@@ -620,15 +659,16 @@
             jax.ShapeDtypeStruct(coords.shape, f32),
             jax.ShapeDtypeStruct(coords.shape, f32),
         ),
-        in_specs=smem(1) + vmem(5),
+        in_specs=smem(1) + vmem(4),
         out_specs=tuple(vmem(2)),
         scratch_shapes=[
+            pltpu.VMEM(every_move.shape, f32),
             pltpu.VMEM((constraint_rows, SUBLANES * domains, LANES), f32),
             pltpu.VMEM((rows.atom_rows, SUBLANES * domains, LANES), f32),
         ],
         compiler_params=params(16),
         name="solve",
-    )(here, around, every_move, weight, inner, cross)
+    )(here, ordered, every_move, weight, matrix)
 
 
 def by_exchange(rows, strides, around, moves, cross_count):

time: 38.4 us -> 42.3 us (1.10)
  waiting for transfers between devices: 6.1 us -> 10.5 us
  local copies, waits for them, and re-layouts: 2.92 us -> 0.01 us
  Pallas kernels: 14.3 us -> 15.7 us
  starting transfers between devices: 12.8 us -> 13.4 us
    all_to_all x2 -> x0, starting transfers between devices: 12.2 us -> none  [the longest x1 7.29 us: shards(): around = lax.all_to_all(packed, 'dom', 0, 0, tiled=True)]
    ppermute x0 -> x6, starting transfers between devices: none -> 11 us  [from_slab(): other = lax.ppermute(block, 'dom', [(i, i ^ step) for i in range(length)])]
    ppermute x0 -> x6, waiting for transfers between devices: none -> 10.4 us  [from_slab(): other = lax.ppermute(block, 'dom', [(i, i ^ step) for i in range(length)])]
    all_to_all x2 -> x0, waiting for transfers between devices: 5.25 us -> none  [the longest x1 3.66 us: shards(): around = lax.all_to_all(packed, 'dom', 0, 0, tiled=True)]
    unnamed x4 -> x3, local copies, waits for them, and re-layouts: 2.92 us -> 0.01 us
    ppermute x2, starting transfers between devices: 0.65 us -> 2.43 us  [passed_along(): lax.ppermute(array, axis, [(i, (i + by) % length) for i in range(length)])]
    pallas_call x1, Pallas kernels: 2.61 us -> 4.24 us  [shards(): pl.pallas_call(functools.partial(force_kernel, rows, copies, holder), out...]
    ppermute x2, waiting for transfers between devices: 0.85 us -> 0.01 us  [passed_along(): lax.ppermute(array, axis, [(i, (i + by) % length) for i in range(length)])]
  transfers between devices with their start and end apart: 4 -> 8, of which waited for: 3 -> 4; matrix products, arithmetic and copies ran while one was open for 0% -> 0% of each run, Pallas kernels for 14% -> 13%
where the time goes in v4:
time: 42.3 us; the launch traced here: 41.7 us
  Pallas kernels  15.7 us (37%)
  starting transfers between devices  13.4 us (32%)
  waiting for transfers between devices  10.5 us (25%)
  between operations  2.01 us (5%)
    ppermute x6, starting transfers between devices, from_slab(): other = lax.ppermute(block, 'dom', [(i, i ^ step) for i in range(length)])  11 us
    ppermute x6, waiting for transfers between devices, from_slab(): other = lax.ppermute(block, 'dom', [(i, i ^ step) for i in range(length)])  10.4 us
    pallas_call x1, Pallas kernels, shards(): pl.pallas_call(functools.partial(solve_kernel, rows, domains, strides), o...  5.09 us
    pallas_call x1, Pallas kernels, shards(): pl.pallas_call(functools.partial(force_kernel, rows, copies, holder), out...  4.24 us
    pallas_call x1, Pallas kernels, shards(): pl.pallas_call(functools.partial(bond_kernel, rows, domains, strides), ou...  4.08 us
    ppermute x2, starting transfers between devices, passed_along(): lax.ppermute(array, axis, [(i, (i + by) % length) for i in range(length)])  2.43 us
    pallas_call x1, Pallas kernels, shards(): pl.pallas_call(functools.partial(own_kernel, rows), out_shape=(jax.ShapeD...  1.51 us
  transfers between devices with their start and end apart: 8, of which 4 were waited for; matrix products, arithmetic and copies ran while one was open for 0% of the time, Pallas kernels for 13%

profile of v4, /device:TPU:0, one launch (start us, length us, event | category | flops | bytes accessed | tf_op | source)
XLA Modules:
  0.0 41.7 jit_solution(1854473983135438705)
XLA Ops:
  1.3 0.8 %pack.1 = (f32[32,128]{1,0:T(8,128)S(1)}, f32[8,128]{1,0:T(8,128)S(1)}) custom-call(s32[1,1]{1,0:T(1,128)S(6)} %copy.17.count_ref, f32[3,1,1,512]{3,2,1,0:T(1,128)} %coords_hbm.1, f32[1,1,512]{2,1,0:T(1,128)} %charge_hbm.1, f32[1,1,512]{2,1,0:T(1,128)} %refs_2_.1, s32[2,1,1,256]{3,2,1,0:T(1,128)} %refs_3_.1, s32[2,1,1,128]{3,2,1,0:T(1,128)} %refs_4_.1, ...), custom_call_target="tpu_custom_call" | custom-call | tf_op jit(solution)/shard_map/pack/pallas_call | solution.py:571
  2.1 2.4 %collective-permute-start.4 = (f32[8,128]{1,0:T(8,128)S(1)}, f32[8,128]{1,0:T(8,128)S(1)}, u32[]{:S(2)}, u32[]{:S(2)}) collective-permute-start(f32[8,128]{1,0:T(8,128)S(1)} %get-tuple-element.13), channel_id=1, source_target_pairs={{0,24},{8,0},{16,8},{24,16},{1,25},{9,1},{17,9},{25,17},{2,26},{10... | collective-permute-start | bytes 12296 | tf_op jit(solution)/shard_map/ppermute | solution.py:23
  4.5 0.0 collective-permute-start.3
  4.5 2.6 %collective-permute-start = (f32[32,128]{1,0:T(8,128)S(1)}, f32[32,128]{1,0:T(8,128)S(1)}, u32[]{:S(2)}, u32[]{:S(2)}) collective-permute-start(f32[32,128]{1,0:T(8,128)S(1)} %get-tuple-element.11), channel_id=1, source_target_pairs={{0,4},{1,5},{2,6},{3,7},{4,0},{5,1},{6,2},{7,3},{8,12},{9,13},{10,... | collective-permute-start | bytes 49160 | tf_op jit(solution)/shard_map/ppermute | solution.py:30
  7.8 1.5 %own.1 = (f32[4,512,128]{2,1,0:T(8,128)S(1)}, f32[4,64,128]{2,1,0:T(8,128)S(1)}, s32[64,128]{1,0:T(8,128)S(1)}, f32[12,128]{1,0:T(8,128)S(1)}) custom-call(f32[3,1,1,512]{3,2,1,0:T(1,128)} %coords_hbm.1, f32[1,1,512]{2,1,0:T(1,128)} %charge_hbm.1, f32[3,1,1,512]{3,2,1,0:T(1,128)} %velocity_hbm.1, s32[1,1,64,128]{3,2,1,0:T(8,128)} %atoms_hbm.1), custom_call_target="tpu_custom_call" | custom-call | flops 4194304 | bytes 1048576 | tf_op jit(solution)/shard_map/own/pallas_call | solution.py:585
  9.3 0.0 collective-permute-done
  9.3 1.6 %collective-permute-start.1 = (f32[64,128]{1,0:T(8,128)S(1)}, f32[64,128]{1,0:T(8,128)S(1)}, u32[]{:S(2)}, u32[]{:S(2)}) collective-permute-start(f32[64,128]{1,0:T(8,128)S(1)} %pad_maximum_fusion.2), channel_id=1, source_target_pairs={{0,2},{1,3},{2,0},{3,1},{4,6},{5,7},{6,4},{7,5},{8,10},{9,11},{10,... | collective-permute-start | bytes 98312 | tf_op jit(solution)/shard_map/ppermute | solution.py:30
  11.0 2.3 %collective-permute-done.1 = f32[64,128]{1,0:T(8,128)S(1)} collective-permute-done((f32[64,128]{1,0:T(8,128)S(1)}, f32[64,128]{1,0:T(8,128)S(1)}, u32[]{:S(2)}, u32[]{:S(2)}) %collective-permute-start.1) | collective-permute-done | bytes 32800 | tf_op jit(solution)/shard_map/ppermute | solution.py:30
  13.3 1.5 %collective-permute-start.2 = (f32[128,128]{1,0:T(8,128)S(1)}, f32[128,128]{1,0:T(8,128)S(1)}, u32[]{:S(2)}, u32[]{:S(2)}) collective-permute-start(f32[128,128]{1,0:T(8,128)S(1)} %pad_maximum_fusion), channel_id=1, source_target_pairs={{0,1},{1,0},{2,3},{3,2},{4,5},{5,4},{6,7},{7,6},{8,9},{9,8},{10,11... | collective-permute-start | bytes 196616 | tf_op jit(solution)/shard_map/ppermute | solution.py:30
  14.8 2.7 %collective-permute-done.2 = f32[128,128]{1,0:T(8,128)S(1)} collective-permute-done((f32[128,128]{1,0:T(8,128)S(1)}, f32[128,128]{1,0:T(8,128)S(1)}, u32[]{:S(2)}, u32[]{:S(2)}) %collective-permute-start.2) | collective-permute-done | bytes 65568 | tf_op jit(solution)/shard_map/ppermute | solution.py:30
  17.6 0.0 collective-permute-done.4.above_ref
  17.6 0.0 collective-permute-done.3.below_ref
  17.6 4.2 %force.1 = f32[16,128]{1,0:T(8,128)S(1)} custom-call(s32[1]{0:T(128)} %bitcast.here_ref, s32[1,1]{1,0:T(1,128)S(6)} %copy.16.live_ref, s32[1,1,64]{2,1,0:T(1,128)} %block_hbm.1, f32[256,128]{1,0:T(8,128)S(1)} %constant_dynamic-update-slice_fusion.blocks_ref.around_ref, f32[8,128]{1,0:T(8,128)S(1)} %collective-permute-done.3.below_ref, ...), custom_call_target="tpu_custom_call" | custom-call | flops 31457280 | bytes 131072 | tf_op jit(solution)/shard_map/force/pallas_call | solution.py:618
  21.8 3.1 %collective-permute-start.5 = (f32[16,128]{1,0:T(8,128)S(1)}, f32[16,128]{1,0:T(8,128)S(1)}, u32[]{:S(2)}, u32[]{:S(2)}) collective-permute-start(f32[16,128]{1,0:T(8,128)S(1)} %force.1), channel_id=1, source_target_pairs={{0,4},{1,5},{2,6},{3,7},{4,0},{5,1},{6,2},{7,3},{8,12},{9,13},{10,... | collective-permute-start | bytes 24584 | tf_op jit(solution)/shard_map/ppermute | solution.py:30
  25.0 1.6 %collective-permute-done.5 = f32[16,128]{1,0:T(8,128)S(1)} collective-permute-done((f32[16,128]{1,0:T(8,128)S(1)}, f32[16,128]{1,0:T(8,128)S(1)}, u32[]{:S(2)}, u32[]{:S(2)}) %collective-permute-start.5) | collective-permute-done | bytes 8224 | tf_op jit(solution)/shard_map/ppermute | solution.py:30
  26.6 0.0 collective-permute-start.6
  26.6 3.7 %collective-permute-done.6 = f32[32,128]{1,0:T(8,128)S(1)} collective-permute-done((f32[32,128]{1,0:T(8,128)S(1)}, f32[32,128]{1,0:T(8,128)S(1)}, u32[]{:S(2)}, u32[]{:S(2)}) %collective-permute-start.6) | collective-permute-done | bytes 16416 | tf_op jit(solution)/shard_map/ppermute | solution.py:30
  30.4 2.1 %collective-permute-start.7 = (f32[64,128]{1,0:T(8,128)S(1)}, f32[64,128]{1,0:T(8,128)S(1)}, u32[]{:S(2)}, u32[]{:S(2)}) collective-permute-start(f32[64,128]{1,0:T(8,128)S(1)} %pad_maximum_fusion.3), channel_id=1, source_target_pairs={{0,1},{1,0},{2,3},{3,2},{4,5},{5,4},{6,7},{7,6},{8,9},{9,8},{10,11... | collective-permute-start | bytes 98312 | tf_op jit(solution)/shard_map/ppermute | solution.py:30
  32.5 4.1 %bonds.1 = (f32[256,128]{1,0:T(8,128)S(1)}, f32[72,128]{1,0:T(8,128)S(1)}, bf16[9216,256]{1,0:T(8,128)(2,1)S(1)}) custom-call(s32[1]{0:T(128)} %bitcast.here_ref, f32[256,128]{1,0:T(8,128)S(1)} %constant_dynamic-update-slice_fusion.blocks_ref.around_ref), custom_call_target="tpu_custom_call" | custom-call | flops 18874368 | bytes 131072 | tf_op jit(solution)/shard_map/bonds/pallas_call | solution.py:639
  36.6 0.0 collective-permute-done.7
  36.6 5.1 %solve.1 = (f32[3,1,1,512]{3,2,1,0:T(1,128)}, f32[3,1,1,512]{3,2,1,0:T(1,128)}) custom-call(s32[1]{0:T(128)} %bitcast.here_ref, f32[256,128]{1,0:T(8,128)S(1)} %get-tuple-element.12.around_ref, f32[128,128]{1,0:T(8,128)S(1)} %pad_maximum_fusion.1.blocks_ref, f32[72,128]{1,0:T(8,128)S(1)} %get-tuple-element.18.weight_ref, ...), custom_call_target="tpu_custom_call" | custom-call | tf_op jit(solution)/shard_map/solve/pallas_call | solution.py:656
  (9 shorter events, 0.0 us)
Async XLA Ops:
  2.1 15.5 %collective-permute-start.4 = (f32[8,128]{1,0:T(8,128)S(1)}, f32[8,128]{1,0:T(8,128)S(1)}, u32[]{:S(2)}, u32[]{:S(2)}) collective-permute-start(f32[8,128]{1,0:T(8,128)S(1)} %get-tuple-element.13), channel_id=1, source_target_pairs={{0,24},{8,0},{16,8},{24,16},{1,25},{9,1},{17,9},{25,17},{2,26},{10... | collective-permute-start | bytes 12296 | tf_op jit(solution)/shard_map/ppermute | solution.py:23
  4.5 13.1 %collective-permute-start.3 = (f32[8,128]{1,0:T(8,128)S(1)}, f32[8,128]{1,0:T(8,128)S(1)}, u32[]{:S(2)}, u32[]{:S(2)}) collective-permute-start(f32[8,128]{1,0:T(8,128)S(1)} %get-tuple-element.13), channel_id=1, source_target_pairs={{0,8},{8,16},{16,24},{24,0},{1,9},{9,17},{17,25},{25,1},{2,10},{10... | collective-permute-start | bytes 12296 | tf_op jit(solution)/shard_map/ppermute | solution.py:23
  4.5 4.8 %collective-permute-start = (f32[32,128]{1,0:T(8,128)S(1)}, f32[32,128]{1,0:T(8,128)S(1)}, u32[]{:S(2)}, u32[]{:S(2)}) collective-permute-start(f32[32,128]{1,0:T(8,128)S(1)} %get-tuple-element.11), channel_id=1, source_target_pairs={{0,4},{1,5},{2,6},{3,7},{4,0},{5,1},{6,2},{7,3},{8,12},{9,13},{10,... | collective-permute-start | bytes 49160 | tf_op jit(solution)/shard_map/ppermute | solution.py:30
  9.3 4.0 %collective-permute-start.1 = (f32[64,128]{1,0:T(8,128)S(1)}, f32[64,128]{1,0:T(8,128)S(1)}, u32[]{:S(2)}, u32[]{:S(2)}) collective-permute-start(f32[64,128]{1,0:T(8,128)S(1)} %pad_maximum_fusion.2), channel_id=1, source_target_pairs={{0,2},{1,3},{2,0},{3,1},{4,6},{5,7},{6,4},{7,5},{8,10},{9,11},{10,... | collective-permute-start | bytes 98312 | tf_op jit(solution)/shard_map/ppermute | solution.py:30
  13.3 4.3 %collective-permute-start.2 = (f32[128,128]{1,0:T(8,128)S(1)}, f32[128,128]{1,0:T(8,128)S(1)}, u32[]{:S(2)}, u32[]{:S(2)}) collective-permute-start(f32[128,128]{1,0:T(8,128)S(1)} %pad_maximum_fusion), channel_id=1, source_target_pairs={{0,1},{1,0},{2,3},{3,2},{4,5},{5,4},{6,7},{7,6},{8,9},{9,8},{10,11... | collective-permute-start | bytes 196616 | tf_op jit(solution)/shard_map/ppermute | solution.py:30
  21.8 4.8 %collective-permute-start.5 = (f32[16,128]{1,0:T(8,128)S(1)}, f32[16,128]{1,0:T(8,128)S(1)}, u32[]{:S(2)}, u32[]{:S(2)}) collective-permute-start(f32[16,128]{1,0:T(8,128)S(1)} %force.1), channel_id=1, source_target_pairs={{0,4},{1,5},{2,6},{3,7},{4,0},{5,1},{6,2},{7,3},{8,12},{9,13},{10,... | collective-permute-start | bytes 24584 | tf_op jit(solution)/shard_map/ppermute | solution.py:30
  26.6 3.7 %collective-permute-start.6 = (f32[32,128]{1,0:T(8,128)S(1)}, f32[32,128]{1,0:T(8,128)S(1)}, u32[]{:S(2)}, u32[]{:S(2)}) collective-permute-start(f32[32,128]{1,0:T(8,128)S(1)} %pad_maximum_fusion.4), channel_id=1, source_target_pairs={{0,2},{1,3},{2,0},{3,1},{4,6},{5,7},{6,4},{7,5},{8,10},{9,11},{10,... | collective-permute-start | bytes 49160 | tf_op jit(solution)/shard_map/ppermute | solution.py:30
  30.4 6.2 %collective-permute-start.7 = (f32[64,128]{1,0:T(8,128)S(1)}, f32[64,128]{1,0:T(8,128)S(1)}, u32[]{:S(2)}, u32[]{:S(2)}) collective-permute-start(f32[64,128]{1,0:T(8,128)S(1)} %pad_maximum_fusion.3), channel_id=1, source_target_pairs={{0,1},{1,0},{2,3},{3,2},{4,5},{5,4},{6,7},{7,6},{8,9},{9,8},{10,11... | collective-permute-start | bytes 98312 | tf_op jit(solution)/shard_map/ppermute | solution.py:30

commit v5 on v4

--- a/solution.py
+++ b/solution.py
@@ -21,33 +21,6 @@
 def passed_along(array, axis, by):
     length = lax.axis_size(axis)
     return lax.ppermute(array, axis, [(i, (i + by) % length) for i in range(length)])
-
-
-def from_slab(block):
-    length = lax.axis_size("dom")
-    step = length // 2
-    while step:
-        other = lax.ppermute(block, "dom", [(i, i ^ step) for i in range(length)])
-        block = jnp.concatenate([block, other], axis=0)
-        step //= 2
-    return block
-
-
-def place_of(index, me, domains):
-    far = index ^ me
-    place, step, bit = 0, 1, domains // 2
-    while bit:
-        place = place + jnp.where((far & bit) != 0, step, 0)
-        step *= 2
-        bit //= 2
-    return place
-
-
-def in_order(source_ref, target_ref, me, domains):
-    count = source_ref.shape[0] // domains
-    for index in range(domains):
-        start = pl.multiple_of(place_of(index, me, domains) * count, SUBLANES)
-        target_ref[pl.ds(index * count, count), :] = source_ref[pl.ds(start, count), :]
 
 
 def strides_of(domains):
@@ -70,8 +43,6 @@
         for _ in range(3):
             self.coords.append(at)
             at += self.atom_rows
-        self.charge = at
-        at += self.atom_rows
         self.mass = at
         at += self.atom_rows
         self.bond_first = at
@@ -88,6 +59,7 @@
         at += self.slot_rows
         self.used = at
         self.count = round_up(at, SUBLANES)
+        self.rim = 4 * self.shell_rows
         self.shell_terms = (self.bond_rows + 5 * self.slot_rows) * LANES
         self.matrix = self.shell_terms + self.bond_rows * LANES
         self.inner_at = (0, self.shell_terms)
@@ -122,7 +94,7 @@
 
 
 def pack_kernel(rows, copies, count_ref, *refs):
-    sources, (out_ref, rim_ref), targets, sem_ref = refs[:6], refs[6:8], refs[8:14], refs[14]
+    sources, (rim_ref, out_ref), targets, sem_ref = refs[:6], refs[6:8], refs[8:14], refs[14]
     for copy in fetched(sources, targets, sem_ref):
         copy.wait()
     coords_ref, charge_ref, mass_ref, bonds_ref, cross_ref, side_ref = targets
@@ -133,13 +105,12 @@
             for copy in range(copies):
                 out_ref[pl.ds(copy * rows.count + row + part, 1), :] = piece
 
-    shell = rows.shell_rows * LANES
     fields = [coords_ref[c, 0] for c in range(3)] + [charge_ref[0]]
     for c in range(4):
-        at = rows.coords[c] if c < 3 else rows.charge
-        put(at, fields[c])
         for part in range(rows.shell_rows):
             rim_ref[pl.ds(c * rows.shell_rows + part, 1), :] = fields[c][:, part * LANES : (part + 1) * LANES]
+    for c in range(3):
+        put(rows.coords[c], fields[c])
     put(rows.mass, mass_ref[0])
     put(rows.bond_first, bonds_ref[0, 0].astype(jnp.float32))
     put(rows.bond_second, bonds_ref[1, 0].astype(jnp.float32))
@@ -149,23 +120,34 @@
     put(rows.side, side.astype(jnp.float32))
     slot = lax.broadcasted_iota(jnp.int32, side.shape, 1)
     put(rows.live, jnp.where(slot < count_ref[0, 0], 1.0, 0.0))
-    if rows.count > rows.used:
-        for copy in range(copies):
-            out_ref[pl.ds(copy * rows.count + rows.used, rows.count - rows.used), :] = jnp.zeros(
-                (rows.count - rows.used, LANES), jnp.float32
-            )
+    for row in range(rows.used, rows.count):
+        put(row, jnp.zeros((1, LANES), jnp.float32))
 
 
 SHRINK = 1.0 / 4.0
 
 
 def own_kernel(
-    rows, coords_hbm, charge_hbm, velocity_hbm, atoms_hbm, own_ref, far_ref, index_ref, speed_ref, coords_ref, charge_ref, velocity_ref, sem_ref
+    rows,
+    coords_hbm,
+    charge_hbm,
+    velocity_hbm,
+    mass_hbm,
+    atoms_hbm,
+    own_ref,
+    far_ref,
+    index_ref,
+    motion_ref,
+    coords_ref,
+    charge_ref,
+    velocity_ref,
+    mass_ref,
+    sem_ref,
 ):
     atom_rows = rows.atom_rows
     copies = fetched(
-        (coords_hbm, charge_hbm, atoms_hbm.at[0, 0], velocity_hbm),
-        (coords_ref, charge_ref, index_ref, velocity_ref),
+        (coords_hbm, charge_hbm, atoms_hbm.at[0, 0], velocity_hbm, mass_hbm),
+        (coords_ref, charge_ref, index_ref, velocity_ref, mass_ref),
         sem_ref,
     )
     down = lax.broadcasted_iota(jnp.int32, (SUBLANES, LANES), 0)
@@ -194,25 +176,25 @@
         for c in range(4):
             far_ref[c, at, :] = pick(table[c], index)
     copies[3].wait()
-    for c in range(3):
+    copies[4].wait()
+    for c in range(4):
+        field = velocity_ref[c, 0] if c < 3 else mass_ref[0]
         for part in range(atom_rows):
-            speed_ref[pl.ds(c * atom_rows + part, 1), :] = velocity_ref[c, 0, :, lanes_of(part)]
+            motion_ref[pl.ds(c * atom_rows + part, 1), :] = field[:, lanes_of(part)]
 
 
 def force_kernel(
     rows,
     copies,
-    holder,
-    here_ref,
     live_ref,
     block_hbm,
-    around_ref,
+    rims_ref,
     below_ref,
     above_ref,
     own_ref,
     near_ref,
     index_ref,
-    speed_ref,
+    motion_ref,
     out_ref,
     table_ref,
     far_ref,
@@ -224,8 +206,6 @@
     tiles = index_ref.shape[0]
     block_copy = pltpu.make_async_copy(block_hbm, block_ref, sem_ref)
     block_copy.start()
-    me = here_ref[0]
-    starts = [rows.coords[0], rows.coords[1], rows.coords[2], rows.charge]
     entry_rows = 6 * shell_rows
 
     def broadcast(row):
@@ -235,9 +215,9 @@
         factor = SHRINK if c < 3 else 1.0
         at = 0
         for neighbour in range(4):
-            base = holder(me, neighbour) * rows.count + starts[c]
             for part in range(shell_rows):
-                table_ref[c, at] = broadcast(around_ref[pl.ds(base + part, 1), :] * factor)
+                row = neighbour * rows.rim + c * shell_rows + part
+                table_ref[c, at] = broadcast(rims_ref[pl.ds(row, 1), :] * factor)
                 at += 1
         for slab_ref in (below_ref, above_ref):
             for part in range(shell_rows):
@@ -282,8 +262,8 @@
     for c in range(3):
         for part in range(atom_rows):
             total = jnp.sum(sum_ref[c, pl.ds(part * LANES, LANES), :].T, axis=0, keepdims=True)
-            mass = around_ref[pl.ds(rows.mass + part, 1), :]
-            moved = time_step * speed_ref[pl.ds(c * atom_rows + part, 1), :] + scale * total * mass
+            mass = motion_ref[pl.ds(3 * atom_rows + part, 1), :]
+            moved = time_step * motion_ref[pl.ds(c * atom_rows + part, 1), :] + scale * total * mass
             for copy in range(copies):
                 out_ref[pl.ds(copy * rows.disp_count + c * atom_rows + part, 1), :] = moved
     if rows.disp_count > rows.disp_used:
@@ -293,8 +273,7 @@
             )
 
 
-def bond_kernel(rows, domains, strides, here_ref, blocks_ref, around_ref, weight_ref, matrix_ref, key_ref):
-    in_order(blocks_ref, around_ref, here_ref[0], domains)
+def bond_kernel(rows, domains, strides, around_ref, weight_ref, matrix_ref, key_ref):
     atom_rows, shell_rows = rows.atom_rows, rows.shell_rows
 
     def load(row):
@@ -339,7 +318,7 @@
 
     down = lax.broadcasted_iota(jnp.int32, (SUBLANES, LANES), 0)
     across = lax.broadcasted_iota(jnp.int32, (SUBLANES, LANES), 1).astype(jnp.float32)
-    pair = 2 * SUBLANES
+    group_rows = 4 * SUBLANES
 
     def column(row, group):
         return take_lanes(jnp.broadcast_to(row, (SUBLANES, LANES)), down + group * SUBLANES)
@@ -353,19 +332,19 @@
                 for end, sign in zip(ends, signs):
                     value = jnp.where(end == lanes, sign, value)
                 halves.append(value)
-            matrix_ref[pl.ds(at, pair), block * LANES : (block + 1) * LANES] = jnp.concatenate(
+            matrix_ref[pl.ds(at, group_rows), block * LANES : (block + 1) * LANES] = jnp.concatenate(
                 halves, axis=0
-            ).astype(jnp.bfloat16)
+            ).astype(matrix_ref.dtype)
 
     def build(domain, _):
         start = pl.multiple_of(domain * rows.matrix, LANES)
         for part in range(rows.bond_rows):
             first = around_ref[pl.ds(domain * rows.count + rows.bond_first + part, 1), :]
             second = around_ref[pl.ds(domain * rows.count + rows.bond_second + part, 1), :]
-            for step in range(LANES // pair):
-                columns = [(column(first, 2 * step + h), column(second, 2 * step + h)) for h in range(2)]
+            for step in range(LANES // group_rows):
+                columns = [(column(first, 4 * step + h), column(second, 4 * step + h)) for h in range(4)]
                 for half in range(2):
-                    put(start + rows.inner_at[half] + part * LANES + step * pair, columns, (1.0, -1.0), half)
+                    put(start + rows.inner_at[half] + part * LANES + step * group_rows, columns, (1.0, -1.0), half)
         for part in range(rows.slot_rows):
             for code in range(5):
                 if code == 0:
@@ -374,9 +353,9 @@
                     owner = lax.rem(domain + (-strides[code - 1]) % domains, domains)
                     row = key_ref[pl.ds((part * 4 + code - 1) * domains + owner, 1), :]
                 sign = 1.0 if code == 0 else -1.0
-                for step in range(LANES // pair):
-                    columns = [(column(row, 2 * step + h),) for h in range(2)]
-                    put(start + rows.cross_at + (part * 5 + code) * LANES + step * pair, columns, (sign,), 0)
+                for step in range(LANES // group_rows):
+                    columns = [(column(row, 4 * step + h),) for h in range(4)]
+                    put(start + rows.cross_at + (part * 5 + code) * LANES + step * group_rows, columns, (sign,), 0)
         return 0
 
     lax.fori_loop(0, domains, build, 0)
@@ -388,19 +367,25 @@
     strides,
     here_ref,
     around_ref,
-    blocks_ref,
+    moves_ref,
     weight_ref,
-    matrix_ref,
+    signs_ref,
     coords_out_ref,
     velocity_out_ref,
-    moves_ref,
     push_ref,
     field_ref,
+    matrix_ref,
 ):
     atom_rows, shell_rows = rows.atom_rows, rows.shell_rows
     bond_rows, slot_rows = rows.bond_rows, rows.slot_rows
     me = here_ref[0]
-    in_order(blocks_ref, moves_ref, me, domains)
+
+    def widen(domain, _):
+        at = pl.ds(pl.multiple_of(domain * rows.matrix, LANES), rows.matrix)
+        matrix_ref[at, :] = signs_ref[at, :].astype(matrix_ref.dtype)
+        return 0
+
+    lax.fori_loop(0, domains, widen, 0)
 
     def load(row):
         return around_ref[pl.ds(row, domains, stride=rows.count), :]
@@ -564,15 +549,15 @@
     strides = strides_of(domains)
     rows = Rows(atoms, bond_atoms.shape[-1], cross_side.shape[-1])
     whole_slab = domains == SUBLANES
-    copies = 1
+    copies = domains if whole_slab else 1
     f32 = jnp.float32
 
     sent = (coords, charge, inv_mass, bond_atoms, cross_atoms, cross_side)
-    packed, rim = pl.pallas_call(
+    rim, static = pl.pallas_call(
         functools.partial(pack_kernel, rows, copies),
         out_shape=(
+            jax.ShapeDtypeStruct((rows.rim, LANES), f32),
             jax.ShapeDtypeStruct((copies * rows.count, LANES), f32),
-            jax.ShapeDtypeStruct((4 * rows.shell_rows, LANES), f32),
         ),
         in_specs=smem(1) + hbm(len(sent)),
         out_specs=tuple(vmem(2)),
@@ -581,44 +566,36 @@
         name="pack",
     )(cross_count, *in_hbm(sent))
 
-    alone = (coords, charge, velocity, tile_atoms)
-    own, near, index, speed = pl.pallas_call(
+    if whole_slab:
+        around = lax.all_to_all(static, "dom", 0, 0, tiled=True)
+        here = lax.axis_index("dom").reshape(1)
+    else:
+        around = jnp.concatenate([static] + [passed_along(static, "dom", -stride) for stride in strides], axis=0)
+    rims = jnp.concatenate([passed_along(rim, "dom", -stride) for stride in strides], axis=0)
+    below = passed_along(rim, "slab", 1)
+    above = passed_along(rim, "slab", -1)
+
+    alone = (coords, charge, velocity, inv_mass, tile_atoms)
+    own, near, index, motion = pl.pallas_call(
         functools.partial(own_kernel, rows),
         out_shape=(
             jax.ShapeDtypeStruct((4, atoms, LANES), f32),
             jax.ShapeDtypeStruct((4, tiles, TILE), f32),
             jax.ShapeDtypeStruct((tiles, TILE), jnp.int32),
-            jax.ShapeDtypeStruct((rows.disp_used, LANES), f32),
+            jax.ShapeDtypeStruct((4 * rows.atom_rows, LANES), f32),
         ),
         in_specs=hbm(len(alone)),
         out_specs=tuple(vmem(4)),
-        scratch_shapes=room_for(alone[:3]) + [pltpu.SemaphoreType.DMA((len(alone),))],
+        scratch_shapes=room_for(alone[:4]) + [pltpu.SemaphoreType.DMA((len(alone),))],
         compiler_params=params(4),
         cost_estimate=cost(64 * atoms * LANES, 16 * atoms * LANES),
         name="own",
     )(*in_hbm(alone))
 
-    below = passed_along(rim, "slab", 1)
-    above = passed_along(rim, "slab", -1)
-    if whole_slab:
-        around = from_slab(packed)
-        here = lax.axis_index("dom").reshape(1)
-
-        def holder(me, neighbour):
-            return place_of(lax.rem(me + strides[neighbour] % domains, domains), me, domains)
-
-    else:
-        around = jnp.concatenate([packed] + [passed_along(packed, "dom", -stride) for stride in strides], axis=0)
-        here = jnp.zeros(1, jnp.int32)
-
-        def holder(me, neighbour):
-            return neighbour + 1
-
-
     moves = pl.pallas_call(
-        functools.partial(force_kernel, rows, copies, holder),
+        functools.partial(force_kernel, rows, copies),
         out_shape=jax.ShapeDtypeStruct((copies * rows.disp_count, LANES), f32),
-        in_specs=smem(2) + hbm(1) + vmem(7),
+        in_specs=smem(1) + hbm(1) + vmem(7),
         out_specs=vmem(1)[0],
         scratch_shapes=[
             pltpu.VMEM((4, 6 * rows.shell_rows, SUBLANES, LANES), f32),
@@ -627,31 +604,30 @@
             pltpu.SMEM(tile_block.shape, jnp.int32),
             pltpu.SemaphoreType.DMA(()),
         ],
-        compiler_params=params(8),
-        cost_estimate=cost(30 * tiles * TILE * TILE, 4 * around.size),
+        compiler_params=params(4),
+        cost_estimate=cost(30 * tiles * TILE * TILE, 4 * own.size),
         name="force",
-    )(here, active_tile_count, *in_hbm([tile_block]), around, below, above, own, near, index, speed)
+    )(active_tile_count, *in_hbm([tile_block]), rims, below, above, own, near, index, motion)
 
     if not whole_slab:
-        return by_exchange(rows, strides, around, moves, cross_count)
+        return by_exchange(rows, strides, around, moves)
 
     constraint_rows = rows.bond_rows + rows.slot_rows
-    ordered, weight, matrix = pl.pallas_call(
+    weight, matrix = pl.pallas_call(
         functools.partial(bond_kernel, rows, domains, strides),
         out_shape=(
-            jax.ShapeDtypeStruct(around.shape, f32),
             jax.ShapeDtypeStruct((constraint_rows * 3 * domains, LANES), f32),
-            jax.ShapeDtypeStruct((domains * rows.matrix, atoms // 2), jnp.bfloat16),
+            jax.ShapeDtypeStruct((domains * rows.matrix, atoms // 2), jnp.float8_e4m3fn),
         ),
-        in_specs=smem(1) + vmem(1),
-        out_specs=tuple(vmem(3)),
+        in_specs=vmem(1),
+        out_specs=tuple(vmem(2)),
         scratch_shapes=[pltpu.VMEM((rows.slot_rows * 4 * domains, LANES), f32)],
         compiler_params=params(16),
         cost_estimate=cost(8 * domains * rows.matrix * atoms // 2, 4 * around.size),
         name="bonds",
-    )(here, around)
-
-    every_move = from_slab(moves)
+    )(around)
+
+    every_move = lax.all_to_all(moves, "dom", 0, 0, tiled=True)
 
     return pl.pallas_call(
         functools.partial(solve_kernel, rows, domains, strides),
@@ -662,16 +638,16 @@
         in_specs=smem(1) + vmem(4),
         out_specs=tuple(vmem(2)),
         scratch_shapes=[
-            pltpu.VMEM(every_move.shape, f32),
             pltpu.VMEM((constraint_rows, SUBLANES * domains, LANES), f32),
             pltpu.VMEM((rows.atom_rows, SUBLANES * domains, LANES), f32),
+            pltpu.VMEM(matrix.shape, jnp.bfloat16),
         ],
         compiler_params=params(16),
         name="solve",
-    )(here, ordered, every_move, weight, matrix)
-
-
-def by_exchange(rows, strides, around, moves, cross_count):
+    )(here, around, every_move, weight, matrix)
+
+
+def by_exchange(rows, strides, around, moves):
     atom_count = rows.atom_rows * LANES
     shell = rows.shell_rows * LANES
     inside = around.reshape(5, rows.count, LANES)

time: 42.3 us -> 44.6 us (1.054); the launches traced: 41.7 us -> 45.4 us
  starting transfers between devices: 13.4 us -> 19.8 us
  waiting for transfers between devices: 10.5 us -> 5.28 us
  Pallas kernels: 15.7 us -> 18.4 us
    ppermute x6 -> x0, starting transfers between devices: 11 us -> none  [from_slab(): other = lax.ppermute(block, 'dom', [(i, i ^ step) for i in range(length)])]
    all_to_all x0 -> x2, starting transfers between devices: none -> 10.7 us  [the longest x1 7.29 us: shards(): around = lax.all_to_all(static, 'dom', 0, 0, tiled=True)]
    ppermute x6 -> x0, waiting for transfers between devices: 10.4 us -> none  [from_slab(): other = lax.ppermute(block, 'dom', [(i, i ^ step) for i in range(length)])]
    ppermute x2 -> x6, starting transfers between devices: 2.43 us -> 9.13 us  [passed_along(): lax.ppermute(array, axis, [(i, (i + by) % length) for i in range(length)])]
    all_to_all x0 -> x2, waiting for transfers between devices: none -> 2.78 us  [the longest x1 2.78 us: shards(): every_move = lax.all_to_all(moves, 'dom', 0, 0, tiled=True)]
    ppermute x2 -> x6, waiting for transfers between devices: 0.01 us -> 2.5 us  [passed_along(): lax.ppermute(array, axis, [(i, (i + by) % length) for i in range(length)])]
    pallas_call x1, Pallas kernels: 4.24 us -> 5.9 us  [shards(): pl.pallas_call(functools.partial(force_kernel, rows, copies), out_shape=j...]
    pallas_call x1, Pallas kernels: 0.81 us -> 1.48 us  [shards(): pl.pallas_call(functools.partial(pack_kernel, rows, copies), out_shape=(j...]
  transfers between devices with their start and end apart: 8 -> 8, of which waited for: 4 -> 2; matrix products, arithmetic and copies ran while one was open for 0% -> 0% of each run, Pallas kernels for 13% -> 25%
where the time goes in v5:
time: 44.6 us; the launch traced here: 45.4 us
  starting transfers between devices  19.8 us (44%)
  Pallas kernels  18.4 us (41%)
  waiting for transfers between devices  5.28 us (12%)
  between operations  2.01 us (5%)
    ppermute x6, starting transfers between devices, passed_along(): lax.ppermute(array, axis, [(i, (i + by) % length) for i in range(length)])  9.13 us
    all_to_all x1, starting transfers between devices, shards(): around = lax.all_to_all(static, 'dom', 0, 0, tiled=True)  7.29 us
    pallas_call x1, Pallas kernels, shards(): pl.pallas_call(functools.partial(force_kernel, rows, copies), out_shape=j...  5.9 us
    pallas_call x1, Pallas kernels, shards(): pl.pallas_call(functools.partial(solve_kernel, rows, domains, strides), o...  5.38 us
    pallas_call x1, Pallas kernels, shards(): pl.pallas_call(functools.partial(bond_kernel, rows, domains, strides), ou...  4.05 us
    all_to_all x1, starting transfers between devices, shards(): every_move = lax.all_to_all(moves, 'dom', 0, 0, tiled=True)  3.36 us
    all_to_all x1, waiting for transfers between devices, shards(): every_move = lax.all_to_all(moves, 'dom', 0, 0, tiled=True)  2.78 us
    ppermute x6, waiting for transfers between devices, passed_along(): lax.ppermute(array, axis, [(i, (i + by) % length) for i in range(length)])  2.5 us
  transfers between devices with their start and end apart: 8, of which 2 were waited for; matrix products, arithmetic and copies ran while one was open for 0% of the time, Pallas kernels for 25%

profile of v5, /device:TPU:0, one launch (start us, length us, event | category | flops | bytes accessed | tf_op | source)
XLA Modules:
  0.0 45.4 jit_solution(10274123592335333220)
XLA Ops:
  1.3 1.5 %pack.1 = (f32[8,128]{1,0:T(8,128)S(1)}, f32[192,128]{1,0:T(8,128)}) custom-call(s32[1,1]{1,0:T(1,128)S(6)} %copy.14.count_ref, f32[3,1,1,512]{3,2,1,0:T(1,128)} %coords_hbm.1, f32[1,1,512]{2,1,0:T(1,128)} %charge_hbm.1, f32[1,1,512]{2,1,0:T(1,128)} %mass_hbm.1, s32[2,1,1,256]{3,2,1,0:T(1,128)} %refs_3_.1, s32[2,1,1,128]{3,2,1,0:T(1,128)} %refs_4_.1, ...), custom_call_target="tpu_custom_call" | custom-call | tf_op jit(solution)/shard_map/pack/pallas_call | solution.py:556
  2.8 7.3 %all-to-all-start = ((f32[8,24,128]{2,1,0:T(8,128)}), f32[8,24,128]{2,1,0:T(8,128)S(1)}, u32[]{:S(2)}, u32[]{:S(2)}) async-start(f32[8,24,128]{2,1,0:T(8,128)} %bitcast.1), calls=%async_computation | async-start | bytes 196608 | tf_op jit(solution)/shard_map/all_to_all | solution.py:570
  10.1 2.0 %collective-permute-start.3 = (f32[8,128]{1,0:T(8,128)S(1)}, f32[8,128]{1,0:T(8,128)S(1)}, u32[]{:S(2)}, u32[]{:S(2)}) collective-permute-start(f32[8,128]{1,0:T(8,128)S(1)} %get-tuple-element.11), channel_id=1, source_target_pairs={{0,2},{1,3},{2,4},{3,5},{4,6},{5,7},{6,0},{7,1},{8,10},{9,11},{10,... | collective-permute-start | bytes 12296 | tf_op jit(solution)/shard_map/ppermute | solution.py:23
  12.1 1.8 %collective-permute-start.2 = (f32[8,128]{1,0:T(8,128)S(1)}, f32[8,128]{1,0:T(8,128)S(1)}, u32[]{:S(2)}, u32[]{:S(2)}) collective-permute-start(f32[8,128]{1,0:T(8,128)S(1)} %get-tuple-element.11), channel_id=1, source_target_pairs={{0,6},{1,7},{2,0},{3,1},{4,2},{5,3},{6,4},{7,5},{8,14},{9,15},{10,... | collective-permute-start | bytes 12296 | tf_op jit(solution)/shard_map/ppermute | solution.py:23
  13.9 2.0 %collective-permute-start.1 = (f32[8,128]{1,0:T(8,128)S(1)}, f32[8,128]{1,0:T(8,128)S(1)}, u32[]{:S(2)}, u32[]{:S(2)}) collective-permute-start(f32[8,128]{1,0:T(8,128)S(1)} %get-tuple-element.11), channel_id=1, source_target_pairs={{0,1},{1,2},{2,3},{3,4},{4,5},{5,6},{6,7},{7,0},{8,9},{9,10},{10,1... | collective-permute-start | bytes 12296 | tf_op jit(solution)/shard_map/ppermute | solution.py:23
  15.9 2.7 %collective-permute-start = (f32[8,128]{1,0:T(8,128)S(1)}, f32[8,128]{1,0:T(8,128)S(1)}, u32[]{:S(2)}, u32[]{:S(2)}) collective-permute-start(f32[8,128]{1,0:T(8,128)S(1)} %get-tuple-element.11), channel_id=1, source_target_pairs={{0,7},{1,0},{2,1},{3,2},{4,3},{5,4},{6,5},{7,6},{8,15},{9,8},{10,9... | collective-permute-start | bytes 12296 | tf_op jit(solution)/shard_map/ppermute | solution.py:23
  18.6 0.0 collective-permute-start.5
  19.3 1.5 %own.1 = (f32[4,512,128]{2,1,0:T(8,128)S(1)}, f32[4,64,128]{2,1,0:T(8,128)S(1)}, s32[64,128]{1,0:T(8,128)S(1)}, f32[16,128]{1,0:T(8,128)S(1)}) custom-call(f32[3,1,1,512]{3,2,1,0:T(1,128)} %coords_hbm.1, f32[1,1,512]{2,1,0:T(1,128)} %charge_hbm.1, f32[3,1,1,512]{3,2,1,0:T(1,128)} %velocity_hbm.1, f32[1,1,512]{2,1,0:T(1,128)} %mass_hbm.1, ...), custom_call_target="tpu_custom_call" | custom-call | flops 4194304 | bytes 1048576 | tf_op jit(solution)/shard_map/own/pallas_call | solution.py:579
  20.8 0.0 collective-permute-done.3
  20.8 0.6 %collective-permute-start.4 = (f32[8,128]{1,0:T(8,128)S(1)}, f32[8,128]{1,0:T(8,128)S(1)}, u32[]{:S(2)}, u32[]{:S(2)}) collective-permute-start(f32[8,128]{1,0:T(8,128)S(1)} %get-tuple-element.11), channel_id=1, source_target_pairs={{0,8},{8,16},{16,24},{24,0},{1,9},{9,17},{17,25},{25,1},{2,10},{10... | collective-permute-start | bytes 12296 | tf_op jit(solution)/shard_map/ppermute | solution.py:23
  21.4 0.0 collective-permute-done.2
  21.4 0.0 collective-permute-done.1
  21.4 0.0 collective-permute-done
  21.4 0.0 collective-permute-done.5.above_ref
  21.4 2.5 %collective-permute-done.4.below_ref = f32[8,128]{1,0:T(8,128)S(1)} collective-permute-done((f32[8,128]{1,0:T(8,128)S(1)}, f32[8,128]{1,0:T(8,128)S(1)}, u32[]{:S(2)}, u32[]{:S(2)}) %collective-permute-start.4) | collective-permute-done | bytes 4128 | tf_op jit(solution)/shard_map/ppermute | solution.py:23
  23.9 5.9 %force.1 = f32[128,128]{1,0:T(8,128)} custom-call(s32[1,1]{1,0:T(1,128)S(6)} %copy.13.live_ref, s32[1,1,64]{2,1,0:T(1,128)} %block_hbm.1, f32[32,128]{1,0:T(8,128)S(1)} %pad_maximum_fusion.rims_ref, f32[8,128]{1,0:T(8,128)S(1)} %collective-permute-done.4.below_ref, f32[8,128]{1,0:T(8,128)S(1)} %collective-permute-done.5.above_ref, ...), custom_call_target="tpu_custom_call" | custom-call | flops 31457280 | bytes 1048576 | tf_op jit(solution)/shard_map/force/pallas_call | solution.py:595
  29.8 0.0 all-to-all-done
  29.9 3.4 %all-to-all-start.1 = ((f32[8,16,128]{2,1,0:T(8,128)}), f32[8,16,128]{2,1,0:T(8,128)S(1)}, u32[]{:S(2)}, u32[]{:S(2)}) async-start(f32[8,16,128]{2,1,0:T(8,128)} %bitcast.3), calls=%async_computation.1 | async-start | bytes 131072 | tf_op jit(solution)/shard_map/all_to_all | solution.py:630
  33.2 4.1 %bonds.1 = (f32[72,128]{1,0:T(8,128)S(1)}, f8e4m3fn[9216,256]{1,0:T(32,128)(4,1)S(1)}) custom-call(f32[192,128]{1,0:T(8,128)S(1)} %bitcast.5), custom_call_target="tpu_custom_call" | custom-call | flops 18874368 | bytes 98304 | tf_op jit(solution)/shard_map/bonds/pallas_call | solution.py:616
  37.3 2.8 %all-to-all-done.1 = f32[8,16,128]{2,1,0:T(8,128)S(1)} async-done(((f32[8,16,128]{2,1,0:T(8,128)}), f32[8,16,128]{2,1,0:T(8,128)S(1)}, u32[]{:S(2)}, u32[]{:S(2)}) %all-to-all-start.1) | async-done | bytes 65568 | tf_op jit(solution)/shard_map/all_to_all | solution.py:630
  40.1 5.4 %solve.1 = (f32[3,1,1,512]{3,2,1,0:T(1,128)}, f32[3,1,1,512]{3,2,1,0:T(1,128)}) custom-call(s32[1]{0:T(128)} %bitcast.here_ref, f32[192,128]{1,0:T(8,128)S(1)} %bitcast.6, f32[128,128]{1,0:T(8,128)S(1)} %bitcast.7, f32[72,128]{1,0:T(8,128)S(1)} %get-tuple-element.16.weight_ref, f8e4m3fn[9216,256]{1,0:T(32,128)(4,1)S(1)} %get-tuple-element.17.signs_ref), custom_call_target="tpu_custom_call" | custom-call | tf_op jit(solution)/shard_map/solve/pallas_call | solution.py:632
  (1 shorter events, 0.0 us)
Async XLA Ops:
  2.8 27.1 %all-to-all-start = ((f32[8,24,128]{2,1,0:T(8,128)}), f32[8,24,128]{2,1,0:T(8,128)S(1)}, u32[]{:S(2)}, u32[]{:S(2)}) async-start(f32[8,24,128]{2,1,0:T(8,128)} %bitcast.1), calls=%async_computation | async-start | bytes 196608 | tf_op jit(solution)/shard_map/all_to_all | solution.py:570
  10.1 10.8 %collective-permute-start.3 = (f32[8,128]{1,0:T(8,128)S(1)}, f32[8,128]{1,0:T(8,128)S(1)}, u32[]{:S(2)}, u32[]{:S(2)}) collective-permute-start(f32[8,128]{1,0:T(8,128)S(1)} %get-tuple-element.11), channel_id=1, source_target_pairs={{0,2},{1,3},{2,4},{3,5},{4,6},{5,7},{6,0},{7,1},{8,10},{9,11},{10,... | collective-permute-start | bytes 12296 | tf_op jit(solution)/shard_map/ppermute | solution.py:23
  12.1 9.3 %collective-permute-start.2 = (f32[8,128]{1,0:T(8,128)S(1)}, f32[8,128]{1,0:T(8,128)S(1)}, u32[]{:S(2)}, u32[]{:S(2)}) collective-permute-start(f32[8,128]{1,0:T(8,128)S(1)} %get-tuple-element.11), channel_id=1, source_target_pairs={{0,6},{1,7},{2,0},{3,1},{4,2},{5,3},{6,4},{7,5},{8,14},{9,15},{10,... | collective-permute-start | bytes 12296 | tf_op jit(solution)/shard_map/ppermute | solution.py:23
  13.9 7.5 %collective-permute-start.1 = (f32[8,128]{1,0:T(8,128)S(1)}, f32[8,128]{1,0:T(8,128)S(1)}, u32[]{:S(2)}, u32[]{:S(2)}) collective-permute-start(f32[8,128]{1,0:T(8,128)S(1)} %get-tuple-element.11), channel_id=1, source_target_pairs={{0,1},{1,2},{2,3},{3,4},{4,5},{5,6},{6,7},{7,0},{8,9},{9,10},{10,1... | collective-permute-start | bytes 12296 | tf_op jit(solution)/shard_map/ppermute | solution.py:23
  15.9 5.5 %collective-permute-start = (f32[8,128]{1,0:T(8,128)S(1)}, f32[8,128]{1,0:T(8,128)S(1)}, u32[]{:S(2)}, u32[]{:S(2)}) collective-permute-start(f32[8,128]{1,0:T(8,128)S(1)} %get-tuple-element.11), channel_id=1, source_target_pairs={{0,7},{1,0},{2,1},{3,2},{4,3},{5,4},{6,5},{7,6},{8,15},{9,8},{10,9... | collective-permute-start | bytes 12296 | tf_op jit(solution)/shard_map/ppermute | solution.py:23
  18.6 2.8 %collective-permute-start.5 = (f32[8,128]{1,0:T(8,128)S(1)}, f32[8,128]{1,0:T(8,128)S(1)}, u32[]{:S(2)}, u32[]{:S(2)}) collective-permute-start(f32[8,128]{1,0:T(8,128)S(1)} %get-tuple-element.11), channel_id=1, source_target_pairs={{0,24},{8,0},{16,8},{24,16},{1,25},{9,1},{17,9},{25,17},{2,26},{10... | collective-permute-start | bytes 12296 | tf_op jit(solution)/shard_map/ppermute | solution.py:23
  20.8 3.1 %collective-permute-start.4 = (f32[8,128]{1,0:T(8,128)S(1)}, f32[8,128]{1,0:T(8,128)S(1)}, u32[]{:S(2)}, u32[]{:S(2)}) collective-permute-start(f32[8,128]{1,0:T(8,128)S(1)} %get-tuple-element.11), channel_id=1, source_target_pairs={{0,8},{8,16},{16,24},{24,0},{1,9},{9,17},{17,25},{25,1},{2,10},{10... | collective-permute-start | bytes 12296 | tf_op jit(solution)/shard_map/ppermute | solution.py:23
  29.9 10.2 %all-to-all-start.1 = ((f32[8,16,128]{2,1,0:T(8,128)}), f32[8,16,128]{2,1,0:T(8,128)S(1)}, u32[]{:S(2)}, u32[]{:S(2)}) async-start(f32[8,16,128]{2,1,0:T(8,128)} %bitcast.3), calls=%async_computation.1 | async-start | bytes 131072 | tf_op jit(solution)/shard_map/all_to_all | solution.py:630

commit v6 on v5

--- a/solution.py
+++ b/solution.py
@@ -43,6 +43,8 @@
         for _ in range(3):
             self.coords.append(at)
             at += self.atom_rows
+        self.charge = at
+        at += self.atom_rows
         self.mass = at
         at += self.atom_rows
         self.bond_first = at
@@ -59,7 +61,6 @@
         at += self.slot_rows
         self.used = at
         self.count = round_up(at, SUBLANES)
-        self.rim = 4 * self.shell_rows
         self.shell_terms = (self.bond_rows + 5 * self.slot_rows) * LANES
         self.matrix = self.shell_terms + self.bond_rows * LANES
         self.inner_at = (0, self.shell_terms)
@@ -81,11 +82,6 @@
     return result
 
 
-def rsqrt(value):
-    guess = lax.rsqrt(value)
-    return guess * (1.5 - 0.5 * value * guess * guess)
-
-
 def fetched(sources, targets, sem_ref):
     copies = [pltpu.make_async_copy(s, t, sem_ref.at[n]) for n, (s, t) in enumerate(zip(sources, targets))]
     for copy in copies:
@@ -94,7 +90,7 @@
 
 
 def pack_kernel(rows, copies, count_ref, *refs):
-    sources, (rim_ref, out_ref), targets, sem_ref = refs[:6], refs[6:8], refs[8:14], refs[14]
+    sources, (out_ref, rim_ref), targets, sem_ref = refs[:6], refs[6:8], refs[8:14], refs[14]
     for copy in fetched(sources, targets, sem_ref):
         copy.wait()
     coords_ref, charge_ref, mass_ref, bonds_ref, cross_ref, side_ref = targets
@@ -105,12 +101,13 @@
             for copy in range(copies):
                 out_ref[pl.ds(copy * rows.count + row + part, 1), :] = piece
 
+    shell = rows.shell_rows * LANES
     fields = [coords_ref[c, 0] for c in range(3)] + [charge_ref[0]]
     for c in range(4):
+        at = rows.coords[c] if c < 3 else rows.charge
+        put(at, fields[c])
         for part in range(rows.shell_rows):
             rim_ref[pl.ds(c * rows.shell_rows + part, 1), :] = fields[c][:, part * LANES : (part + 1) * LANES]
-    for c in range(3):
-        put(rows.coords[c], fields[c])
     put(rows.mass, mass_ref[0])
     put(rows.bond_first, bonds_ref[0, 0].astype(jnp.float32))
     put(rows.bond_second, bonds_ref[1, 0].astype(jnp.float32))
@@ -120,11 +117,39 @@
     put(rows.side, side.astype(jnp.float32))
     slot = lax.broadcasted_iota(jnp.int32, side.shape, 1)
     put(rows.live, jnp.where(slot < count_ref[0, 0], 1.0, 0.0))
-    for row in range(rows.used, rows.count):
-        put(row, jnp.zeros((1, LANES), jnp.float32))
+    if rows.count > rows.used:
+        for copy in range(copies):
+            out_ref[pl.ds(copy * rows.count + rows.used, rows.count - rows.used), :] = jnp.zeros(
+                (rows.count - rows.used, LANES), jnp.float32
+            )
 
 
 SHRINK = 1.0 / 4.0
+
+
+TERMS = 32
+
+
+def narrow(value):
+    return value.astype(jnp.bfloat16).astype(jnp.float32)
+
+
+def split(value):
+    high = narrow(value)
+    middle = narrow(value - high)
+    return high, middle, value - high - middle
+
+
+def distance_terms(place, offset, own):
+    factor = 1.0 if own else -2.0
+    terms = []
+    for value in place:
+        high, middle, low = split(value)
+        pick_from = (high, high, middle, middle, high, low) if own else (high, middle, high, middle, low, high)
+        terms.extend(factor * part for part in pick_from)
+    square = place[0] * place[0] + place[1] * place[1] + place[2] * place[2] + offset
+    ones = [jnp.ones_like(square)] * 3
+    return terms + (list(split(square)) + ones if own else ones + list(split(square)))
 
 
 def own_kernel(
@@ -134,6 +159,7 @@
     velocity_hbm,
     mass_hbm,
     atoms_hbm,
+    terms_ref,
     own_ref,
     far_ref,
     index_ref,
@@ -151,6 +177,7 @@
         sem_ref,
     )
     down = lax.broadcasted_iota(jnp.int32, (SUBLANES, LANES), 0)
+    across = lax.broadcasted_iota(jnp.int32, (SUBLANES, LANES), 1)
     copies[0].wait()
     copies[1].wait()
 
@@ -164,11 +191,18 @@
             [jnp.broadcast_to(field[:, lanes_of(part)], (SUBLANES, LANES)) for part in range(atom_rows)]
         )
     for part in range(atom_rows):
-        for group in range(LANES // SUBLANES):
-            at = part * LANES + group * SUBLANES
-            for c in range(4):
-                value = take_lanes(table[c][part], down + group * SUBLANES)
-                own_ref[c, pl.ds(at, SUBLANES), :] = value if c < 3 else value * 8.0
+        for pair in range(LANES // SUBLANES // 2):
+            halves = []
+            for group in (2 * pair, 2 * pair + 1):
+                at = part * LANES + group * SUBLANES
+                values = [take_lanes(table[c][part], down + group * SUBLANES) for c in range(4)]
+                own_ref[pl.ds(at, SUBLANES), :] = values[3] * 8.0
+                row = jnp.zeros((SUBLANES, LANES), jnp.float32)
+                for lane, term in enumerate(distance_terms(values[:3], 0.0, True)):
+                    row = jnp.where(across == lane, term, row)
+                halves.append(row)
+            at = part * LANES + pair * 2 * SUBLANES
+            terms_ref[pl.ds(at, 2 * SUBLANES), :] = jnp.concatenate(halves, axis=0).astype(jnp.bfloat16)
     copies[2].wait()
     for group in range(index_ref.shape[0] // SUBLANES):
         at = pl.ds(group * SUBLANES, SUBLANES)
@@ -177,8 +211,8 @@
             far_ref[c, at, :] = pick(table[c], index)
     copies[3].wait()
     copies[4].wait()
-    for c in range(4):
-        field = velocity_ref[c, 0] if c < 3 else mass_ref[0]
+    fields = [velocity_ref[c, 0] for c in range(3)] + [coords_ref[c, 0] * SHRINK for c in range(3)] + [mass_ref[0]]
+    for c, field in enumerate(fields):
         for part in range(atom_rows):
             motion_ref[pl.ds(c * atom_rows + part, 1), :] = field[:, lanes_of(part)]
 
@@ -186,11 +220,14 @@
 def force_kernel(
     rows,
     copies,
+    holders,
+    here_ref,
     live_ref,
     block_hbm,
-    rims_ref,
+    around_ref,
     below_ref,
     above_ref,
+    terms_ref,
     own_ref,
     near_ref,
     index_ref,
@@ -198,6 +235,7 @@
     out_ref,
     table_ref,
     far_ref,
+    far_terms_ref,
     sum_ref,
     block_ref,
     sem_ref,
@@ -206,7 +244,10 @@
     tiles = index_ref.shape[0]
     block_copy = pltpu.make_async_copy(block_hbm, block_ref, sem_ref)
     block_copy.start()
+    me = here_ref[0]
+    starts = [rows.coords[0], rows.coords[1], rows.coords[2], rows.charge]
     entry_rows = 6 * shell_rows
+    blocks = around_ref.shape[0] // rows.count
 
     def broadcast(row):
         return jnp.broadcast_to(row, (SUBLANES, LANES))
@@ -215,9 +256,9 @@
         factor = SHRINK if c < 3 else 1.0
         at = 0
         for neighbour in range(4):
+            base = lax.rem(me + holders[neighbour], blocks) * rows.count + starts[c]
             for part in range(shell_rows):
-                row = neighbour * rows.rim + c * shell_rows + part
-                table_ref[c, at] = broadcast(rims_ref[pl.ds(row, 1), :] * factor)
+                table_ref[c, at] = broadcast(around_ref[pl.ds(base + part, 1), :] * factor)
                 at += 1
         for slab_ref in (below_ref, above_ref):
             for part in range(shell_rows):
@@ -235,35 +276,51 @@
             values = [jnp.where(here, take_lanes(table_ref[c, k], lanes), values[c]) for c in range(4)]
         for c in range(4):
             far_ref[c, at, :] = values[c]
+        terms = distance_terms(values[:3], 1.0 / cutoff_sq, False)
+        terms = terms + [jnp.zeros_like(terms[0])] * (TERMS - len(terms))
+        for row, term in enumerate(terms):
+            far_terms_ref[pl.ds(group * SUBLANES * TERMS + row, SUBLANES, stride=TERMS), :] = term
 
     sum_ref[...] = jnp.zeros(sum_ref.shape, jnp.float32)
     block_copy.wait()
 
-    def add_tile(tile, _):
+    def distances(tile):
+        base = pl.multiple_of(block_ref[0, 0, tile] * TILE, TILE)
+        far = far_terms_ref[pl.ds(pl.multiple_of(tile * TERMS, TERMS), TERMS), :]
+        return jnp.dot(
+            terms_ref[pl.ds(base, TILE), :TERMS], far.astype(jnp.bfloat16), preferred_element_type=jnp.float32
+        )
+
+    def add_tile(tile, shifted):
+        following = distances(jnp.minimum(tile + 1, tiles - 1))
         base = block_ref[0, 0, tile] * TILE
         far = [broadcast(far_ref[c, pl.ds(tile, 1), :]) for c in range(4)]
         for group in range(TILE // SUBLANES):
             at = pl.ds(pl.multiple_of(base + group * SUBLANES, SUBLANES), SUBLANES)
-            gap = [own_ref[c, at, :] - far[c] for c in range(3)]
-            square = gap[0] * gap[0] + gap[1] * gap[1] + gap[2] * gap[2]
-            shifted = square + 1.0 / cutoff_sq
-            inverse = pl.reciprocal(shifted, approx=True)
-            inverse = inverse * (2.0 - shifted * inverse)
-            switch = jnp.maximum(1.0 - square, 0.0)
+            square = shifted[group * SUBLANES : (group + 1) * SUBLANES, :]
+            inverse = pl.reciprocal(square, approx=True)
+            switch = jnp.maximum(1.0 + 1.0 / cutoff_sq - square, 0.0)
             weight = inverse * switch
-            strength = (inverse - own_ref[3, at, :] * far[3]) * (weight * weight)
+            strength = (inverse - own_ref[at, :] * far[3]) * (weight * weight)
             for c in range(3):
-                sum_ref[c, at, :] = sum_ref[c, at, :] + strength * gap[c]
-        return 0
-
-    lax.fori_loop(0, live_ref[0, 0], add_tile, 0)
+                sum_ref[c, at, :] = sum_ref[c, at, :] + strength * far[c]
+            sum_ref[3, at, :] = sum_ref[3, at, :] + strength
+        return following
+
+    lax.fori_loop(0, live_ref[0, 0], add_tile, distances(0))
 
     scale = time_step * time_step * force_scale * 4.0 / 2048.0
-    for c in range(3):
-        for part in range(atom_rows):
-            total = jnp.sum(sum_ref[c, pl.ds(part * LANES, LANES), :].T, axis=0, keepdims=True)
-            mass = motion_ref[pl.ds(3 * atom_rows + part, 1), :]
-            moved = time_step * motion_ref[pl.ds(c * atom_rows + part, 1), :] + scale * total * mass
+
+    def lane_sums(c, part):
+        return jnp.sum(sum_ref[c, pl.ds(part * LANES, LANES), :].T, axis=0, keepdims=True)
+
+    for part in range(atom_rows):
+        strength = lane_sums(3, part)
+        mass = motion_ref[pl.ds(6 * atom_rows + part, 1), :]
+        for c in range(3):
+            speed = motion_ref[pl.ds(c * atom_rows + part, 1), :]
+            place = motion_ref[pl.ds((3 + c) * atom_rows + part, 1), :]
+            moved = time_step * speed + scale * (place * strength - lane_sums(c, part)) * mass
             for copy in range(copies):
                 out_ref[pl.ds(copy * rows.disp_count + c * atom_rows + part, 1), :] = moved
     if rows.disp_count > rows.disp_used:
@@ -287,7 +344,7 @@
     def weights(first, second, row):
         gap = [first[c] - second[c] for c in range(3)]
         length_sq = gap[0] * gap[0] + gap[1] * gap[1] + gap[2] * gap[2] + length_floor
-        scale = rsqrt(length_sq) * rsqrt(first[3] + second[3])
+        scale = lax.rsqrt(length_sq) * lax.rsqrt(first[3] + second[3])
         return [gap[c] * scale for c in range(3)]
 
     at = 0
@@ -317,24 +374,23 @@
         at += 1
 
     down = lax.broadcasted_iota(jnp.int32, (SUBLANES, LANES), 0)
-    across = lax.broadcasted_iota(jnp.int32, (SUBLANES, LANES), 1).astype(jnp.float32)
     group_rows = 4 * SUBLANES
 
-    def column(row, group):
-        return take_lanes(jnp.broadcast_to(row, (SUBLANES, LANES)), down + group * SUBLANES)
-
-    def put(at, columns, signs, half):
+    kind = jnp.bfloat16 if shell_rows * LANES <= 256 else jnp.float32
+    across = lax.broadcasted_iota(jnp.int32, (group_rows, LANES), 1).astype(jnp.float32)
+    lanes = [(across + float(block * LANES)).astype(kind) for block in range(shell_rows)]
+
+    def column(row, step, half=0):
+        row = jnp.broadcast_to(row, (SUBLANES, LANES))
+        groups = [take_lanes(row, down + at) for at in range(step * group_rows, (step + 1) * group_rows, SUBLANES)]
+        return (jnp.concatenate(groups, axis=0) - float(half * shell_rows * LANES)).astype(kind)
+
+    def put(at, ends, signs):
         for block in range(shell_rows):
-            lanes = across + float((half * shell_rows + block) * LANES)
-            halves = []
-            for ends in columns:
-                value = 0.0
-                for end, sign in zip(ends, signs):
-                    value = jnp.where(end == lanes, sign, value)
-                halves.append(value)
-            matrix_ref[pl.ds(at, group_rows), block * LANES : (block + 1) * LANES] = jnp.concatenate(
-                halves, axis=0
-            ).astype(matrix_ref.dtype)
+            value = jnp.zeros((group_rows, LANES), kind)
+            for end, sign in zip(ends, signs):
+                value = jnp.where(end == lanes[block], jnp.full((group_rows, LANES), sign, kind), value)
+            matrix_ref[pl.ds(at, group_rows), block * LANES : (block + 1) * LANES] = value.astype(matrix_ref.dtype)
 
     def build(domain, _):
         start = pl.multiple_of(domain * rows.matrix, LANES)
@@ -342,9 +398,9 @@
             first = around_ref[pl.ds(domain * rows.count + rows.bond_first + part, 1), :]
             second = around_ref[pl.ds(domain * rows.count + rows.bond_second + part, 1), :]
             for step in range(LANES // group_rows):
-                columns = [(column(first, 4 * step + h), column(second, 4 * step + h)) for h in range(4)]
                 for half in range(2):
-                    put(start + rows.inner_at[half] + part * LANES + step * group_rows, columns, (1.0, -1.0), half)
+                    ends = (column(first, step, half), column(second, step, half))
+                    put(start + rows.inner_at[half] + part * LANES + step * group_rows, ends, (1.0, -1.0))
         for part in range(rows.slot_rows):
             for code in range(5):
                 if code == 0:
@@ -354,8 +410,8 @@
                     row = key_ref[pl.ds((part * 4 + code - 1) * domains + owner, 1), :]
                 sign = 1.0 if code == 0 else -1.0
                 for step in range(LANES // group_rows):
-                    columns = [(column(row, 4 * step + h),) for h in range(4)]
-                    put(start + rows.cross_at + (part * 5 + code) * LANES + step * group_rows, columns, (sign,), 0)
+                    at = start + rows.cross_at + (part * 5 + code) * LANES + step * group_rows
+                    put(at, (column(row, step),), (sign,))
         return 0
 
     lax.fori_loop(0, domains, build, 0)
@@ -553,11 +609,11 @@
     f32 = jnp.float32
 
     sent = (coords, charge, inv_mass, bond_atoms, cross_atoms, cross_side)
-    rim, static = pl.pallas_call(
+    packed, rim = pl.pallas_call(
         functools.partial(pack_kernel, rows, copies),
         out_shape=(
-            jax.ShapeDtypeStruct((rows.rim, LANES), f32),
             jax.ShapeDtypeStruct((copies * rows.count, LANES), f32),
+            jax.ShapeDtypeStruct((4 * rows.shell_rows, LANES), f32),
         ),
         in_specs=smem(1) + hbm(len(sent)),
         out_specs=tuple(vmem(2)),
@@ -566,51 +622,55 @@
         name="pack",
     )(cross_count, *in_hbm(sent))
 
-    if whole_slab:
-        around = lax.all_to_all(static, "dom", 0, 0, tiled=True)
-        here = lax.axis_index("dom").reshape(1)
-    else:
-        around = jnp.concatenate([static] + [passed_along(static, "dom", -stride) for stride in strides], axis=0)
-    rims = jnp.concatenate([passed_along(rim, "dom", -stride) for stride in strides], axis=0)
-    below = passed_along(rim, "slab", 1)
-    above = passed_along(rim, "slab", -1)
-
     alone = (coords, charge, velocity, inv_mass, tile_atoms)
-    own, near, index, motion = pl.pallas_call(
+    own = pl.pallas_call(
         functools.partial(own_kernel, rows),
         out_shape=(
-            jax.ShapeDtypeStruct((4, atoms, LANES), f32),
+            jax.ShapeDtypeStruct((atoms, LANES), jnp.bfloat16),
+            jax.ShapeDtypeStruct((atoms, LANES), f32),
             jax.ShapeDtypeStruct((4, tiles, TILE), f32),
             jax.ShapeDtypeStruct((tiles, TILE), jnp.int32),
-            jax.ShapeDtypeStruct((4 * rows.atom_rows, LANES), f32),
+            jax.ShapeDtypeStruct((7 * rows.atom_rows, LANES), f32),
         ),
         in_specs=hbm(len(alone)),
-        out_specs=tuple(vmem(4)),
+        out_specs=tuple(vmem(5)),
         scratch_shapes=room_for(alone[:4]) + [pltpu.SemaphoreType.DMA((len(alone),))],
         compiler_params=params(4),
         cost_estimate=cost(64 * atoms * LANES, 16 * atoms * LANES),
         name="own",
     )(*in_hbm(alone))
 
+    below = passed_along(rim, "slab", 1)
+    above = passed_along(rim, "slab", -1)
+    if whole_slab:
+        around = lax.all_to_all(packed, "dom", 0, 0, tiled=True)
+        here = lax.axis_index("dom").reshape(1)
+        holders = [stride % domains for stride in strides]
+    else:
+        around = jnp.concatenate([packed] + [passed_along(packed, "dom", -stride) for stride in strides], axis=0)
+        here = jnp.zeros(1, jnp.int32)
+        holders = [1, 2, 3, 4]
+
     moves = pl.pallas_call(
-        functools.partial(force_kernel, rows, copies),
+        functools.partial(force_kernel, rows, copies, holders),
         out_shape=jax.ShapeDtypeStruct((copies * rows.disp_count, LANES), f32),
-        in_specs=smem(1) + hbm(1) + vmem(7),
+        in_specs=smem(2) + hbm(1) + vmem(8),
         out_specs=vmem(1)[0],
         scratch_shapes=[
             pltpu.VMEM((4, 6 * rows.shell_rows, SUBLANES, LANES), f32),
             pltpu.VMEM((4, tiles, LANES), f32),
-            pltpu.VMEM((3, atoms, LANES), f32),
+            pltpu.VMEM((tiles * TERMS, LANES), f32),
+            pltpu.VMEM((4, atoms, LANES), f32),
             pltpu.SMEM(tile_block.shape, jnp.int32),
             pltpu.SemaphoreType.DMA(()),
         ],
-        compiler_params=params(4),
-        cost_estimate=cost(30 * tiles * TILE * TILE, 4 * own.size),
+        compiler_params=params(8),
+        cost_estimate=cost(30 * tiles * TILE * TILE, 4 * around.size),
         name="force",
-    )(active_tile_count, *in_hbm([tile_block]), rims, below, above, own, near, index, motion)
+    )(here, active_tile_count, *in_hbm([tile_block]), around, below, above, *own)
 
     if not whole_slab:
-        return by_exchange(rows, strides, around, moves)
+        return by_exchange(rows, strides, around, moves, cross_count)
 
     constraint_rows = rows.bond_rows + rows.slot_rows
     weight, matrix = pl.pallas_call(
@@ -647,7 +707,7 @@
     )(here, around, every_move, weight, matrix)
 
 
-def by_exchange(rows, strides, around, moves):
+def by_exchange(rows, strides, around, moves, cross_count):
     atom_count = rows.atom_rows * LANES
     shell = rows.shell_rows * LANES
     inside = around.reshape(5, rows.count, LANES)

time: 44.6 us -> 43.6 us (0.978); the launches traced: 45.4 us -> 43.2 us
  starting transfers between devices: 19.8 us -> 14.7 us
  waiting for transfers between devices: 5.28 us -> 7.95 us
    ppermute x6 -> x2, starting transfers between devices: 9.13 us -> 0.65 us  [passed_along(): lax.ppermute(array, axis, [(i, (i + by) % length) for i in range(length)])]
    all_to_all x1, waiting for transfers between devices: 0.01 us -> 3.66 us  [shards(): around = lax.all_to_all(packed, 'dom', 0, 0, tiled=True)]
    all_to_all x1, starting transfers between devices: 3.36 us -> 6.75 us  [shards(): every_move = lax.all_to_all(moves, 'dom', 0, 0, tiled=True)]
    ppermute x6 -> x2, waiting for transfers between devices: 2.5 us -> 0.68 us  [passed_along(): lax.ppermute(array, axis, [(i, (i + by) % length) for i in range(length)])]
    all_to_all x1, waiting for transfers between devices: 2.78 us -> 3.6 us  [shards(): every_move = lax.all_to_all(moves, 'dom', 0, 0, tiled=True)]
    pallas_call x1, Pallas kernels: 5.9 us -> 6.68 us  [shards(): pl.pallas_call(functools.partial(force_kernel, rows, copies, holders), ou...]
    pallas_call x1, Pallas kernels: 4.05 us -> 3.3 us  [shards(): pl.pallas_call(functools.partial(bond_kernel, rows, domains, strides), ou...]
  transfers between devices with their start and end apart: 8 -> 4, of which waited for: 2 -> 3; matrix products, arithmetic and copies ran while one was open for 0% -> 0% of each run, Pallas kernels for 25% -> 12%
where the time goes in v6:
time: 43.6 us; the launch traced here: 43.2 us
  Pallas kernels  18.6 us (43%)
  starting transfers between devices  14.7 us (34%)
  waiting for transfers between devices  7.95 us (18%)
  between operations  1.97 us (5%)
    all_to_all x1, starting transfers between devices, shards(): around = lax.all_to_all(packed, 'dom', 0, 0, tiled=True)  7.29 us
    all_to_all x1, starting transfers between devices, shards(): every_move = lax.all_to_all(moves, 'dom', 0, 0, tiled=True)  6.75 us
    pallas_call x1, Pallas kernels, shards(): pl.pallas_call(functools.partial(force_kernel, rows, copies, holders), ou...  6.68 us
    pallas_call x1, Pallas kernels, shards(): pl.pallas_call(functools.partial(solve_kernel, rows, domains, strides), o...  5.38 us
    all_to_all x1, waiting for transfers between devices, shards(): around = lax.all_to_all(packed, 'dom', 0, 0, tiled=True)  3.66 us
    all_to_all x1, waiting for transfers between devices, shards(): every_move = lax.all_to_all(moves, 'dom', 0, 0, tiled=True)  3.6 us
    pallas_call x1, Pallas kernels, shards(): pl.pallas_call(functools.partial(bond_kernel, rows, domains, strides), ou...  3.3 us
    pallas_call x1, Pallas kernels, shards(): pl.pallas_call(functools.partial(own_kernel, rows), out_shape=(jax.ShapeD...  1.68 us
  transfers between devices with their start and end apart: 4, of which 3 were waited for; matrix products, arithmetic and copies ran while one was open for 0% of the time, Pallas kernels for 12%

profile of v6, /device:TPU:0, one launch (start us, length us, event | category | flops | bytes accessed | tf_op | source)
XLA Modules:
  0.0 43.2 jit_solution(9007172399934210138)
XLA Ops:
  1.3 1.5 %pack.1 = (f32[256,128]{1,0:T(8,128)}, f32[8,128]{1,0:T(8,128)S(1)}) custom-call(s32[1,1]{1,0:T(1,128)S(6)} %copy.14.count_ref, f32[3,1,1,512]{3,2,1,0:T(1,128)} %coords_hbm.1, f32[1,1,512]{2,1,0:T(1,128)} %charge_hbm.1, f32[1,1,512]{2,1,0:T(1,128)} %mass_hbm.1, s32[2,1,1,256]{3,2,1,0:T(1,128)} %refs_3_.1, s32[2,1,1,128]{3,2,1,0:T(1,128)} %refs_4_.1, ...), custom_call_target="tpu_custom_call" | custom-call | tf_op jit(solution)/shard_map/pack/pallas_call | solution.py:612
  2.8 7.3 %all-to-all-start = ((f32[8,32,128]{2,1,0:T(8,128)}), f32[8,32,128]{2,1,0:T(8,128)S(1)}, u32[]{:S(2)}, u32[]{:S(2)}) async-start(f32[8,32,128]{2,1,0:T(8,128)} %bitcast.1), calls=%async_computation | async-start | bytes 262144 | tf_op jit(solution)/shard_map/all_to_all | solution.py:646
  10.1 0.7 %collective-permute-start.1 = (f32[8,128]{1,0:T(8,128)S(1)}, f32[8,128]{1,0:T(8,128)S(1)}, u32[]{:S(2)}, u32[]{:S(2)}) collective-permute-start(f32[8,128]{1,0:T(8,128)S(1)} %get-tuple-element.12), channel_id=1, source_target_pairs={{0,24},{8,0},{16,8},{24,16},{1,25},{9,1},{17,9},{25,17},{2,26},{10... | collective-permute-start | bytes 12296 | tf_op jit(solution)/shard_map/ppermute | solution.py:23
  10.7 0.0 collective-permute-start
  11.4 1.7 %own.1 = (bf16[512,128]{1,0:T(8,128)(2,1)S(1)}, f32[512,128]{1,0:T(8,128)S(1)}, f32[4,64,128]{2,1,0:T(8,128)S(1)}, s32[64,128]{1,0:T(8,128)S(1)}, f32[28,128]{1,0:T(8,128)S(1)}) custom-call(f32[3,1,1,512]{3,2,1,0:T(1,128)} %coords_hbm.1, f32[1,1,512]{2,1,0:T(1,128)} %charge_hbm.1, f32[3,1,1,512]{3,2,1,0:T(1,128)} %velocity_hbm.1, f32[1,1,512]{2,1,0:T(1,128)} %mass_hbm.1, ...), custom_call_target="tpu_custom_call" | custom-call | flops 4194304 | bytes 1048576 | tf_op jit(solution)/shard_map/own/pallas_call | solution.py:626
  13.1 0.0 collective-permute-done.1.above_ref
  13.1 0.7 %collective-permute-done.below_ref = f32[8,128]{1,0:T(8,128)S(1)} collective-permute-done((f32[8,128]{1,0:T(8,128)S(1)}, f32[8,128]{1,0:T(8,128)S(1)}, u32[]{:S(2)}, u32[]{:S(2)}) %collective-permute-start) | collective-permute-done | bytes 4128 | tf_op jit(solution)/shard_map/ppermute | solution.py:23
  13.8 3.7 %all-to-all-done = f32[8,32,128]{2,1,0:T(8,128)S(1)} async-done(((f32[8,32,128]{2,1,0:T(8,128)}), f32[8,32,128]{2,1,0:T(8,128)S(1)}, u32[]{:S(2)}, u32[]{:S(2)}) %all-to-all-start) | async-done | bytes 131104 | tf_op jit(solution)/shard_map/all_to_all | solution.py:646
  17.4 6.7 %force.1 = f32[128,128]{1,0:T(8,128)} custom-call(s32[1]{0:T(128)} %bitcast.here_ref, s32[1,1]{1,0:T(1,128)S(6)} %copy.13.live_ref, s32[1,1,64]{2,1,0:T(1,128)} %block_hbm.1, f32[256,128]{1,0:T(8,128)S(1)} %bitcast.5, f32[8,128]{1,0:T(8,128)S(1)} %collective-permute-done.below_ref, f32[8,128]{1,0:T(8,128)S(1)} %collective-permute-done.1.above_ref, ...), custom_call_target="tpu_custom_call" | custom-call | flops 31457280 | bytes 131072 | tf_op jit(solution)/shard_map/force/pallas_call | solution.py:654
  24.1 6.7 %all-to-all-start.1 = ((f32[8,16,128]{2,1,0:T(8,128)}), f32[8,16,128]{2,1,0:T(8,128)S(1)}, u32[]{:S(2)}, u32[]{:S(2)}) async-start(f32[8,16,128]{2,1,0:T(8,128)} %bitcast.3), calls=%async_computation.1 | async-start | bytes 131072 | tf_op jit(solution)/shard_map/all_to_all | solution.py:690
  30.9 3.3 %bonds.1 = (f32[72,128]{1,0:T(8,128)S(1)}, f8e4m3fn[9216,256]{1,0:T(32,128)(4,1)S(1)}) custom-call(f32[256,128]{1,0:T(8,128)S(1)} %bitcast.6), custom_call_target="tpu_custom_call" | custom-call | flops 18874368 | bytes 131072 | tf_op jit(solution)/shard_map/bonds/pallas_call | solution.py:676
  34.2 3.6 %all-to-all-done.1 = f32[8,16,128]{2,1,0:T(8,128)S(1)} async-done(((f32[8,16,128]{2,1,0:T(8,128)}), f32[8,16,128]{2,1,0:T(8,128)S(1)}, u32[]{:S(2)}, u32[]{:S(2)}) %all-to-all-start.1) | async-done | bytes 65568 | tf_op jit(solution)/shard_map/all_to_all | solution.py:690
  37.8 5.4 %solve.1 = (f32[3,1,1,512]{3,2,1,0:T(1,128)}, f32[3,1,1,512]{3,2,1,0:T(1,128)}) custom-call(s32[1]{0:T(128)} %bitcast.here_ref, f32[256,128]{1,0:T(8,128)S(1)} %bitcast.7, f32[128,128]{1,0:T(8,128)S(1)} %bitcast.8, f32[72,128]{1,0:T(8,128)S(1)} %get-tuple-element.18.weight_ref, f8e4m3fn[9216,256]{1,0:T(32,128)(4,1)S(1)} %get-tuple-element.19.signs_ref), custom_call_target="tpu_custom_call" | custom-call | tf_op jit(solution)/shard_map/solve/pallas_call | solution.py:692
Async XLA Ops:
  2.8 14.6 %all-to-all-start = ((f32[8,32,128]{2,1,0:T(8,128)}), f32[8,32,128]{2,1,0:T(8,128)S(1)}, u32[]{:S(2)}, u32[]{:S(2)}) async-start(f32[8,32,128]{2,1,0:T(8,128)} %bitcast.1), calls=%async_computation | async-start | bytes 262144 | tf_op jit(solution)/shard_map/all_to_all | solution.py:646
  10.1 3.0 %collective-permute-start.1 = (f32[8,128]{1,0:T(8,128)S(1)}, f32[8,128]{1,0:T(8,128)S(1)}, u32[]{:S(2)}, u32[]{:S(2)}) collective-permute-start(f32[8,128]{1,0:T(8,128)S(1)} %get-tuple-element.12), channel_id=1, source_target_pairs={{0,24},{8,0},{16,8},{24,16},{1,25},{9,1},{17,9},{25,17},{2,26},{10... | collective-permute-start | bytes 12296 | tf_op jit(solution)/shard_map/ppermute | solution.py:23
  10.7 3.0 %collective-permute-start = (f32[8,128]{1,0:T(8,128)S(1)}, f32[8,128]{1,0:T(8,128)S(1)}, u32[]{:S(2)}, u32[]{:S(2)}) collective-permute-start(f32[8,128]{1,0:T(8,128)S(1)} %get-tuple-element.12), channel_id=1, source_target_pairs={{0,8},{8,16},{16,24},{24,0},{1,9},{9,17},{17,25},{25,1},{2,10},{10... | collective-permute-start | bytes 12296 | tf_op jit(solution)/shard_map/ppermute | solution.py:23
  24.1 13.7 %all-to-all-start.1 = ((f32[8,16,128]{2,1,0:T(8,128)}), f32[8,16,128]{2,1,0:T(8,128)S(1)}, u32[]{:S(2)}, u32[]{:S(2)}) async-start(f32[8,16,128]{2,1,0:T(8,128)} %bitcast.3), calls=%async_computation.1 | async-start | bytes 131072 | tf_op jit(solution)/shard_map/all_to_all | solution.py:690
